TPU v7x, 32 devices: a whole 2x2x4 slice. The times are simulated.
32 devices in a mesh: blk: 8 (over y, x, core), feat: 4 (over z).
Axes of the slice: x: 2, y: 2, z: 4, core: 2. Of those that a mesh axis runs over, the one named last changes fastest.
Arguments:
- features: bfloat16 [256, 16384], P('feat', 'blk'), may hold values from -6 to 6
- adj_tiles: bfloat16 [8, 4, 8, 48, 128, 128], P('blk', 'feat'), may hold values from -0.0546875 to 0.0546875
- tile_rows: int32 [8, 4, 8, 48], P('blk', 'feat'), may hold values from 0 to 15
- tile_cols: int32 [8, 4, 8, 48], P('blk', 'feat'), may hold values from 0 to 15
- counts: int32 [8, 4, 8], P('blk', 'feat'), may hold values from 1 to 48, as said below
- weight: bfloat16 [256, 256], replicated, may hold values from -0.375 to 0.375
- cotangent: bfloat16 [256, 16384], P(None, ('blk', 'feat')), may hold values from -6 to 6
Outputs:
- activated: bfloat16 [256, 16384], P(None, ('blk', 'feat'))
- weight_grad: float32 [256, 256], P('feat')
Inputs may be any that keep to these rules, and one draw needn't show every extreme that they name: Only the first counts slots of a partition, group and source partition are live; the slots a partition takes from its own nodes are all live in every group.
All inputs are finite; a program needn't handle non-finite values.
Results may differ from a plain program's by a relative error of at most 0.02.
Values may be sent and summed in bfloat16 or wider, within the bound.
No kernel may reach another device: no remote copies, remote signals or barrier semaphores. Data moves between devices by JAX's collectives and lax.ppermute only.
A program may use at most 320 MiB of HBM per device.

v0:
```python
import math

import jax
import jax.numpy as jnp
from jax import lax
from jax.sharding import PartitionSpec as P


def tile_terms(slot_tiles, gathered, rows_here, live_mask, row_tiles):
    products = jnp.einsum("kij,fkj->fki", slot_tiles, gathered, preferred_element_type=jnp.float32)
    tile_range = jnp.arange(row_tiles, dtype=jnp.int32)
    placing = ((rows_here[:, None] == tile_range[None, :]) & live_mask[:, None]).astype(
        jnp.bfloat16
    )
    high_part = lax.optimization_barrier(products.astype(jnp.bfloat16))
    low_part = (products - high_part.astype(jnp.float32)).astype(jnp.bfloat16)
    summed = jnp.einsum("fki,kr->fri", high_part, placing, preferred_element_type=jnp.float32)
    summed = summed + jnp.einsum(
        "fki,kr->fri", low_part, placing, preferred_element_type=jnp.float32
    )
    return summed.reshape(products.shape[0], row_tiles * products.shape[2])


def source_term(col_panel, job, source, accum, row_tiles):
    job_tiles, job_rows, job_cols, job_counts = job
    slot_tiles = lax.dynamic_index_in_dim(job_tiles, source, 0, False)
    slot_rows = lax.dynamic_index_in_dim(job_rows, source, 0, False)
    slot_cols = lax.dynamic_index_in_dim(job_cols, source, 0, False)
    slot_count = lax.dynamic_index_in_dim(job_counts, source, 0, False)
    slot_cap = slot_tiles.shape[0]
    gathered = jnp.take(col_panel, slot_cols, axis=1)
    live_mask = jnp.arange(slot_cap, dtype=jnp.int32) < slot_count
    return accum + tile_terms(slot_tiles, gathered, slot_rows, live_mask, row_tiles)


def shards(features, adj_tiles, tile_rows, tile_cols, counts, weight, cotangent):
    blocks = lax.axis_size("blk")
    groups = lax.axis_size("feat")
    group_width = features.shape[0]
    feat_width = group_width * groups
    rows_here = features.shape[1]
    tile_size = adj_tiles.shape[-1]
    row_tiles = rows_here // tile_size
    slot_cap = adj_tiles.shape[3]
    local_tiles = adj_tiles.reshape(blocks, slot_cap, tile_size, tile_size)
    local_rows = tile_rows.reshape(blocks, slot_cap)
    local_cols = tile_cols.reshape(blocks, slot_cap)
    local_counts = counts.reshape(blocks)
    jobs = [(local_tiles, local_rows, local_cols, local_counts)]
    full_rows = lax.all_gather(features, "feat", axis=0, tiled=True)
    start_sums = tuple((jnp.zeros((feat_width, rows_here), jnp.float32) for job in jobs))
    shard_piece = lax.all_gather(full_rows, "blk", axis=1, tiled=True)

    def add_source(offset, inner):
        col_panel = lax.dynamic_slice_in_dim(shard_piece, offset * rows_here, rows_here, 1)
        col_panel = col_panel.reshape(feat_width, row_tiles, tile_size)
        return tuple(
            (
                source_term(col_panel, job, offset, total, row_tiles)
                for job, total in zip(jobs, inner)
            )
        )

    sums_all = lax.fori_loop(0, shard_piece.shape[1] // rows_here, add_source, start_sums)
    partial_value = sums_all[0]
    aggregated = lax.psum_scatter(
        partial_value.astype(jnp.bfloat16), "feat", scatter_dimension=1, tiled=True
    )
    preact = jnp.dot(weight, aggregated, preferred_element_type=jnp.float32)
    sigmoid_z = jax.nn.sigmoid(preact)
    activated = (preact * sigmoid_z).astype(jnp.bfloat16)
    slope = (cotangent.astype(jnp.float32) * sigmoid_z * (1.0 + preact * (1.0 - sigmoid_z))).astype(
        jnp.bfloat16
    )
    grad_scale = 1.0 / math.sqrt(blocks * rows_here)
    local_grad = (
        lax.dot_general(
            slope, aggregated, (((1,), (1,)), ((), ())), preferred_element_type=jnp.float32
        )
        * grad_scale
    )
    grad_whole = lax.psum(local_grad, ("blk", "feat"))
    grad_share = feat_width // groups
    weight_grad = lax.dynamic_slice_in_dim(
        grad_whole, lax.axis_index("feat") * grad_share, grad_share, 0
    )
    return (activated, weight_grad)


def solution(mesh):
    in_specs = (
        P("feat", "blk"),
        P("blk", "feat", None, None, None, None),
        P("blk", "feat", None, None),
        P("blk", "feat", None, None),
        P("blk", "feat", None),
        P(),
        P(None, ("blk", "feat")),
    )
    out_specs = (P(None, ("blk", "feat")), P("feat", None))
    return jax.shard_map(shards, mesh=mesh, in_specs=in_specs, out_specs=out_specs, check_vma=False)
```

profile of v0, /device:TPU:0, one launch (start us, length us, event | category | flops | bytes accessed | tf_op | source)
XLA Modules:
  0.0 430.2 jit_solution(8758939744443424589)
XLA Ops:
  8.0 32.3 %all-gather.3.cloned.1.call-done = bf16[256,2048]{1,0:T(8,128)(2,1)} async-done(((bf16[64,2048]{1,0:T(8,128)(2,1)}), bf16[256,2048]{1,0:T(8,128)(2,1)}) %all-gather.3.cloned.1.call-update) | async-done | bytes 1048592 | tf_op jit(solution)/shard_map/all_gather | solution.py:50
  40.3 55.7 %all-gather.5.cloned.1.call-done = bf16[256,16384]{1,0:T(8,128)(2,1)} async-done(((bf16[256,2048]{1,0:T(8,128)(2,1)}), bf16[256,16384]{1,0:T(8,128)(2,1)}) %all-gather.5.cloned.1.call-update) | async-done | bytes 8388624 | tf_op jit(solution)/shard_map/all_gather | solution.py:52
  96.1 166.1 %while.14 = (s32[]{:T(128)}, f32[256,2048]{1,0:T(8,128)}, s32[8,48]{1,0:T(8,128)}, s32[8]{0:T(128)}, s32[8,48]{1,0:T(8,128)}, /*index=5*/bf16[256,16384]{1,0:T(8...) while((s32[]{:T(128)}, f32[256,2048]{1,0:T(8,128)}, ...), condition=%wide.region_1.2_spmd.clone, body=%wide.region_0.1_spmd.clone.sunk | while | flops 512758272 | bytes 58202896 | solution.py:64
  99.3 2.8 gather_fusion
  102.7 3.4 bitcast_convert_fusion.2
  111.1 1.9 fusion.48
  112.9 2.5 bitcast_add_fusion.2
  118.7 2.8 gather_fusion
  122.1 3.4 bitcast_convert_fusion.2
  132.3 4.1 bitcast_add_fusion.2
  139.6 2.8 gather_fusion
  143.1 3.4 bitcast_convert_fusion.2
  153.3 4.1 bitcast_add_fusion.2
  160.6 2.8 gather_fusion
  164.0 3.4 bitcast_convert_fusion.2
  174.2 4.1 bitcast_add_fusion.2
  181.5 2.8 gather_fusion
  185.0 3.4 bitcast_convert_fusion.2
  195.2 4.1 bitcast_add_fusion.2
  202.5 2.8 gather_fusion
  206.0 3.4 bitcast_convert_fusion.2
  216.2 4.1 bitcast_add_fusion.2
  223.5 2.8 gather_fusion
  226.9 3.4 bitcast_convert_fusion.2
  237.1 4.1 bitcast_add_fusion.2
  244.4 2.8 gather_fusion
  247.9 3.4 bitcast_convert_fusion.2
  258.1 4.1 bitcast_add_fusion.2
  262.2 2.8 convert_element_type.36
  265.2 27.1 %reduce-scatter.2.cloned.1.call-done = bf16[256,512]{1,0:T(8,128)(2,1)} async-done(((bf16[256,2048]{1,0:T(8,128)(2,1)}), bf16[256,512]{1,0:T(8,128)(2,1)}) %reduce-scatter.2.cloned.1.call-update) | async-done | bytes 262160 | tf_op jit(solution)/shard_map/reduce_scatter | solution.py:66
  293.6 2.1 convolution_multiply_fusion
  296.5 125.7 %all-reduce.2.cloned.1.call-done = f32[256,256]{1,0:T(8,128)} async-done(((f32[256,256]{1,0:T(8,128)}), f32[256,256]{1,0:T(8,128)}) %all-reduce.2.cloned.1.call-update) | async-done | bytes 262160 | tf_op jit(solution)/shard_map/psum | solution.py:82
  (128 shorter events, 88.0 us)
Async XLA Ops:
  7.2 285.1 %copy-start = (bf16[256,256]{1,0:T(8,128)(2,1)S(1)}, bf16[256,256]{1,0:T(8,128)(2,1)}, u32[]{:S(2)}) copy-start(bf16[256,256]{1,0:T(8,128)(2,1)} %param.14) | copy-start | bytes 393220
  7.2 33.1 %all-gather.3.cloned.1.call-start = ((), (), s32[]{:S(2)}) async-start(), calls=%async_computation.1 | async-start | bytes 1310720 | tf_op jit(solution)/shard_map/all_gather | solution.py:50
  7.9 88.2 %all-gather.5.cloned.1.call-start = ((), (), s32[]{:S(2)}) async-start(), calls=%async_computation.2 | async-start | bytes 9437184 | tf_op jit(solution)/shard_map/all_gather | solution.py:52
  40.3 252.0 %reduce-scatter.2.cloned.1.call-start = ((), (), s32[]{:S(2)}) async-start(), calls=%async_computation.3 | async-start | bytes 1310720 | tf_op jit(solution)/shard_map/reduce_scatter | solution.py:66
  106.1 1.2 copy-start.2
  125.5 1.2 copy-start.2
  146.5 1.2 copy-start.2
  167.4 1.2 copy-start.2
  188.4 1.2 copy-start.2
  209.4 1.2 copy-start.2
  230.3 1.2 copy-start.2
  251.3 1.2 copy-start.2
  262.2 2.8 copy-start.1
  265.0 157.2 %all-reduce.2.cloned.1.call-start = ((), (), s32[]{:S(2)}) async-start(), calls=%async_computation.4 | async-start | bytes 524288 | tf_op jit(solution)/shard_map/psum | solution.py:82
Sparse Core Ops, SparseCore 0:
  9.6 30.6 all-gather.2
  42.1 53.8 all-gather.4
  265.1 27.1 reduce-scatter.1
  298.5 123.6 all-reduce.1
where the time goes:
time: 432 us; the launch traced here: 430 us
  waiting for transfers between devices  242 us (56%)
  matrix products  59.9 us (14%)
  other arithmetic  59.5 us (14%)
  local copies, waits for them, and re-layouts  54.8 us (13%)
  between operations  13.8 us (3%)
    psum x1, waiting for transfers between devices, shards(): grad_whole = lax.psum(local_grad, ('blk', 'feat'))  126 us
    all_gather x1, waiting for transfers between devices, shards(): shard_piece = lax.all_gather(full_rows, 'blk', axis=1, tiled=True)  55.7 us
    all_gather x1, waiting for transfers between devices, shards(): full_rows = lax.all_gather(features, 'feat', axis=0, tiled=True)  32.3 us
    add x8, other arithmetic, source_term(): accum + tile_terms(slot_tiles, gathered, slot_rows, live_mask, row_tiles)  31.2 us
    reduce_scatter x1, waiting for transfers between devices, shards(): lax.psum_scatter(partial_value.astype(jnp.bfloat16), 'feat', scatter_dime...  27.1 us
    dot_general x8, matrix products, tile_terms(): jnp.einsum('kij,fkj->fki', slot_tiles, gathered, preferred_element_type=j...  27 us
    gather x8, local copies, waits for them, and re-layouts, source_term(): gathered = jnp.take(col_panel, slot_cols, axis=1)  22.1 us
    dot_general x8, matrix products, tile_terms(): jnp.einsum('fki,kr->fri', high_part, placing, preferred_element_type=jnp....  15 us
  transfers between devices with their start and end apart: 4, of which 4 were waited for; matrix products, arithmetic and copies ran while one was open for 0% of the time, Pallas kernels for 0%

commit v1 on v0

v1 whole, which is shorter than its diff:
```python
import functools
import math

import jax
import jax.numpy as jnp
from jax import lax
from jax.experimental import pallas as pl
from jax.experimental.pallas import tpu as pltpu
from jax.sharding import PartitionSpec as P

CHUNK = 8
UNROLL = 4


def hop(value, axis, bit):
    size = lax.axis_size(axis)
    return lax.ppermute(value, axis, [(i, i ^ bit) for i in range(size)])


def aggregate_kernel(offsets, groups, first, last, *refs):
    n_src = len(offsets)
    rows_ref, cols_ref, counts_ref, tiles_ref = refs[:4]
    unit_refs = refs[4 : 4 + n_src * groups]
    rest = refs[4 + n_src * groups :]
    if first:
        out_refs, scratch = rest[:1], rest[1:]
    elif last:
        acc_in, out_refs, scratch = rest[0], rest[1:3], rest[3:]
    else:
        acc_in, out_refs, scratch = rest[0], rest[1:2], rest[2:]
    feat, tiles, acc, unit_sems, tile_sems, acc_sem = scratch
    blk = lax.axis_index("blk")
    z = lax.axis_index("feat")
    slots = tiles_ref.shape[1]
    size = tiles_ref.shape[2]
    width = unit_refs[0].shape[0]
    nodes = unit_refs[0].shape[1]
    row_tiles = nodes // size
    chunks = slots // CHUNK

    def unit_copy(i, k):
        start = pl.multiple_of(lax.bitwise_xor(z, k) * width, width)
        return pltpu.make_async_copy(
            unit_refs[i * groups + k],
            feat.at[i, pl.ds(start, width), :],
            unit_sems.at[i, k],
        )

    def tile_copy(i, source, chunk):
        at = pl.ds(chunk * CHUNK, CHUNK)
        return pltpu.make_async_copy(tiles_ref.at[source, at], tiles.at[i, at], tile_sems.at[i, chunk])

    sources = [lax.bitwise_xor(blk, jnp.int32(off)) for off in offsets]
    live = [counts_ref[source] for source in sources]
    if not first:
        acc_copy = pltpu.make_async_copy(acc_in, acc.at[pl.ds(0, nodes)], acc_sem)
        acc_copy.start()
    for i in range(n_src):
        for k in range(groups):
            unit_copy(i, k).start()
        for chunk in range(chunks):

            @pl.when(chunk * CHUNK < live[i])
            def _():
                tile_copy(i, sources[i], chunk).start()

    if first:
        acc[pl.ds(0, nodes), :] = jnp.zeros((nodes, acc.shape[1]), jnp.float32)
    else:
        acc_copy.wait()
    for i in range(n_src):
        for k in range(groups):
            unit_copy(i, k).wait()

        def do_chunk(chunk, _):
            tile_copy(i, sources[i], chunk).wait()

            def do_some(part, _):
                base = chunk * CHUNK + part * UNROLL
                for u in range(UNROLL):
                    slot = base + u
                    row = jnp.where(slot < live[i], rows_ref[sources[i], slot], row_tiles)
                    col = cols_ref[sources[i], slot]
                    at = pl.ds(pl.multiple_of(row * size, size), size)
                    term = lax.dot_general(
                        tiles[i, slot],
                        feat[i, :, pl.ds(pl.multiple_of(col * size, size), size)],
                        (((1,), (1,)), ((), ())),
                        preferred_element_type=jnp.float32,
                    )
                    acc[at, :] += term
                return 0

            parts = jnp.minimum((live[i] - chunk * CHUNK + UNROLL - 1) // UNROLL, CHUNK // UNROLL)
            return lax.fori_loop(0, parts, do_some, 0)

        lax.fori_loop(0, (live[i] + CHUNK - 1) // CHUNK, do_chunk, 0)
    if last:
        send_ref, keep_ref = out_refs
        share = nodes // groups
        mine = lax.rem(z, 2)
        for d in range(groups // 2):
            keep_at = pl.multiple_of((2 * d + mine) * share, share)
            send_at = pl.multiple_of((2 * d + 1 - mine) * share, share)
            send_ref[d] = acc[pl.ds(send_at, share), :].astype(jnp.bfloat16)
            keep_ref[d] = acc[pl.ds(keep_at, share), :]
    else:
        out_copy = pltpu.make_async_copy(acc.at[pl.ds(0, nodes)], out_refs[0], acc_sem)
        out_copy.start()
        out_copy.wait()


def aggregate(offsets, groups, rows, cols, counts, tiles, units, acc, last):
    n_src = len(offsets)
    slots, size = tiles.shape[1], tiles.shape[2]
    width, nodes = units[0].shape
    feat_width = width * groups
    first = acc is None
    any_spec = pl.BlockSpec(memory_space=pl.ANY)
    smem = pl.BlockSpec(memory_space=pltpu.SMEM)
    vmem = pl.BlockSpec(memory_space=pltpu.VMEM)
    share = nodes // groups
    if last:
        out_shape = (
            jax.ShapeDtypeStruct((groups // 2, share, feat_width), jnp.bfloat16),
            jax.ShapeDtypeStruct((groups // 2, share, feat_width), jnp.float32),
        )
        out_specs = (vmem, vmem)
    else:
        out_shape = jax.ShapeDtypeStruct((nodes, feat_width), jnp.float32)
        out_specs = any_spec
    extra = [] if first else [acc]
    return pl.pallas_call(
        functools.partial(aggregate_kernel, offsets, groups, first, last),
        out_shape=out_shape,
        in_specs=[smem] * 3 + [any_spec] * (1 + len(units) + len(extra)),
        out_specs=out_specs,
        scratch_shapes=[
            pltpu.VMEM((n_src, feat_width, nodes), jnp.bfloat16),
            pltpu.VMEM((n_src, slots, size, size), jnp.bfloat16),
            pltpu.VMEM((nodes + size, feat_width), jnp.float32),
            pltpu.SemaphoreType.DMA((n_src, groups)),
            pltpu.SemaphoreType.DMA((n_src, slots // CHUNK)),
            pltpu.SemaphoreType.DMA,
        ],
        compiler_params=pltpu.CompilerParams(vmem_limit_bytes=40 * 1024 * 1024),
    )(rows, cols, counts, tiles, *units, *extra)


def low_bit(m):
    return m & -m


def high_bit(m):
    return 1 << (m.bit_length() - 1)


def shards(features, adj_tiles, tile_rows, tile_cols, counts, weight, cotangent):
    blocks = lax.axis_size("blk")
    groups = lax.axis_size("feat")
    width, nodes = features.shape
    feat_width = width * groups
    tile_size = adj_tiles.shape[-1]
    slot_cap = adj_tiles.shape[3]
    tiles = adj_tiles.reshape(blocks, slot_cap, tile_size, tile_size)
    rows = tile_rows.reshape(blocks, slot_cap)
    cols = tile_cols.reshape(blocks, slot_cap)
    live = counts.reshape(blocks)
    z = lax.axis_index("feat")
    chips = blocks // 2

    held = {(0, 0): features}
    for k in range(1, groups):
        bit = low_bit(k)
        held[k, 0] = hop(held[k ^ bit, 0], "feat", bit)
    for k in range(groups):
        for m in range(1, chips):
            bit = low_bit(m) if k % 2 == 0 else high_bit(m)
            held[k, m] = hop(held[k, m ^ bit], "blk", 2 * bit)
    other = {key: hop(value, "blk", 1) for key, value in held.items()}

    weights_of = [bin(m).count("1") for m in range(chips)]
    acc = None
    stages = sorted(set(weights_of))
    for stage in stages:
        offsets, units = [], []
        for m in range(chips):
            if weights_of[m] == stage:
                for side, table in ((0, held), (1, other)):
                    offsets.append(2 * m + side)
                    units += [table[k, m] for k in range(groups)]
        acc = aggregate(tuple(offsets), groups, rows, cols, live, tiles, units, acc, stage == stages[-1])
    send, keep = acc
    total = keep + hop(send, "feat", 1).astype(jnp.float32)
    bit = 2
    while bit < groups:
        mine = lax.rem(z // bit, 2)
        pairs = total.reshape(total.shape[0] // 2, 2, *total.shape[1:])
        send = lax.dynamic_index_in_dim(pairs, 1 - mine, 1, False).astype(jnp.bfloat16)
        keep = lax.dynamic_index_in_dim(pairs, mine, 1, False)
        total = keep + hop(send, "feat", bit).astype(jnp.float32)
        bit *= 2
    aggregated = total[0].astype(jnp.bfloat16)

    preact = lax.dot_general(
        weight, aggregated, (((1,), (1,)), ((), ())), preferred_element_type=jnp.float32
    )
    sigmoid_z = jax.nn.sigmoid(preact)
    activated = (preact * sigmoid_z).astype(jnp.bfloat16)
    slope = (cotangent.astype(jnp.float32) * sigmoid_z * (1.0 + preact * (1.0 - sigmoid_z))).astype(
        jnp.bfloat16
    )
    local_grad = jnp.dot(slope, aggregated, preferred_element_type=jnp.float32)
    terms = lax.all_to_all(
        local_grad.astype(jnp.bfloat16).reshape(groups, feat_width // groups, feat_width), "feat", 0, 0
    )
    grad = jnp.sum(terms.astype(jnp.float32), axis=0)
    sent = grad.astype(jnp.bfloat16)
    grad = sent.astype(jnp.float32) + hop(sent, "blk", 1).astype(jnp.float32)
    sent = grad.astype(jnp.bfloat16)
    parts = [(hop(sent, "blk", 2 * m) if m else sent).astype(jnp.float32) for m in range(chips)]
    while len(parts) > 1:
        parts = [parts[i] + parts[i + 1] for i in range(0, len(parts), 2)]
    return activated, parts[0] * (1.0 / math.sqrt(blocks * nodes))


def solution(mesh):
    in_specs = (
        P("feat", "blk"),
        P("blk", "feat", None, None, None, None),
        P("blk", "feat", None, None),
        P("blk", "feat", None, None),
        P("blk", "feat", None),
        P(),
        P(None, ("blk", "feat")),
    )
    out_specs = (P(None, ("blk", "feat")), P("feat", None))
    return jax.shard_map(shards, mesh=mesh, in_specs=in_specs, out_specs=out_specs, check_vma=False)
```

time: 432 us -> 126 us (0.29)
  waiting for transfers between devices: 242 us -> 62.3 us
  matrix products: 59.9 us -> 0.76 us
  other arithmetic: 59.5 us -> 0.84 us
  local copies, waits for them, and re-layouts: 54.8 us -> 4.01 us
  starting transfers between devices: 0.16 us -> 33.7 us
  Pallas kernels: 0 us -> 13.3 us
  between operations: 13.8 us -> 0.83 us
  blocking collectives: 0 us -> 9.1 us
    psum x1 -> x0, waiting for transfers between devices: 126 us -> none  [shards(): grad_whole = lax.psum(local_grad, ('blk', 'feat'))]
    all_gather x2 -> x0, waiting for transfers between devices: 88 us -> none  [the longest x1 55.7 us: shards(): shard_piece = lax.all_gather(full_rows, 'blk', axis=1, tiled=True)]
    ppermute x0 -> x37, waiting for transfers between devices: none -> 62.3 us  [hop(): return lax.ppermute(value, axis, [(i, i ^ bit) for i in range(size)])]
    dot_general x26 -> x2, matrix products: 59.9 us -> 0.76 us  [the longest x1 0.42 us: shards(): local_grad = jnp.dot(slope, aggregated, preferred_element_type=jnp.float32)]
    ppermute x0 -> x37, starting transfers between devices: none -> 33.7 us  [hop(): return lax.ppermute(value, axis, [(i, i ^ bit) for i in range(size)])]
    add x8 -> x1, other arithmetic: 31.2 us -> 0.1 us  [shards(): total = keep + hop(send, 'feat', 1).astype(jnp.float32)]
    reduce_scatter x1 -> x0, waiting for transfers between devices: 27.1 us -> none  [shards(): lax.psum_scatter(partial_value.astype(jnp.bfloat16), 'feat', scatter_dime...]
    gather x8 -> x0, local copies, waits for them, and re-layouts: 22.1 us -> none  [source_term(): gathered = jnp.take(col_panel, slot_cols, axis=1)]
  transfers between devices with their start and end apart: 4 -> 37, of which waited for: 4 -> 14; matrix products, arithmetic and copies ran while one was open for 0% -> 1% of each run, Pallas kernels for 0% -> 8%
where the time goes in v1:
time: 126 us; the launch traced here: 125 us
  waiting for transfers between devices  62.3 us (49%)
  starting transfers between devices  33.7 us (27%)
  Pallas kernels  13.3 us (11%)
  blocking collectives  9.1 us (7%)
  local copies, waits for them, and re-layouts  4.01 us (3%)
    ppermute x37, waiting for transfers between devices, hop(): return lax.ppermute(value, axis, [(i, i ^ bit) for i in range(size)])  62.3 us
    ppermute x37, starting transfers between devices, hop(): return lax.ppermute(value, axis, [(i, i ^ bit) for i in range(size)])  33.7 us
    pallas_call x3, Pallas kernels, aggregate(): pl.pallas_call(functools.partial(aggregate_kernel, offsets, groups, first...  13.3 us
    all_to_all x1, blocking collectives, shards(): lax.all_to_all(local_grad.astype(jnp.bfloat16).reshape(groups, feat_width...  9.1 us
    unnamed x14, local copies, waits for them, and re-layouts  3.97 us
  transfers between devices with their start and end apart: 37, of which 14 were waited for; matrix products, arithmetic and copies ran while one was open for 1% of the time, Pallas kernels for 8%

profile of v1, /device:TPU:0, one launch (start us, length us, event | category | flops | bytes accessed | tf_op | source)
XLA Modules:
  0.0 124.9 jit_solution(4059911971981773284)
XLA Ops:
  0.6 4.1 %collective-permute-start.5 = (bf16[64,2048]{1,0:T(8,128)(2,1)}, bf16[64,2048]{1,0:T(8,128)(2,1)S(1)}, u32[]{:S(2)}, u32[]{:S(2)}) collective-permute-start(bf16[64,2048]{1,0:T(8,128)(2,1)} %refs_4_.1), channel_id=1, source_target_pairs={{0,2},{1,3},{2,0},{3,1},{4,6},{5,7},{6,4},{7,5},{8,10},{9,11},{10,... | collective-permute-start | bytes 786440 | tf_op jit(solution)/shard_map/ppermute | solution.py:17
  4.7 1.6 %collective-permute-start.2 = (bf16[64,2048]{1,0:T(8,128)(2,1)}, bf16[64,2048]{1,0:T(8,128)(2,1)S(1)}, u32[]{:S(2)}, u32[]{:S(2)}) collective-permute-start(bf16[64,2048]{1,0:T(8,128)(2,1)} %refs_4_.1), channel_id=1, source_target_pairs={{0,1},{1,0},{2,3},{3,2},{4,5},{5,4},{6,7},{7,6},{8,9},{9,8},{10,11... | collective-permute-start | bytes 786440 | tf_op jit(solution)/shard_map/ppermute | solution.py:17
  6.3 1.5 %collective-permute-start = (bf16[64,2048]{1,0:T(8,128)(2,1)}, bf16[64,2048]{1,0:T(8,128)(2,1)S(1)}, u32[]{:S(2)}, u32[]{:S(2)}) collective-permute-start(bf16[64,2048]{1,0:T(8,128)(2,1)} %refs_4_.1), channel_id=1, source_target_pairs={{0,16},{4,20},{8,24},{12,28},{16,0},{20,4},{24,8},{28,12},{1,17},{... | collective-permute-start | bytes 786440 | tf_op jit(solution)/shard_map/ppermute | solution.py:17
  7.8 1.5 %collective-permute-start.15 = (bf16[64,2048]{1,0:T(8,128)(2,1)}, bf16[64,2048]{1,0:T(8,128)(2,1)S(1)}, u32[]{:S(2)}, u32[]{:S(2)}) collective-permute-start(bf16[64,2048]{1,0:T(8,128)(2,1)} %refs_4_.1), channel_id=1, source_target_pairs={{0,8},{4,12},{8,0},{12,4},{16,24},{20,28},{24,16},{28,20},{1,9},{5... | collective-permute-start | bytes 786440 | tf_op jit(solution)/shard_map/ppermute | solution.py:17
  9.3 7.6 %collective-permute-done.5.refs_6_ = bf16[64,2048]{1,0:T(8,128)(2,1)S(1)} collective-permute-done((bf16[64,2048]{1,0:T(8,128)(2,1)}, bf16[64,2048]{1,0:T(8,128)(2,1)S(1)}, u32[]{:S(2)}, u32[]{:S(2)}) %collective-permute-start.5) | collective-permute-done | bytes 262176 | tf_op jit(solution)/shard_map/ppermute | solution.py:17
  18.2 1.5 %collective-permute-start.6 = (bf16[64,2048]{1,0:T(8,128)(2,1)S(1)}, bf16[64,2048]{1,0:T(8,128)(2,1)S(1)}, u32[]{:S(2)}, u32[]{:S(2)}) collective-permute-start(bf16[64,2048]{1,0:T(8,128)(2,1)S(1)} %collective-permute-done.5.refs_6_), channel_id=1, source_target_pairs={{0,16},{4,20},{8,24},{12,28},{16,0},{20,4},{24,8},{28,12},{1,17},{... | collective-permute-start | bytes 786440 | tf_op jit(solution)/shard_map/ppermute | solution.py:17
  19.8 1.5 %collective-permute-start.3 = (bf16[64,2048]{1,0:T(8,128)(2,1)S(1)}, bf16[64,2048]{1,0:T(8,128)(2,1)S(1)}, u32[]{:S(2)}, u32[]{:S(2)}) collective-permute-start(bf16[64,2048]{1,0:T(8,128)(2,1)S(1)} %collective-permute-done.2.refs_5_), channel_id=1, source_target_pairs={{0,8},{4,12},{8,0},{12,4},{16,24},{20,28},{24,16},{28,20},{1,9},{5... | collective-permute-start | bytes 786440 | tf_op jit(solution)/shard_map/ppermute | solution.py:17
  21.2 3.2 %collective-permute-done.8.refs_7_ = bf16[64,2048]{1,0:T(8,128)(2,1)S(1)} collective-permute-done((bf16[64,2048]{1,0:T(8,128)(2,1)S(1)}, bf16[64,2048]{1,0:T(8,128)(2,1)S(1)}, u32[]{:S(2)}, u32[]{:S(2)}) %collective-permute-start.8) | collective-permute-done | bytes 262176 | tf_op jit(solution)/shard_map/ppermute | solution.py:17
  24.4 1.3 %collective-permute-start.16 = (bf16[64,2048]{1,0:T(8,128)(2,1)S(1)}, bf16[64,2048]{1,0:T(8,128)(2,1)S(1)}, u32[]{:S(2)}, u32[]{:S(2)}) collective-permute-start(bf16[64,2048]{1,0:T(8,128)(2,1)S(1)} %collective-permute-done.5.refs_6_), channel_id=1, source_target_pairs={{0,8},{4,12},{8,0},{12,4},{16,24},{20,28},{24,16},{28,20},{1,9},{5... | collective-permute-start | bytes 786440 | tf_op jit(solution)/shard_map/ppermute | solution.py:17
  25.7 1.5 %collective-permute-start.21 = (bf16[64,2048]{1,0:T(8,128)(2,1)S(1)}, bf16[64,2048]{1,0:T(8,128)(2,1)S(1)}, u32[]{:S(2)}, u32[]{:S(2)}) collective-permute-start(bf16[64,2048]{1,0:T(8,128)(2,1)S(1)} %collective-permute-done.2.refs_5_), channel_id=1, source_target_pairs={{0,16},{4,20},{8,24},{12,28},{16,0},{20,4},{24,8},{28,12},{1,17},{... | collective-permute-start | bytes 786440 | tf_op jit(solution)/shard_map/ppermute | solution.py:17
  27.7 1.2 collective-permute-done.3.refs_5_
  29.0 1.5 %collective-permute-start.1 = (bf16[64,2048]{1,0:T(8,128)(2,1)S(1)}, bf16[64,2048]{1,0:T(8,128)(2,1)S(1)}, u32[]{:S(2)}, u32[]{:S(2)}) collective-permute-start(bf16[64,2048]{1,0:T(8,128)(2,1)S(1)} %collective-permute-done.refs_12_), channel_id=1, source_target_pairs={{0,8},{4,12},{8,0},{12,4},{16,24},{20,28},{24,16},{28,20},{1,9},{5... | collective-permute-start | bytes 786440 | tf_op jit(solution)/shard_map/ppermute | solution.py:17
  30.4 4.1 %collective-permute-done.16.refs_6_ = bf16[64,2048]{1,0:T(8,128)(2,1)S(1)} collective-permute-done((bf16[64,2048]{1,0:T(8,128)(2,1)S(1)}, bf16[64,2048]{1,0:T(8,128)(2,1)S(1)}, u32[]{:S(2)}, u32[]{:S(2)}) %collective-permute-start.16) | collective-permute-done | bytes 262176 | tf_op jit(solution)/shard_map/ppermute | solution.py:17
  34.6 1.5 %collective-permute-start.9 = (bf16[64,2048]{1,0:T(8,128)(2,1)S(1)}, bf16[64,2048]{1,0:T(8,128)(2,1)S(1)}, u32[]{:S(2)}, u32[]{:S(2)}) collective-permute-start(bf16[64,2048]{1,0:T(8,128)(2,1)S(1)} %collective-permute-done.8.refs_7_), channel_id=1, source_target_pairs={{0,8},{4,12},{8,0},{12,4},{16,24},{20,28},{24,16},{28,20},{1,9},{5... | collective-permute-start | bytes 786440 | tf_op jit(solution)/shard_map/ppermute | solution.py:17
  36.6 3.6 %collective-permute-done.1.refs_4_ = bf16[64,2048]{1,0:T(8,128)(2,1)S(1)} collective-permute-done((bf16[64,2048]{1,0:T(8,128)(2,1)S(1)}, bf16[64,2048]{1,0:T(8,128)(2,1)S(1)}, u32[]{:S(2)}, u32[]{:S(2)}) %collective-permute-start.1) | collective-permute-done | bytes 262176 | tf_op jit(solution)/shard_map/ppermute | solution.py:17
  40.7 3.9 %collective-permute-done.9.refs_7_ = bf16[64,2048]{1,0:T(8,128)(2,1)S(1)} collective-permute-done((bf16[64,2048]{1,0:T(8,128)(2,1)S(1)}, bf16[64,2048]{1,0:T(8,128)(2,1)S(1)}, u32[]{:S(2)}, u32[]{:S(2)}) %collective-permute-start.9) | collective-permute-done | bytes 262176 | tf_op jit(solution)/shard_map/ppermute | solution.py:17
  44.6 1.5 %collective-permute-start.7 = (bf16[64,2048]{1,0:T(8,128)(2,1)S(1)}, bf16[64,2048]{1,0:T(8,128)(2,1)S(1)}, u32[]{:S(2)}, u32[]{:S(2)}) collective-permute-start(bf16[64,2048]{1,0:T(8,128)(2,1)S(1)} %collective-permute-done.6.refs_14_), channel_id=1, source_target_pairs={{0,8},{4,12},{8,0},{12,4},{16,24},{20,28},{24,16},{28,20},{1,9},{5... | collective-permute-start | bytes 786440 | tf_op jit(solution)/shard_map/ppermute | solution.py:17
  46.6 1.6 %collective-permute-start.10 = (bf16[64,2048]{1,0:T(8,128)(2,1)S(1)}, bf16[64,2048]{1,0:T(8,128)(2,1)S(1)}, u32[]{:S(2)}, u32[]{:S(2)}) collective-permute-start(bf16[64,2048]{1,0:T(8,128)(2,1)S(1)} %collective-permute-done.9.refs_7_), channel_id=1, source_target_pairs={{0,16},{4,20},{8,24},{12,28},{16,0},{20,4},{24,8},{28,12},{1,17},{... | collective-permute-start | bytes 786440 | tf_op jit(solution)/shard_map/ppermute | solution.py:17
  48.4 5.0 %collective-permute-done.7.refs_6_ = bf16[64,2048]{1,0:T(8,128)(2,1)S(1)} collective-permute-done((bf16[64,2048]{1,0:T(8,128)(2,1)S(1)}, bf16[64,2048]{1,0:T(8,128)(2,1)S(1)}, u32[]{:S(2)}, u32[]{:S(2)}) %collective-permute-start.7) | collective-permute-done | bytes 262176 | tf_op jit(solution)/shard_map/ppermute | solution.py:17
  53.3 1.9 %collective-permute-done.4.refs_5_ = bf16[64,2048]{1,0:T(8,128)(2,1)S(1)} collective-permute-done((bf16[64,2048]{1,0:T(8,128)(2,1)S(1)}, bf16[64,2048]{1,0:T(8,128)(2,1)S(1)}, u32[]{:S(2)}, u32[]{:S(2)}) %collective-permute-start.4) | collective-permute-done | bytes 262176 | tf_op jit(solution)/shard_map/ppermute | solution.py:17
  55.8 4.4 %collective-permute-done.10.refs_7_ = bf16[64,2048]{1,0:T(8,128)(2,1)S(1)} collective-permute-done((bf16[64,2048]{1,0:T(8,128)(2,1)S(1)}, bf16[64,2048]{1,0:T(8,128)(2,1)S(1)}, u32[]{:S(2)}, u32[]{:S(2)}) %collective-permute-start.10) | collective-permute-done | bytes 262176 | tf_op jit(solution)/shard_map/ppermute | solution.py:17
  63.2 6.0 %shard_map.86.refs_20_ = f32[2048,256]{1,0:T(8,128)S(1)} custom-call(s32[8,48]{1,0:T(8,128)S(1)} %bitcast.12, s32[8,48]{1,0:T(8,128)S(1)} %bitcast.15, s32[8]{0:T(128)S(1)} %bitcast.18, bf16[8,48,128,128]{3,2,1,0:T(8,128)(2,1)} %bitcast.21, bf16[64,2048]{1,0:T(8,128)(2,1)S(1)} %copy-done.1, bf16[64,2048]{1,0:T(8,128)(2,1)S(1)} %collective-permute-done.2.refs_5_, ...), custom_call_target="tpu_custom_call" | custom-call | tf_op jit(solution)/shard_map/pallas_call | solution.py:133
  69.2 3.8 %shard_map.87.refs_12_ = f32[2048,256]{1,0:T(8,128)S(1)} custom-call(s32[8,48]{1,0:T(8,128)S(1)} %bitcast.13, s32[8,48]{1,0:T(8,128)S(1)} %bitcast.16, s32[8]{0:T(128)S(1)} %bitcast.19, bf16[8,48,128,128]{3,2,1,0:T(8,128)(2,1)} %bitcast.22, bf16[64,2048]{1,0:T(8,128)(2,1)S(1)} %collective-permute-done.15.refs_4_, ...), custom_call_target="tpu_custom_call" | custom-call | tf_op jit(solution)/shard_map/pallas_call | solution.py:133
  73.0 3.5 %shard_map.88 = (bf16[2,512,256]{2,1,0:T(8,128)(2,1)S(1)}, f32[2,512,256]{2,1,0:T(8,128)S(1)}) custom-call(s32[8,48]{1,0:T(8,128)S(1)} %bitcast.14, s32[8,48]{1,0:T(8,128)S(1)} %bitcast.17, s32[8]{0:T(128)S(1)} %bitcast.20, bf16[8,48,128,128]{3,2,1,0:T(8,128)(2,1)} %bitcast.23, bf16[64,2048]{1,0:T(8,128)(2,1)S(1)} %collective-permute-done.1.refs_4_, ...), custom_call_target="tpu_custom_call" | custom-call | tf_op jit(solution)/shard_map/pallas_call | solution.py:133
  76.5 1.4 %collective-permute-start.31 = (bf16[2,512,256]{2,1,0:T(8,128)(2,1)S(1)}, bf16[2,512,256]{2,1,0:T(8,128)(2,1)S(1)}, u32[]{:S(2)}, u32[]{:S(2)}) collective-permute-start(bf16[2,512,256]{2,1,0:T(8,128)(2,1)S(1)} %get-tuple-element.5), channel_id=1, source_target_pairs={{0,1},{1,0},{2,3},{3,2},{4,5},{5,4},{6,7},{7,6},{8,9},{9,8},{10,11... | collective-permute-start | bytes 1572872 | tf_op jit(solution)/shard_map/ppermute | solution.py:17
  77.9 12.0 %collective-permute-done.31 = bf16[2,512,256]{2,1,0:T(8,128)(2,1)S(1)} collective-permute-done((bf16[2,512,256]{2,1,0:T(8,128)(2,1)S(1)}, bf16[2,512,256]{2,1,0:T(8,128)(2,1)S(1)}, u32[]{:S(2)}, u32[]{:S(2)}) %collective-permute-start.31) | collective-permute-done | bytes 524320 | tf_op jit(solution)/shard_map/ppermute | solution.py:17
  90.0 2.8 %collective-permute-start.32 = (bf16[1,512,256]{2,1,0:T(8,128)(2,1)S(1)}, bf16[1,512,256]{2,1,0:T(8,128)(2,1)S(1)}, u32[]{:S(2)}, u32[]{:S(2)}) collective-permute-start(bf16[1,512,256]{2,1,0:T(8,128)(2,1)S(1)} %dynamic-slice_convert_fusion), channel_id=1, source_target_pairs={{0,2},{1,3},{2,0},{3,1},{4,6},{5,7},{6,4},{7,5},{8,10},{9,11},{10,... | collective-permute-start | bytes 786440 | tf_op jit(solution)/shard_map/ppermute | solution.py:17
  93.0 10.4 %collective-permute-done.32 = bf16[1,512,256]{2,1,0:T(8,128)(2,1)S(1)} collective-permute-done((bf16[1,512,256]{2,1,0:T(8,128)(2,1)S(1)}, bf16[1,512,256]{2,1,0:T(8,128)(2,1)S(1)}, u32[]{:S(2)}, u32[]{:S(2)}) %collective-permute-start.32) | collective-permute-done | bytes 262176 | tf_op jit(solution)/shard_map/ppermute | solution.py:17
  104.2 9.1 %all_to_all.5 = bf16[4,64,256]{2,1,0:T(8,128)(2,1)S(1)} all-to-all(bf16[4,64,256]{2,1,0:T(8,128)(2,1)S(1)} %bitcast.24), channel_id=1, replica_groups=mesh['blk'=8,'feat'=4] {'feat'}, dimensions={0} | all-to-all | bytes 262144 | tf_op jit(solution)/shard_map/all_to_all | solution.py:214
  113.4 1.2 collective-permute-done.33
  115.2 4.2 %collective-permute-start.35 = (bf16[64,256]{1,0:T(8,128)(2,1)S(1)}, bf16[64,256]{1,0:T(8,128)(2,1)S(1)}, u32[]{:S(2)}, u32[]{:S(2)}) collective-permute-start(bf16[64,256]{1,0:T(8,128)(2,1)S(1)} %add_convert_fusion.1), channel_id=1, source_target_pairs={{0,16},{4,20},{8,24},{12,28},{16,0},{20,4},{24,8},{28,12},{1,17},{... | collective-permute-start | bytes 98312 | tf_op jit(solution)/shard_map/ppermute | solution.py:17
  121.3 2.9 %collective-permute-done.36 = bf16[64,256]{1,0:T(8,128)(2,1)S(1)} collective-permute-done((bf16[64,256]{1,0:T(8,128)(2,1)S(1)}, bf16[64,256]{1,0:T(8,128)(2,1)S(1)}, u32[]{:S(2)}, u32[]{:S(2)}) %collective-permute-start.36) | collective-permute-done | bytes 32800 | tf_op jit(solution)/shard_map/ppermute | solution.py:17
  (68 shorter events, 11.3 us)
Async XLA Ops:
  0.6 16.3 %collective-permute-start.5 = (bf16[64,2048]{1,0:T(8,128)(2,1)}, bf16[64,2048]{1,0:T(8,128)(2,1)S(1)}, u32[]{:S(2)}, u32[]{:S(2)}) collective-permute-start(bf16[64,2048]{1,0:T(8,128)(2,1)} %refs_4_.1), channel_id=1, source_target_pairs={{0,2},{1,3},{2,0},{3,1},{4,6},{5,7},{6,4},{7,5},{8,10},{9,11},{10,... | collective-permute-start | bytes 786440 | tf_op jit(solution)/shard_map/ppermute | solution.py:17
  4.7 13.0 %collective-permute-start.2 = (bf16[64,2048]{1,0:T(8,128)(2,1)}, bf16[64,2048]{1,0:T(8,128)(2,1)S(1)}, u32[]{:S(2)}, u32[]{:S(2)}) collective-permute-start(bf16[64,2048]{1,0:T(8,128)(2,1)} %refs_4_.1), channel_id=1, source_target_pairs={{0,1},{1,0},{2,3},{3,2},{4,5},{5,4},{6,7},{7,6},{8,9},{9,8},{10,11... | collective-permute-start | bytes 786440 | tf_op jit(solution)/shard_map/ppermute | solution.py:17
  6.3 11.4 %collective-permute-start.27 = (bf16[64,2048]{1,0:T(8,128)(2,1)}, bf16[64,2048]{1,0:T(8,128)(2,1)S(1)}, u32[]{:S(2)}, u32[]{:S(2)}) collective-permute-start(bf16[64,2048]{1,0:T(8,128)(2,1)} %refs_4_.1), channel_id=1, source_target_pairs={{0,4},{4,0},{8,12},{12,8},{16,20},{20,16},{24,28},{28,24},{1,5},{5... | collective-permute-start | bytes 786440 | tf_op jit(solution)/shard_map/ppermute | solution.py:17
  6.3 11.9 %collective-permute-start = (bf16[64,2048]{1,0:T(8,128)(2,1)}, bf16[64,2048]{1,0:T(8,128)(2,1)S(1)}, u32[]{:S(2)}, u32[]{:S(2)}) collective-permute-start(bf16[64,2048]{1,0:T(8,128)(2,1)} %refs_4_.1), channel_id=1, source_target_pairs={{0,16},{4,20},{8,24},{12,28},{16,0},{20,4},{24,8},{28,12},{1,17},{... | collective-permute-start | bytes 786440 | tf_op jit(solution)/shard_map/ppermute | solution.py:17
  7.8 11.9 %collective-permute-start.15 = (bf16[64,2048]{1,0:T(8,128)(2,1)}, bf16[64,2048]{1,0:T(8,128)(2,1)S(1)}, u32[]{:S(2)}, u32[]{:S(2)}) collective-permute-start(bf16[64,2048]{1,0:T(8,128)(2,1)} %refs_4_.1), channel_id=1, source_target_pairs={{0,8},{4,12},{8,0},{12,4},{16,24},{20,28},{24,16},{28,20},{1,9},{5... | collective-permute-start | bytes 786440 | tf_op jit(solution)/shard_map/ppermute | solution.py:17
  17.0 7.4 %collective-permute-start.8 = (bf16[64,2048]{1,0:T(8,128)(2,1)S(1)}, bf16[64,2048]{1,0:T(8,128)(2,1)S(1)}, u32[]{:S(2)}, u32[]{:S(2)}) collective-permute-start(bf16[64,2048]{1,0:T(8,128)(2,1)S(1)} %collective-permute-done.5.refs_6_), channel_id=1, source_target_pairs={{0,1},{1,0},{2,3},{3,2},{4,5},{5,4},{6,7},{7,6},{8,9},{9,8},{10,11... | collective-permute-start | bytes 786440 | tf_op jit(solution)/shard_map/ppermute | solution.py:17
  17.7 8.0 %collective-permute-start.29 = (bf16[64,2048]{1,0:T(8,128)(2,1)S(1)}, bf16[64,2048]{1,0:T(8,128)(2,1)S(1)}, u32[]{:S(2)}, u32[]{:S(2)}) collective-permute-start(bf16[64,2048]{1,0:T(8,128)(2,1)S(1)} %collective-permute-done.5.refs_6_), channel_id=1, source_target_pairs={{0,4},{4,0},{8,12},{12,8},{16,20},{20,16},{24,28},{28,24},{1,5},{5... | collective-permute-start | bytes 786440 | tf_op jit(solution)/shard_map/ppermute | solution.py:17
  17.7 9.5 %collective-permute-start.28 = (bf16[64,2048]{1,0:T(8,128)(2,1)S(1)}, bf16[64,2048]{1,0:T(8,128)(2,1)S(1)}, u32[]{:S(2)}, u32[]{:S(2)}) collective-permute-start(bf16[64,2048]{1,0:T(8,128)(2,1)S(1)} %collective-permute-done.2.refs_5_), channel_id=1, source_target_pairs={{0,4},{4,0},{8,12},{12,8},{16,20},{20,16},{24,28},{28,24},{1,5},{5... | collective-permute-start | bytes 786440 | tf_op jit(solution)/shard_map/ppermute | solution.py:17
  18.2 9.0 %collective-permute-start.6 = (bf16[64,2048]{1,0:T(8,128)(2,1)S(1)}, bf16[64,2048]{1,0:T(8,128)(2,1)S(1)}, u32[]{:S(2)}, u32[]{:S(2)}) collective-permute-start(bf16[64,2048]{1,0:T(8,128)(2,1)S(1)} %collective-permute-done.5.refs_6_), channel_id=1, source_target_pairs={{0,16},{4,20},{8,24},{12,28},{16,0},{20,4},{24,8},{28,12},{1,17},{... | collective-permute-start | bytes 786440 | tf_op jit(solution)/shard_map/ppermute | solution.py:17
  19.8 9.2 %collective-permute-start.3 = (bf16[64,2048]{1,0:T(8,128)(2,1)S(1)}, bf16[64,2048]{1,0:T(8,128)(2,1)S(1)}, u32[]{:S(2)}, u32[]{:S(2)}) collective-permute-start(bf16[64,2048]{1,0:T(8,128)(2,1)S(1)} %collective-permute-done.2.refs_5_), channel_id=1, source_target_pairs={{0,8},{4,12},{8,0},{12,4},{16,24},{20,28},{24,16},{28,20},{1,9},{5... | collective-permute-start | bytes 786440 | tf_op jit(solution)/shard_map/ppermute | solution.py:17
  24.4 10.2 %collective-permute-start.16 = (bf16[64,2048]{1,0:T(8,128)(2,1)S(1)}, bf16[64,2048]{1,0:T(8,128)(2,1)S(1)}, u32[]{:S(2)}, u32[]{:S(2)}) collective-permute-start(bf16[64,2048]{1,0:T(8,128)(2,1)S(1)} %collective-permute-done.5.refs_6_), channel_id=1, source_target_pairs={{0,8},{4,12},{8,0},{12,4},{16,24},{20,28},{24,16},{28,20},{1,9},{5... | collective-permute-start | bytes 786440 | tf_op jit(solution)/shard_map/ppermute | solution.py:17
  25.7 8.9 %collective-permute-start.21 = (bf16[64,2048]{1,0:T(8,128)(2,1)S(1)}, bf16[64,2048]{1,0:T(8,128)(2,1)S(1)}, u32[]{:S(2)}, u32[]{:S(2)}) collective-permute-start(bf16[64,2048]{1,0:T(8,128)(2,1)S(1)} %collective-permute-done.2.refs_5_), channel_id=1, source_target_pairs={{0,16},{4,20},{8,24},{12,28},{16,0},{20,4},{24,8},{28,12},{1,17},{... | collective-permute-start | bytes 786440 | tf_op jit(solution)/shard_map/ppermute | solution.py:17
  27.2 8.9 %collective-permute-start.23 = (bf16[64,2048]{1,0:T(8,128)(2,1)S(1)}, bf16[64,2048]{1,0:T(8,128)(2,1)S(1)}, u32[]{:S(2)}, u32[]{:S(2)}) collective-permute-start(bf16[64,2048]{1,0:T(8,128)(2,1)S(1)} %collective-permute-done.refs_12_), channel_id=1, source_target_pairs={{0,4},{4,0},{8,12},{12,8},{16,20},{20,16},{24,28},{28,24},{1,5},{5... | collective-permute-start | bytes 786440 | tf_op jit(solution)/shard_map/ppermute | solution.py:17
  27.2 9.4 %collective-permute-start.17 = (bf16[64,2048]{1,0:T(8,128)(2,1)S(1)}, bf16[64,2048]{1,0:T(8,128)(2,1)S(1)}, u32[]{:S(2)}, u32[]{:S(2)}) collective-permute-start(bf16[64,2048]{1,0:T(8,128)(2,1)S(1)} %collective-permute-done.15.refs_4_), channel_id=1, source_target_pairs={{0,4},{4,0},{8,12},{12,8},{16,20},{20,16},{24,28},{28,24},{1,5},{5... | collective-permute-start | bytes 786440 | tf_op jit(solution)/shard_map/ppermute | solution.py:17
  29.0 11.2 %collective-permute-start.1 = (bf16[64,2048]{1,0:T(8,128)(2,1)S(1)}, bf16[64,2048]{1,0:T(8,128)(2,1)S(1)}, u32[]{:S(2)}, u32[]{:S(2)}) collective-permute-start(bf16[64,2048]{1,0:T(8,128)(2,1)S(1)} %collective-permute-done.refs_12_), channel_id=1, source_target_pairs={{0,8},{4,12},{8,0},{12,4},{16,24},{20,28},{24,16},{28,20},{1,9},{5... | collective-permute-start | bytes 786440 | tf_op jit(solution)/shard_map/ppermute | solution.py:17
  34.6 10.0 %collective-permute-start.9 = (bf16[64,2048]{1,0:T(8,128)(2,1)S(1)}, bf16[64,2048]{1,0:T(8,128)(2,1)S(1)}, u32[]{:S(2)}, u32[]{:S(2)}) collective-permute-start(bf16[64,2048]{1,0:T(8,128)(2,1)S(1)} %collective-permute-done.8.refs_7_), channel_id=1, source_target_pairs={{0,8},{4,12},{8,0},{12,4},{16,24},{20,28},{24,16},{28,20},{1,9},{5... | collective-permute-start | bytes 786440 | tf_op jit(solution)/shard_map/ppermute | solution.py:17
  36.1 8.5 %collective-permute-start.22 = (bf16[64,2048]{1,0:T(8,128)(2,1)S(1)}, bf16[64,2048]{1,0:T(8,128)(2,1)S(1)}, u32[]{:S(2)}, u32[]{:S(2)}) collective-permute-start(bf16[64,2048]{1,0:T(8,128)(2,1)S(1)} %collective-permute-done.8.refs_7_), channel_id=1, source_target_pairs={{0,16},{4,20},{8,24},{12,28},{16,0},{20,4},{24,8},{28,12},{1,17},{... | collective-permute-start | bytes 786440 | tf_op jit(solution)/shard_map/ppermute | solution.py:17
  36.6 9.5 %collective-permute-start.25 = (bf16[64,2048]{1,0:T(8,128)(2,1)S(1)}, bf16[64,2048]{1,0:T(8,128)(2,1)S(1)}, u32[]{:S(2)}, u32[]{:S(2)}) collective-permute-start(bf16[64,2048]{1,0:T(8,128)(2,1)S(1)} %collective-permute-done.6.refs_14_), channel_id=1, source_target_pairs={{0,4},{4,0},{8,12},{12,8},{16,20},{20,16},{24,28},{28,24},{1,5},{5... | collective-permute-start | bytes 786440 | tf_op jit(solution)/shard_map/ppermute | solution.py:17
  40.2 6.4 %collective-permute-start.18 = (bf16[64,2048]{1,0:T(8,128)(2,1)S(1)}, bf16[64,2048]{1,0:T(8,128)(2,1)S(1)}, u32[]{:S(2)}, u32[]{:S(2)}) collective-permute-start(bf16[64,2048]{1,0:T(8,128)(2,1)S(1)} %collective-permute-done.3.refs_5_), channel_id=1, source_target_pairs={{0,4},{4,0},{8,12},{12,8},{16,20},{20,16},{24,28},{28,24},{1,5},{5... | collective-permute-start | bytes 786440 | tf_op jit(solution)/shard_map/ppermute | solution.py:17
  40.2 6.4 %collective-permute-start.19 = (bf16[64,2048]{1,0:T(8,128)(2,1)S(1)}, bf16[64,2048]{1,0:T(8,128)(2,1)S(1)}, u32[]{:S(2)}, u32[]{:S(2)}) collective-permute-start(bf16[64,2048]{1,0:T(8,128)(2,1)S(1)} %collective-permute-done.16.refs_6_), channel_id=1, source_target_pairs={{0,4},{4,0},{8,12},{12,8},{16,20},{20,16},{24,28},{28,24},{1,5},{5... | collective-permute-start | bytes 786440 | tf_op jit(solution)/shard_map/ppermute | solution.py:17
  44.6 8.7 %collective-permute-start.7 = (bf16[64,2048]{1,0:T(8,128)(2,1)S(1)}, bf16[64,2048]{1,0:T(8,128)(2,1)S(1)}, u32[]{:S(2)}, u32[]{:S(2)}) collective-permute-start(bf16[64,2048]{1,0:T(8,128)(2,1)S(1)} %collective-permute-done.6.refs_14_), channel_id=1, source_target_pairs={{0,8},{4,12},{8,0},{12,4},{16,24},{20,28},{24,16},{28,20},{1,9},{5... | collective-permute-start | bytes 786440 | tf_op jit(solution)/shard_map/ppermute | solution.py:17
  46.1 9.1 %collective-permute-start.4 = (bf16[64,2048]{1,0:T(8,128)(2,1)S(1)}, bf16[64,2048]{1,0:T(8,128)(2,1)S(1)}, u32[]{:S(2)}, u32[]{:S(2)}) collective-permute-start(bf16[64,2048]{1,0:T(8,128)(2,1)S(1)} %collective-permute-done.3.refs_5_), channel_id=1, source_target_pairs={{0,16},{4,20},{8,24},{12,28},{16,0},{20,4},{24,8},{28,12},{1,17},{... | collective-permute-start | bytes 786440 | tf_op jit(solution)/shard_map/ppermute | solution.py:17
  46.6 8.6 %collective-permute-start.20 = (bf16[64,2048]{1,0:T(8,128)(2,1)S(1)}, bf16[64,2048]{1,0:T(8,128)(2,1)S(1)}, u32[]{:S(2)}, u32[]{:S(2)}) collective-permute-start(bf16[64,2048]{1,0:T(8,128)(2,1)S(1)} %collective-permute-done.9.refs_7_), channel_id=1, source_target_pairs={{0,4},{4,0},{8,12},{12,8},{16,20},{20,16},{24,28},{28,24},{1,5},{5... | collective-permute-start | bytes 786440 | tf_op jit(solution)/shard_map/ppermute | solution.py:17
  46.6 13.5 %collective-permute-start.10 = (bf16[64,2048]{1,0:T(8,128)(2,1)S(1)}, bf16[64,2048]{1,0:T(8,128)(2,1)S(1)}, u32[]{:S(2)}, u32[]{:S(2)}) collective-permute-start(bf16[64,2048]{1,0:T(8,128)(2,1)S(1)} %collective-permute-done.9.refs_7_), channel_id=1, source_target_pairs={{0,16},{4,20},{8,24},{12,28},{16,0},{20,4},{24,8},{28,12},{1,17},{... | collective-permute-start | bytes 786440 | tf_op jit(solution)/shard_map/ppermute | solution.py:17
  48.2 24.8 %collective-permute-start.11 = (bf16[64,2048]{1,0:T(8,128)(2,1)S(1)}, bf16[64,2048]{1,0:T(8,128)(2,1)S(1)}, u32[]{:S(2)}, u32[]{:S(2)}) collective-permute-start(bf16[64,2048]{1,0:T(8,128)(2,1)S(1)} %collective-permute-done.1.refs_4_), channel_id=1, source_target_pairs={{0,4},{4,0},{8,12},{12,8},{16,20},{20,16},{24,28},{28,24},{1,5},{5... | collective-permute-start | bytes 786440 | tf_op jit(solution)/shard_map/ppermute | solution.py:17
  53.3 15.9 %collective-permute-start.26 = (bf16[64,2048]{1,0:T(8,128)(2,1)S(1)}, bf16[64,2048]{1,0:T(8,128)(2,1)S(1)}, u32[]{:S(2)}, u32[]{:S(2)}) collective-permute-start(bf16[64,2048]{1,0:T(8,128)(2,1)S(1)} %collective-permute-done.22.refs_15_), channel_id=1, source_target_pairs={{0,4},{4,0},{8,12},{12,8},{16,20},{20,16},{24,28},{28,24},{1,5},{5... | collective-permute-start | bytes 786440 | tf_op jit(solution)/shard_map/ppermute | solution.py:17
  55.3 17.7 %collective-permute-start.13 = (bf16[64,2048]{1,0:T(8,128)(2,1)S(1)}, bf16[64,2048]{1,0:T(8,128)(2,1)S(1)}, u32[]{:S(2)}, u32[]{:S(2)}) collective-permute-start(bf16[64,2048]{1,0:T(8,128)(2,1)S(1)} %collective-permute-done.7.refs_6_), channel_id=1, source_target_pairs={{0,4},{4,0},{8,12},{12,8},{16,20},{20,16},{24,28},{28,24},{1,5},{5... | collective-permute-start | bytes 786440 | tf_op jit(solution)/shard_map/ppermute | solution.py:17
  55.3 17.7 %collective-permute-start.12 = (bf16[64,2048]{1,0:T(8,128)(2,1)S(1)}, bf16[64,2048]{1,0:T(8,128)(2,1)S(1)}, u32[]{:S(2)}, u32[]{:S(2)}) collective-permute-start(bf16[64,2048]{1,0:T(8,128)(2,1)S(1)} %collective-permute-done.4.refs_5_), channel_id=1, source_target_pairs={{0,4},{4,0},{8,12},{12,8},{16,20},{20,16},{24,28},{28,24},{1,5},{5... | collective-permute-start | bytes 786440 | tf_op jit(solution)/shard_map/ppermute | solution.py:17
  60.2 12.8 %collective-permute-start.14 = (bf16[64,2048]{1,0:T(8,128)(2,1)S(1)}, bf16[64,2048]{1,0:T(8,128)(2,1)S(1)}, u32[]{:S(2)}, u32[]{:S(2)}) collective-permute-start(bf16[64,2048]{1,0:T(8,128)(2,1)S(1)} %collective-permute-done.10.refs_7_), channel_id=1, source_target_pairs={{0,4},{4,0},{8,12},{12,8},{16,20},{20,16},{24,28},{28,24},{1,5},{5... | collective-permute-start | bytes 786440 | tf_op jit(solution)/shard_map/ppermute | solution.py:17
  76.5 13.3 %collective-permute-start.31 = (bf16[2,512,256]{2,1,0:T(8,128)(2,1)S(1)}, bf16[2,512,256]{2,1,0:T(8,128)(2,1)S(1)}, u32[]{:S(2)}, u32[]{:S(2)}) collective-permute-start(bf16[2,512,256]{2,1,0:T(8,128)(2,1)S(1)} %get-tuple-element.5), channel_id=1, source_target_pairs={{0,1},{1,0},{2,3},{3,2},{4,5},{5,4},{6,7},{7,6},{8,9},{9,8},{10,11... | collective-permute-start | bytes 1572872 | tf_op jit(solution)/shard_map/ppermute | solution.py:17
  90.0 13.3 %collective-permute-start.32 = (bf16[1,512,256]{2,1,0:T(8,128)(2,1)S(1)}, bf16[1,512,256]{2,1,0:T(8,128)(2,1)S(1)}, u32[]{:S(2)}, u32[]{:S(2)}) collective-permute-start(bf16[1,512,256]{2,1,0:T(8,128)(2,1)S(1)} %dynamic-slice_convert_fusion), channel_id=1, source_target_pairs={{0,2},{1,3},{2,0},{3,1},{4,6},{5,7},{6,4},{7,5},{8,10},{9,11},{10,... | collective-permute-start | bytes 786440 | tf_op jit(solution)/shard_map/ppermute | solution.py:17
  115.2 6.1 %collective-permute-start.35 = (bf16[64,256]{1,0:T(8,128)(2,1)S(1)}, bf16[64,256]{1,0:T(8,128)(2,1)S(1)}, u32[]{:S(2)}, u32[]{:S(2)}) collective-permute-start(bf16[64,256]{1,0:T(8,128)(2,1)S(1)} %add_convert_fusion.1), channel_id=1, source_target_pairs={{0,16},{4,20},{8,24},{12,28},{16,0},{20,4},{24,8},{28,12},{1,17},{... | collective-permute-start | bytes 98312 | tf_op jit(solution)/shard_map/ppermute | solution.py:17
  (11 other events, 143.3 us)

commit v2 on v1

v2 whole, which is shorter than its diff:
```python
import functools
import math

import jax
import jax.numpy as jnp
from jax import lax
from jax.experimental import pallas as pl
from jax.experimental.pallas import tpu as pltpu
from jax.sharding import PartitionSpec as P

CHUNK = 8
EARLY = 10**10
WIDE = 16


def hop(value, axis, bit):
    size = lax.axis_size(axis)
    return lax.ppermute(value, axis, [(i, i ^ bit) for i in range(size)])


def in_hbm(*values):
    return [pltpu.with_memory_space_constraint(value, pltpu.HBM) for value in values]


def in_vmem(*values):
    return [pltpu.with_memory_space_constraint(value, pltpu.VMEM) for value in values]


def pair_kernel(own_ref, sibling_ref, *refs):
    core = lax.rem(lax.axis_index("blk"), 2)
    refs[-1][core] = own_ref[...]
    refs[-1][1 - core] = sibling_ref[...]


def pick_kernel(even_ref, odd_ref, *refs):
    core = lax.rem(lax.axis_index("blk"), 2)

    @pl.when(core == 0)
    def _():
        refs[-1][...] = even_ref[...]

    @pl.when(core == 1)
    def _():
        refs[-1][...] = odd_ref[...]


def pick_part_kernel(pair_ref, *refs):
    refs[-1][...] = pair_ref[lax.rem(lax.axis_index("blk"), 2)]


def copying(kernel, shape, values, earlier, flops=0):
    vmem = pl.BlockSpec(memory_space=pltpu.VMEM)
    return pl.pallas_call(
        kernel,
        out_shape=pltpu.VMEM(shape, values[0].dtype),
        in_specs=[vmem] * len(values) + [pl.BlockSpec(memory_space=pl.ANY)] * len(earlier),
        out_specs=vmem,
        compiler_params=pltpu.CompilerParams(vmem_limit_bytes=1024 * 1024),
        cost_estimate=pl.CostEstimate(
            flops=flops, bytes_accessed=4 * math.prod(shape), transcendentals=0
        ),
    )(*in_vmem(*values), *earlier)


def same_kernel(value_ref, *refs):
    refs[-1][...] = value_ref[...]


def after(value, *earlier, flops=0):
    return copying(same_kernel, value.shape, [value], earlier, flops)


def pair_of(own, sibling, *earlier):
    return copying(pair_kernel, (2, *own.shape), [own, sibling], earlier)


def pick(even, odd, *earlier):
    return copying(pick_kernel, even.shape, [even, odd], earlier)


def pick_part(pair, *earlier):
    return copying(pick_part_kernel, pair.shape[1:], [pair], earlier)


def aggregate_kernel(sources, n_units, n_earlier, halves, first, *refs):
    *list_hbm, tiles_ref = refs[:4]
    unit_refs = refs[4 : 4 + n_units]
    rest = list(refs[4 + n_units + n_earlier :])
    acc_in = None if first else rest.pop(0)
    n_out = 4 if halves else 1
    out_refs = rest[:n_out]
    rows_ref, cols_ref, counts_ref, feat, tiles, acc, unit_sems, tile_sems, list_sems, acc_sem = rest[n_out:]
    blk = lax.axis_index("blk")
    z = lax.axis_index("feat")
    n_src = len(sources)
    groups = len(sources[0][1])
    slots = tiles_ref.shape[3]
    size = tiles_ref.shape[4]
    width, nodes = unit_refs[0].shape[-2:]
    row_tiles = nodes // size
    chunks = slots // CHUNK
    odd = lax.rem(blk, 2) == 1

    def unit_copy(i, k, side=0):
        unit, part = sources[i][1][k][side]
        ref = unit_refs[unit] if part is None else unit_refs[unit].at[part]
        start = pl.multiple_of(lax.bitwise_xor(z, jnp.int32(k)) * width, width)
        return pltpu.make_async_copy(ref, feat.at[i, pl.ds(start, width), :], unit_sems.at[i, k])

    def start_unit_copy(i, k):
        even, on_odd = sources[i][1][k]
        if even == on_odd:
            unit_copy(i, k).start()
            return
        pl.when(jnp.logical_not(odd))(lambda: unit_copy(i, k, 0).start())
        pl.when(odd)(lambda: unit_copy(i, k, 1).start())

    def tile_copy(i, chunk):
        at = pl.ds(chunk * CHUNK, CHUNK)
        return pltpu.make_async_copy(
            tiles_ref.at[0, 0, parts[i], at], tiles.at[i, at], tile_sems.at[i, chunk]
        )

    list_copies = [
        pltpu.make_async_copy(source, target, list_sems.at[i])
        for i, (source, target) in enumerate(zip(list_hbm, (rows_ref, cols_ref, counts_ref)))
    ]
    for copy in list_copies:
        copy.start()
    if not first:
        acc_copy = pltpu.make_async_copy(acc_in, acc.at[pl.ds(0, nodes)], acc_sem)
        acc_copy.start()
    for i in range(n_src):
        for k in range(groups):
            start_unit_copy(i, k)
    for copy in list_copies:
        copy.wait()
    parts = [lax.bitwise_xor(blk, jnp.int32(off)) for off, _ in sources]
    live = [counts_ref[0, 0, part] for part in parts]
    for i in range(n_src):
        for chunk in range(chunks):

            @pl.when(chunk * CHUNK < live[i])
            def _():
                tile_copy(i, chunk).start()

    if first:
        acc[pl.ds(0, nodes), :] = jnp.zeros((nodes, acc.shape[1]), jnp.float32)
    else:
        acc_copy.wait()
    for i in range(n_src):
        for k in range(groups):
            unit_copy(i, k).wait()
        for chunk in range(chunks):

            @pl.when(chunk * CHUNK < live[i])
            def _():
                tile_copy(i, chunk).wait()

        def add_tiles(base, count):
            for u in range(count):
                slot = base + u
                row = jnp.where(slot < live[i], rows_ref[0, 0, parts[i], slot], row_tiles)
                col = cols_ref[0, 0, parts[i], slot]
                term = lax.dot_general(
                    tiles[i, slot],
                    feat[i, :, pl.ds(pl.multiple_of(col * size, size), size)],
                    (((1,), (1,)), ((), ())),
                    preferred_element_type=jnp.float32,
                )
                acc[pl.ds(pl.multiple_of(row * size, size), size), :] += term
            return 0

        wide = live[i] // WIDE
        left = (live[i] - wide * WIDE + CHUNK - 1) // CHUNK
        lax.fori_loop(0, wide, lambda p, _: add_tiles(p * WIDE, WIDE), 0)
        lax.fori_loop(0, left, lambda p, _: add_tiles(wide * WIDE + p * CHUNK, CHUNK), 0)
    if not halves:
        out_copy = pltpu.make_async_copy(acc.at[pl.ds(0, nodes)], out_refs[0], acc_sem)
        out_copy.start()
        out_copy.wait()
        return
    share = nodes // groups
    half = share // 2
    for part, bit in ((0, 1), (1, 2)):
        send_ref, keep_ref = out_refs[2 * part : 2 * part + 2]
        for j, step in enumerate((0, 3 ^ bit)):
            mine = lax.bitwise_xor(z, jnp.int32(step)) * share + part * half
            theirs = lax.bitwise_xor(z, jnp.int32(step ^ bit)) * share + part * half
            keep_ref[j] = acc[pl.ds(pl.multiple_of(mine, half), half), :]
            send_ref[j] = acc[pl.ds(pl.multiple_of(theirs, half), half), :].astype(jnp.bfloat16)


def aggregate(sources, lists, units, acc, halves, earlier=()):
    rows, cols, counts, tiles = lists
    n_src = len(sources)
    groups = len(sources[0][1])
    slots, size = tiles.shape[3], tiles.shape[4]
    width, nodes = units[0].shape[-2:]
    feat_width = width * groups
    any_spec = pl.BlockSpec(memory_space=pl.ANY)
    vmem = pl.BlockSpec(memory_space=pltpu.VMEM)
    if halves:
        dims = (2, nodes // groups // 2, feat_width)
        out_shape = [jax.ShapeDtypeStruct(dims, jnp.bfloat16), jax.ShapeDtypeStruct(dims, jnp.float32)] * 2
        out_spec = vmem
    else:
        out_shape = [jax.ShapeDtypeStruct((nodes, feat_width), jnp.float32)]
        out_spec = any_spec
    extra = [] if acc is None else [acc]
    return pl.pallas_call(
        functools.partial(aggregate_kernel, sources, len(units), len(earlier), halves, acc is None),
        out_shape=tuple(out_shape),
        in_specs=[any_spec] * (4 + len(units) + len(earlier) + len(extra)),
        out_specs=(out_spec,) * len(out_shape),
        scratch_shapes=[
            pltpu.SMEM(rows.shape, jnp.int32),
            pltpu.SMEM(cols.shape, jnp.int32),
            pltpu.SMEM(counts.shape, jnp.int32),
            pltpu.VMEM((n_src, feat_width, nodes), jnp.bfloat16),
            pltpu.VMEM((n_src, slots, size, size), jnp.bfloat16),
            pltpu.VMEM((nodes + size, feat_width), jnp.float32),
            pltpu.SemaphoreType.DMA((n_src, groups)),
            pltpu.SemaphoreType.DMA((n_src, slots // CHUNK)),
            pltpu.SemaphoreType.DMA((3,)),
            pltpu.SemaphoreType.DMA,
        ],
        compiler_params=pltpu.CompilerParams(vmem_limit_bytes=(6 + 3 * n_src) * 1024 * 1024),
        cost_estimate=pl.CostEstimate(
            flops=2 * n_src * slots * size * size * feat_width * 4,
            bytes_accessed=n_src * (slots * size * size + feat_width * nodes) * 2,
            transcendentals=0,
        ),
    )(*in_hbm(rows, cols, counts, tiles), *units, *earlier, *extra)


def low_bit(m):
    return m & -m


def plain(first, groups):
    return tuple(((first + k, None),) * 2 for k in range(groups))


def gather_any(features, lists):
    groups, chips = lax.axis_size("feat"), lax.axis_size("blk") // 2
    held = {(0, 0): features}
    for k in range(1, groups):
        bit = low_bit(k)
        held[k, 0] = hop(held[k ^ bit, 0], "feat", bit)
    for k in range(groups):
        for m in range(1, chips):
            bit = low_bit(m) if k % 2 == 0 else 1 << (m.bit_length() - 1)
            held[k, m] = hop(held[k, m ^ bit], "blk", 2 * bit)
    other = {key: hop(value, "blk", 1) for key, value in held.items()}
    acc = None
    for m in range(chips):
        sources, units = [], []
        for side, table in ((0, held), (1, other)):
            sources.append((2 * m + side, plain(len(units), groups)))
            units += [table[k, m] for k in range(groups)]
        acc = aggregate(tuple(sources), lists, units, acc, False)[0]
    return acc


def sum_any(total, groups):
    z = lax.axis_index("feat")
    total = total.reshape(groups, total.shape[0] // groups, total.shape[1])
    bit = 1
    while bit < groups:
        mine = lax.rem(z // bit, 2)
        pairs = total.reshape(total.shape[0] // 2, 2, *total.shape[1:])
        send = lax.dynamic_index_in_dim(pairs, 1 - mine, 1, False).astype(jnp.bfloat16)
        keep = lax.dynamic_index_in_dim(pairs, mine, 1, False)
        total = keep + hop(send, "feat", bit).astype(jnp.float32)
        bit *= 2
    return total[0].astype(jnp.bfloat16)


def gather_2x2x4(features, lists):
    def swap(value):
        return hop(value, "blk", 1)

    def cross(value, even_bit, odd_bit):
        perm = [(i, i ^ (odd_bit if i % 2 else even_bit)) for i in range(8)]
        return lax.ppermute(value, "blk", perm)

    own, sibling, near, distant, distant_too = {0: features}, {}, {}, {}, {}
    own[2] = after(hop(own[0], "feat", 2), flops=4 * EARLY)
    own[1] = hop(own[0], "feat", 1)
    beside = [hop(own[0], "blk", 2), hop(own[0], "blk", 4)]
    sibling[0] = swap(own[0])
    distant[0] = cross(pick(beside[1], beside[0]), 2, 4)
    sibling[1] = swap(own[1])
    near[1] = cross(pair_of(own[1], sibling[1], own[2], distant[0]), 2, 4)
    own[3] = hop(own[2], "feat", 1)
    sibling[2] = swap(own[2])
    distant[3] = hop(distant[0], "feat", 3)
    distant_too[3] = swap(distant[3])
    near[2] = cross(pair_of(own[2], sibling[2], near[1]), 2, 4)
    distant[1] = hop(distant[0], "feat", 1)
    distant_too[1] = swap(distant[1])
    sibling[3] = swap(own[3])
    near[3] = cross(pair_of(own[3], sibling[3], near[2], distant_too[3]), 2, 4)
    distant[2] = after(cross(pick_part(near[2]), 4, 2), flops=EARLY)

    units = [own[k] for k in range(4)] + [sibling[k] for k in range(4)]
    sources = ((0, plain(0, 4)), (1, plain(4, 4)))
    acc = aggregate(sources, lists, units, None, False)[0]

    beside_too = [swap(pick(beside[0], beside[0], acc)), swap(beside[1])]
    near_too = {k: swap(near[k]) for k in range(1, 4)}
    for k in (0, 2):
        distant_too[k] = swap(distant[k])
    units = [distant[k] for k in range(4)] + [distant_too[k] for k in range(4)]
    units += [near[k] for k in range(1, 4)] + [near_too[k] for k in range(1, 4)] + beside + beside_too
    sources = [(6, plain(0, 4)), (7, plain(4, 4))]
    for along, bit in enumerate((2, 4)):
        for side in range(2):
            slices = [((14 + 2 * side + along, None),) * 2]
            for k in range(1, 4):
                table = (8, 11) if along == 0 else (11, 8)
                slices.append(((table[0] + k - 1, side), (table[1] + k - 1, 1 - side)))
            sources.append((bit + side, tuple(slices)))
    return aggregate(tuple(sources), lists, units, acc, True)


def sum_2x2x4(send_a, keep_a, send_b, keep_b):
    got_a = hop(send_a, "feat", 1).astype(jnp.float32)
    got_b = hop(send_b, "feat", 2).astype(jnp.float32)
    more_a = hop((keep_a[1] + got_a[1]).astype(jnp.bfloat16), "feat", 2).astype(jnp.float32)
    more_b = hop((keep_b[1] + got_b[1]).astype(jnp.bfloat16), "feat", 1).astype(jnp.float32)
    total = [keep_a[0] + got_a[0] + more_a, keep_b[0] + got_b[0] + more_b]
    return jnp.concatenate(total).astype(jnp.bfloat16)


def shards(features, adj_tiles, tile_rows, tile_cols, counts, weight, cotangent):
    blocks = lax.axis_size("blk")
    groups = lax.axis_size("feat")
    width, nodes = features.shape
    feat_width = width * groups
    chips = blocks // 2
    lists = (tile_rows, tile_cols, counts, adj_tiles)

    if blocks == 8 and groups == 4:
        aggregated = sum_2x2x4(*gather_2x2x4(features, lists))
    else:
        aggregated = sum_any(gather_any(features, lists), groups)

    preact = lax.dot_general(
        weight, aggregated, (((1,), (1,)), ((), ())), preferred_element_type=jnp.float32
    )
    sigmoid_z = jax.nn.sigmoid(preact)
    activated = (preact * sigmoid_z).astype(jnp.bfloat16)
    slope = (cotangent.astype(jnp.float32) * sigmoid_z * (1.0 + preact * (1.0 - sigmoid_z))).astype(
        jnp.bfloat16
    )
    local_grad = jnp.dot(slope, aggregated, preferred_element_type=jnp.float32)
    terms = lax.all_to_all(
        local_grad.astype(jnp.bfloat16).reshape(groups, feat_width // groups, feat_width), "feat", 0, 0
    )
    grad = jnp.sum(terms.astype(jnp.float32), axis=0)
    sent = grad.astype(jnp.bfloat16)
    grad = sent.astype(jnp.float32) + hop(sent, "blk", 1).astype(jnp.float32)
    sent = grad.astype(jnp.bfloat16)
    parts = [(hop(sent, "blk", 2 * m) if m else sent).astype(jnp.float32) for m in range(chips)]
    while len(parts) > 1:
        parts = [parts[i] + parts[i + 1] for i in range(0, len(parts), 2)]
    return activated, parts[0] * (1.0 / math.sqrt(blocks * nodes))


def solution(mesh):
    in_specs = (
        P("feat", "blk"),
        P("blk", "feat", None, None, None, None),
        P("blk", "feat", None, None),
        P("blk", "feat", None, None),
        P("blk", "feat", None),
        P(),
        P(None, ("blk", "feat")),
    )
    out_specs = (P(None, ("blk", "feat")), P("feat", None))
    return jax.shard_map(shards, mesh=mesh, in_specs=in_specs, out_specs=out_specs, check_vma=False)
```

time: 126 us -> 103 us (0.82); the launches traced: 125 us -> 104 us
  starting transfers between devices: 33.7 us -> 26.2 us
  waiting for transfers between devices: 62.3 us -> 54.8 us
  Pallas kernels: 13.3 us -> 9.42 us
  local copies, waits for them, and re-layouts: 4.01 us -> 1 us
    ppermute x37 -> x28, waiting for transfers between devices: 62.3 us -> 44.8 us  [hop(): return lax.ppermute(value, axis, [(i, i ^ bit) for i in range(size)])]
    ppermute x37 -> x28, starting transfers between devices: 33.7 us -> 22.3 us  [hop(): return lax.ppermute(value, axis, [(i, i ^ bit) for i in range(size)])]
    ppermute x0 -> x5, waiting for transfers between devices: none -> 9.99 us  [cross(): return lax.ppermute(value, 'blk', perm)]
    ppermute x0 -> x5, starting transfers between devices: none -> 3.93 us  [cross(): return lax.ppermute(value, 'blk', perm)]
    pallas_call x3 -> x10, Pallas kernels: 13.3 us -> 9.42 us  [the longest x2 9.15 us: aggregate(): pl.pallas_call(functools.partial(aggregate_kernel, sources, len(units), l...]
    unnamed x14 -> x8, local copies, waits for them, and re-layouts: 3.97 us -> 1 us
  transfers between devices with their start and end apart: 37 -> 33, of which waited for: 14 -> 20; matrix products, arithmetic and copies ran while one was open for 1% -> 1% of each run, Pallas kernels for 8% -> 5%
where the time goes in v2:
time: 103 us; the launch traced here: 104 us
  waiting for transfers between devices  54.8 us (53%)
  starting transfers between devices  26.2 us (25%)
  blocking collectives  9.99 us (10%)
  Pallas kernels  9.42 us (9%)
    ppermute x28, waiting for transfers between devices, hop(): return lax.ppermute(value, axis, [(i, i ^ bit) for i in range(size)])  44.8 us
    ppermute x28, starting transfers between devices, hop(): return lax.ppermute(value, axis, [(i, i ^ bit) for i in range(size)])  22.3 us
    ppermute x5, waiting for transfers between devices, cross(): return lax.ppermute(value, 'blk', perm)  9.99 us
    all_to_all x1, blocking collectives, shards(): lax.all_to_all(local_grad.astype(jnp.bfloat16).reshape(groups, feat_width...  9.99 us
    pallas_call x2, Pallas kernels, aggregate(): pl.pallas_call(functools.partial(aggregate_kernel, sources, len(units), l...  9.15 us
    ppermute x5, starting transfers between devices, cross(): return lax.ppermute(value, 'blk', perm)  3.93 us
  transfers between devices with their start and end apart: 33, of which 20 were waited for; matrix products, arithmetic and copies ran while one was open for 1% of the time, Pallas kernels for 5%

profile of v2, /device:TPU:0, one launch (start us, length us, event | category | flops | bytes accessed | tf_op | source)
XLA Modules:
  0.0 104.0 jit_solution(16511933770908231164)
XLA Ops:
  0.6 3.0 %collective-permute-start = (bf16[64,2048]{1,0:T(8,128)(2,1)}, bf16[64,2048]{1,0:T(8,128)(2,1)S(1)}, u32[]{:S(2)}, u32[]{:S(2)}) collective-permute-start(bf16[64,2048]{1,0:T(8,128)(2,1)} %refs_4_.1), channel_id=1, source_target_pairs={{0,16},{4,20},{8,24},{12,28},{16,0},{20,4},{24,8},{28,12},{1,17},{... | collective-permute-start | bytes 786440 | tf_op jit(solution)/shard_map/ppermute | solution.py:18
  3.7 1.5 %collective-permute-start.1 = (bf16[64,2048]{1,0:T(8,128)(2,1)}, bf16[64,2048]{1,0:T(8,128)(2,1)S(1)}, u32[]{:S(2)}, u32[]{:S(2)}) collective-permute-start(bf16[64,2048]{1,0:T(8,128)(2,1)} %refs_4_.1), channel_id=1, source_target_pairs={{0,8},{4,12},{8,0},{12,4},{16,24},{20,28},{24,16},{28,20},{1,9},{5... | collective-permute-start | bytes 786440 | tf_op jit(solution)/shard_map/ppermute | solution.py:18
  5.2 1.6 %collective-permute-start.6 = (bf16[64,2048]{1,0:T(8,128)(2,1)}, bf16[64,2048]{1,0:T(8,128)(2,1)S(1)}, u32[]{:S(2)}, u32[]{:S(2)}) collective-permute-start(bf16[64,2048]{1,0:T(8,128)(2,1)} %refs_4_.1), channel_id=1, source_target_pairs={{0,1},{1,0},{2,3},{3,2},{4,5},{5,4},{6,7},{7,6},{8,9},{9,8},{10,11... | collective-permute-start | bytes 786440 | tf_op jit(solution)/shard_map/ppermute | solution.py:18
  6.7 2.6 %collective-permute-start.4 = (bf16[64,2048]{1,0:T(8,128)(2,1)}, bf16[64,2048]{1,0:T(8,128)(2,1)S(1)}, u32[]{:S(2)}, u32[]{:S(2)}) collective-permute-start(bf16[64,2048]{1,0:T(8,128)(2,1)} %refs_4_.1), channel_id=1, source_target_pairs={{0,2},{1,3},{2,0},{3,1},{4,6},{5,7},{6,4},{7,5},{8,10},{9,11},{10,... | collective-permute-start | bytes 786440 | tf_op jit(solution)/shard_map/ppermute | solution.py:18
  9.3 0.9 collective-permute-done.even_ref.refs_19_
  10.2 1.5 %collective-permute-done.1.odd_ref.even_ref.refs_18_ = bf16[64,2048]{1,0:T(8,128)(2,1)S(1)} collective-permute-done((bf16[64,2048]{1,0:T(8,128)(2,1)}, bf16[64,2048]{1,0:T(8,128)(2,1)S(1)}, u32[]{:S(2)}, u32[]{:S(2)}) %collective-permute-start.1) | collective-permute-done | bytes 262176 | tf_op jit(solution)/shard_map/ppermute | solution.py:18
  11.7 1.6 %collective-permute-start.2 = (bf16[64,2048]{1,0:T(8,128)(2,1)S(1)}, bf16[64,2048]{1,0:T(8,128)(2,1)S(1)}, u32[]{:S(2)}, u32[]{:S(2)}) collective-permute-start(bf16[64,2048]{1,0:T(8,128)(2,1)S(1)} %shard_map.86), channel_id=1, source_target_pairs={{0,8},{4,20},{8,0},{12,28},{16,24},{20,4},{24,16},{28,12},{1,9},{5... | collective-permute-start | bytes 786440 | tf_op jit(solution)/shard_map/ppermute | solution.py:286
  13.2 5.1 %collective-permute-done.6.own_ref.refs_5_ = bf16[64,2048]{1,0:T(8,128)(2,1)S(1)} collective-permute-done((bf16[64,2048]{1,0:T(8,128)(2,1)}, bf16[64,2048]{1,0:T(8,128)(2,1)S(1)}, u32[]{:S(2)}, u32[]{:S(2)}) %collective-permute-start.6) | collective-permute-done | bytes 262176 | tf_op jit(solution)/shard_map/ppermute | solution.py:18
  18.4 2.4 %collective-permute-done.4.value_ref = bf16[64,2048]{1,0:T(8,128)(2,1)S(1)} collective-permute-done((bf16[64,2048]{1,0:T(8,128)(2,1)}, bf16[64,2048]{1,0:T(8,128)(2,1)S(1)}, u32[]{:S(2)}, u32[]{:S(2)}) %collective-permute-start.4) | collective-permute-done | bytes 262176 | tf_op jit(solution)/shard_map/ppermute | solution.py:18
  21.9 2.0 %collective-permute-start.11 = (bf16[64,2048]{1,0:T(8,128)(2,1)S(1)}, bf16[64,2048]{1,0:T(8,128)(2,1)S(1)}, u32[]{:S(2)}, u32[]{:S(2)}) collective-permute-start(bf16[64,2048]{1,0:T(8,128)(2,1)S(1)} %collective-permute-done.2.refs_1_.refs_4_), channel_id=1, source_target_pairs={{0,3},{1,2},{2,1},{3,0},{4,7},{5,6},{6,5},{7,4},{8,11},{9,10},{10,... | collective-permute-start | bytes 786440 | tf_op jit(solution)/shard_map/ppermute | solution.py:18
  23.9 6.2 %collective-permute-done.8.refs_0_.refs_12_ = bf16[2,64,2048]{2,1,0:T(8,128)(2,1)S(1)} collective-permute-done((bf16[2,64,2048]{2,1,0:T(8,128)(2,1)S(1)}, bf16[2,64,2048]{2,1,0:T(8,128)(2,1)S(1)}, u32[]{:S(2)}, u32[]{:S(2)}) %collective-permute-start.8) | collective-permute-done | bytes 524320 | tf_op jit(solution)/shard_map/ppermute | solution.py:286
  30.8 5.9 %collective-permute-done.11.refs_7_ = bf16[64,2048]{1,0:T(8,128)(2,1)S(1)} collective-permute-done((bf16[64,2048]{1,0:T(8,128)(2,1)S(1)}, bf16[64,2048]{1,0:T(8,128)(2,1)S(1)}, u32[]{:S(2)}, u32[]{:S(2)}) %collective-permute-start.11) | collective-permute-done | bytes 262176 | tf_op jit(solution)/shard_map/ppermute | solution.py:18
  37.1 1.0 collective-permute-done.15.refs_1_.refs_11_
  38.1 1.2 %collective-permute-done.9.pair_ref.refs_0_.refs_13_ = bf16[2,64,2048]{2,1,0:T(8,128)(2,1)S(1)} collective-permute-done((bf16[2,64,2048]{2,1,0:T(8,128)(2,1)S(1)}, bf16[2,64,2048]{2,1,0:T(8,128)(2,1)S(1)}, u32[]{:S(2)}, u32[]{:S(2)}) %collective-permute-start.9) | collective-permute-done | bytes 524320 | tf_op jit(solution)/shard_map/ppermute | solution.py:286
  41.5 4.5 %shard_map.93.refs_0_.refs_22_ = f32[2048,256]{1,0:T(8,128)S(1)} custom-call(s32[1,1,8,48]{3,2,1,0:T(8,128)} %refs_0_.3, s32[1,1,8,48]{3,2,1,0:T(8,128)} %refs_1_.3, s32[1,1,8]{2,1,0:T(1,128)} %refs_2_.3, bf16[1,1,8,48,128,128]{5,4,3,2,1,0:T(8,128)(2,1)} %refs_3_.3, bf16[64,2048]{1,0:T(8,128)(2,1)S(1)} %copy-done.1, ...), custom_call_target="tpu_custom_call" | custom-call | flops 3221225472 | bytes 5242880 | tf_op jit(solution)/shard_map/pallas_call | solution.py:211
  46.1 0.8 collective-permute-start.23
  46.9 1.8 %collective-permute-done.3.refs_5_ = bf16[64,2048]{1,0:T(8,128)(2,1)S(1)} collective-permute-done((bf16[64,2048]{1,0:T(8,128)(2,1)S(1)}, bf16[64,2048]{1,0:T(8,128)(2,1)S(1)}, u32[]{:S(2)}, u32[]{:S(2)}) %collective-permute-start.3) | collective-permute-done | bytes 262176 | tf_op jit(solution)/shard_map/ppermute | solution.py:18
  49.6 1.9 %collective-permute-done.18.refs_14_ = bf16[2,64,2048]{2,1,0:T(8,128)(2,1)S(1)} collective-permute-done((bf16[2,64,2048]{2,1,0:T(8,128)(2,1)S(1)}, bf16[2,64,2048]{2,1,0:T(8,128)(2,1)S(1)}, u32[]{:S(2)}, u32[]{:S(2)}) %collective-permute-start.18) | collective-permute-done | bytes 524320 | tf_op jit(solution)/shard_map/ppermute | solution.py:286
  52.2 1.6 %collective-permute-done.13.refs_9_ = bf16[64,2048]{1,0:T(8,128)(2,1)S(1)} collective-permute-done((bf16[64,2048]{1,0:T(8,128)(2,1)S(1)}, bf16[64,2048]{1,0:T(8,128)(2,1)S(1)}, u32[]{:S(2)}, u32[]{:S(2)}) %collective-permute-start.13) | collective-permute-done | bytes 262176 | tf_op jit(solution)/shard_map/ppermute | solution.py:18
  54.2 4.6 %shard_map.95 = (bf16[2,256,256]{2,1,0:T(8,128)(2,1)S(1)}, f32[2,256,256]{2,1,0:T(8,128)S(1)}, bf16[2,256,256]{2,1,0:T(8,128)(2,1)S(1)}, f32[2,256,256]{2,1,0:T(8,128)S(1)}) custom-call(s32[1,1,8,48]{3,2,1,0:T(8,128)} %refs_0_.3, s32[1,1,8,48]{3,2,1,0:T(8,128)} %refs_1_.3, s32[1,1,8]{2,1,0:T(1,128)} %refs_2_.3, bf16[1,1,8,48,128,128]{5,4,3,2,1,0:T(8,128)(2,1)} %refs_3_.3, ...), custom_call_target="tpu_custom_call" | custom-call | flops 9663676416 | bytes 15728640 | tf_op jit(solution)/shard_map/pallas_call | solution.py:211
  59.3 2.6 %collective-permute-start.27 = (bf16[2,256,256]{2,1,0:T(8,128)(2,1)S(1)}, bf16[2,256,256]{2,1,0:T(8,128)(2,1)S(1)}, u32[]{:S(2)}, u32[]{:S(2)}) collective-permute-start(bf16[2,256,256]{2,1,0:T(8,128)(2,1)S(1)} %get-tuple-element.9), channel_id=1, source_target_pairs={{0,2},{1,3},{2,0},{3,1},{4,6},{5,7},{6,4},{7,5},{8,10},{9,11},{10,... | collective-permute-start | bytes 786440 | tf_op jit(solution)/shard_map/ppermute | solution.py:18
  62.0 11.1 %collective-permute-done.25 = bf16[2,256,256]{2,1,0:T(8,128)(2,1)S(1)} collective-permute-done((bf16[2,256,256]{2,1,0:T(8,128)(2,1)S(1)}, bf16[2,256,256]{2,1,0:T(8,128)(2,1)S(1)}, u32[]{:S(2)}, u32[]{:S(2)}) %collective-permute-start.25) | collective-permute-done | bytes 262176 | tf_op jit(solution)/shard_map/ppermute | solution.py:18
  73.3 0.9 collective-permute-done.27
  74.9 6.4 %collective-permute-done.26 = bf16[256,256]{1,0:T(8,128)(2,1)S(1)} collective-permute-done((bf16[256,256]{1,0:T(8,128)(2,1)S(1)}, bf16[256,256]{1,0:T(8,128)(2,1)S(1)}, u32[]{:S(2)}, u32[]{:S(2)}) %collective-permute-start.26) | collective-permute-done | bytes 131104 | tf_op jit(solution)/shard_map/ppermute | solution.py:18
  81.3 0.8 collective-permute-done.28
  82.9 10.0 %all_to_all.5 = bf16[4,64,256]{2,1,0:T(8,128)(2,1)S(1)} all-to-all(bf16[4,64,256]{2,1,0:T(8,128)(2,1)S(1)} %bitcast.20), channel_id=1, replica_groups=mesh['blk'=8,'feat'=4] {'feat'}, dimensions={0} | all-to-all | bytes 262144 | tf_op jit(solution)/shard_map/all_to_all | solution.py:359
  93.0 1.2 %collective-permute-done.29 = bf16[64,256]{1,0:T(8,128)(2,1)S(1)} collective-permute-done((bf16[64,256]{1,0:T(8,128)(2,1)S(1)}, bf16[64,256]{1,0:T(8,128)(2,1)S(1)}, u32[]{:S(2)}, u32[]{:S(2)}) %collective-permute-start.29) | collective-permute-done | bytes 32800 | tf_op jit(solution)/shard_map/ppermute | solution.py:18
  94.2 2.9 %collective-permute-start.30 = (bf16[64,256]{1,0:T(8,128)(2,1)S(1)}, bf16[64,256]{1,0:T(8,128)(2,1)S(1)}, u32[]{:S(2)}, u32[]{:S(2)}) collective-permute-start(bf16[64,256]{1,0:T(8,128)(2,1)S(1)} %add_convert_fusion), channel_id=1, source_target_pairs={{0,8},{4,12},{8,0},{12,4},{16,24},{20,28},{24,16},{28,20},{1,9},{5... | collective-permute-start | bytes 98312 | tf_op jit(solution)/shard_map/ppermute | solution.py:18
  97.1 1.4 %collective-permute-start.31 = (bf16[64,256]{1,0:T(8,128)(2,1)S(1)}, bf16[64,256]{1,0:T(8,128)(2,1)S(1)}, u32[]{:S(2)}, u32[]{:S(2)}) collective-permute-start(bf16[64,256]{1,0:T(8,128)(2,1)S(1)} %add_convert_fusion), channel_id=1, source_target_pairs={{0,16},{4,20},{8,24},{12,28},{16,0},{20,4},{24,8},{28,12},{1,17},{... | collective-permute-start | bytes 98312 | tf_op jit(solution)/shard_map/ppermute | solution.py:18
  98.6 0.8 copy.10
  99.5 1.5 %collective-permute-done.31 = bf16[64,256]{1,0:T(8,128)(2,1)S(1)} collective-permute-done((bf16[64,256]{1,0:T(8,128)(2,1)S(1)}, bf16[64,256]{1,0:T(8,128)(2,1)S(1)}, u32[]{:S(2)}, u32[]{:S(2)}) %collective-permute-start.31) | collective-permute-done | bytes 32800 | tf_op jit(solution)/shard_map/ppermute | solution.py:18
  101.0 2.3 %collective-permute-done.32 = bf16[64,256]{1,0:T(8,128)(2,1)S(1)} collective-permute-done((bf16[64,256]{1,0:T(8,128)(2,1)S(1)}, bf16[64,256]{1,0:T(8,128)(2,1)S(1)}, u32[]{:S(2)}, u32[]{:S(2)}) %collective-permute-start.32) | collective-permute-done | bytes 32800 | tf_op jit(solution)/shard_map/ppermute | solution.py:18
  (64 shorter events, 9.4 us)
Async XLA Ops:
  0.6 9.6 %collective-permute-start = (bf16[64,2048]{1,0:T(8,128)(2,1)}, bf16[64,2048]{1,0:T(8,128)(2,1)S(1)}, u32[]{:S(2)}, u32[]{:S(2)}) collective-permute-start(bf16[64,2048]{1,0:T(8,128)(2,1)} %refs_4_.1), channel_id=1, source_target_pairs={{0,16},{4,20},{8,24},{12,28},{16,0},{20,4},{24,8},{28,12},{1,17},{... | collective-permute-start | bytes 786440 | tf_op jit(solution)/shard_map/ppermute | solution.py:18
  3.7 8.0 %collective-permute-start.1 = (bf16[64,2048]{1,0:T(8,128)(2,1)}, bf16[64,2048]{1,0:T(8,128)(2,1)S(1)}, u32[]{:S(2)}, u32[]{:S(2)}) collective-permute-start(bf16[64,2048]{1,0:T(8,128)(2,1)} %refs_4_.1), channel_id=1, source_target_pairs={{0,8},{4,12},{8,0},{12,4},{16,24},{20,28},{24,16},{28,20},{1,9},{5... | collective-permute-start | bytes 786440 | tf_op jit(solution)/shard_map/ppermute | solution.py:18
  5.2 13.2 %collective-permute-start.6 = (bf16[64,2048]{1,0:T(8,128)(2,1)}, bf16[64,2048]{1,0:T(8,128)(2,1)S(1)}, u32[]{:S(2)}, u32[]{:S(2)}) collective-permute-start(bf16[64,2048]{1,0:T(8,128)(2,1)} %refs_4_.1), channel_id=1, source_target_pairs={{0,1},{1,0},{2,3},{3,2},{4,5},{5,4},{6,7},{7,6},{8,9},{9,8},{10,11... | collective-permute-start | bytes 786440 | tf_op jit(solution)/shard_map/ppermute | solution.py:18
  6.7 14.0 %collective-permute-start.4 = (bf16[64,2048]{1,0:T(8,128)(2,1)}, bf16[64,2048]{1,0:T(8,128)(2,1)S(1)}, u32[]{:S(2)}, u32[]{:S(2)}) collective-permute-start(bf16[64,2048]{1,0:T(8,128)(2,1)} %refs_4_.1), channel_id=1, source_target_pairs={{0,2},{1,3},{2,0},{3,1},{4,6},{5,7},{6,4},{7,5},{8,10},{9,11},{10,... | collective-permute-start | bytes 786440 | tf_op jit(solution)/shard_map/ppermute | solution.py:18
  11.7 9.1 %collective-permute-start.2 = (bf16[64,2048]{1,0:T(8,128)(2,1)S(1)}, bf16[64,2048]{1,0:T(8,128)(2,1)S(1)}, u32[]{:S(2)}, u32[]{:S(2)}) collective-permute-start(bf16[64,2048]{1,0:T(8,128)(2,1)S(1)} %shard_map.86), channel_id=1, source_target_pairs={{0,8},{4,20},{8,0},{12,28},{16,24},{20,4},{24,16},{28,12},{1,9},{5... | collective-permute-start | bytes 786440 | tf_op jit(solution)/shard_map/ppermute | solution.py:286
  18.4 2.4 %collective-permute-start.7 = (bf16[64,2048]{1,0:T(8,128)(2,1)S(1)}, bf16[64,2048]{1,0:T(8,128)(2,1)S(1)}, u32[]{:S(2)}, u32[]{:S(2)}) collective-permute-start(bf16[64,2048]{1,0:T(8,128)(2,1)S(1)} %collective-permute-done.6.own_ref.refs_5_), channel_id=1, source_target_pairs={{0,4},{4,0},{8,12},{12,8},{16,20},{20,16},{24,28},{28,24},{1,5},{5... | collective-permute-start | bytes 786440 | tf_op jit(solution)/shard_map/ppermute | solution.py:18
  20.8 9.2 %collective-permute-start.8 = (bf16[2,64,2048]{2,1,0:T(8,128)(2,1)S(1)}, bf16[2,64,2048]{2,1,0:T(8,128)(2,1)S(1)}, u32[]{:S(2)}, u32[]{:S(2)}) collective-permute-start(bf16[2,64,2048]{2,1,0:T(8,128)(2,1)S(1)} %shard_map.88), channel_id=1, source_target_pairs={{0,8},{4,20},{8,0},{12,28},{16,24},{20,4},{24,16},{28,12},{1,9},{5... | collective-permute-start | bytes 1572872 | tf_op jit(solution)/shard_map/ppermute | solution.py:286
  21.4 2.5 %collective-permute-start.5 = (bf16[64,2048]{1,0:T(8,128)(2,1)S(1)}, bf16[64,2048]{1,0:T(8,128)(2,1)S(1)}, u32[]{:S(2)}, u32[]{:S(2)}) collective-permute-start(bf16[64,2048]{1,0:T(8,128)(2,1)S(1)} %shard_map.87.refs_0_.own_ref.refs_6_), channel_id=1, source_target_pairs={{0,4},{4,0},{8,12},{12,8},{16,20},{20,16},{24,28},{28,24},{1,5},{5... | collective-permute-start | bytes 786440 | tf_op jit(solution)/shard_map/ppermute | solution.py:18
  21.4 9.3 %collective-permute-start.16 = (bf16[64,2048]{1,0:T(8,128)(2,1)S(1)}, bf16[64,2048]{1,0:T(8,128)(2,1)S(1)}, u32[]{:S(2)}, u32[]{:S(2)}) collective-permute-start(bf16[64,2048]{1,0:T(8,128)(2,1)S(1)} %shard_map.87.refs_0_.own_ref.refs_6_), channel_id=1, source_target_pairs={{0,1},{1,0},{2,3},{3,2},{4,5},{5,4},{6,7},{7,6},{8,9},{9,8},{10,11... | collective-permute-start | bytes 786440 | tf_op jit(solution)/shard_map/ppermute | solution.py:18
  21.9 14.7 %collective-permute-start.11 = (bf16[64,2048]{1,0:T(8,128)(2,1)S(1)}, bf16[64,2048]{1,0:T(8,128)(2,1)S(1)}, u32[]{:S(2)}, u32[]{:S(2)}) collective-permute-start(bf16[64,2048]{1,0:T(8,128)(2,1)S(1)} %collective-permute-done.2.refs_1_.refs_4_), channel_id=1, source_target_pairs={{0,3},{1,2},{2,1},{3,0},{4,7},{5,6},{6,5},{7,4},{8,11},{9,10},{10,... | collective-permute-start | bytes 786440 | tf_op jit(solution)/shard_map/ppermute | solution.py:18
  30.1 9.2 %collective-permute-start.9 = (bf16[2,64,2048]{2,1,0:T(8,128)(2,1)S(1)}, bf16[2,64,2048]{2,1,0:T(8,128)(2,1)S(1)}, u32[]{:S(2)}, u32[]{:S(2)}) collective-permute-start(bf16[2,64,2048]{2,1,0:T(8,128)(2,1)S(1)} %shard_map.89), channel_id=1, source_target_pairs={{0,8},{4,20},{8,0},{12,28},{16,24},{20,4},{24,16},{28,12},{1,9},{5... | collective-permute-start | bytes 1572872 | tf_op jit(solution)/shard_map/ppermute | solution.py:286
  30.8 6.4 %collective-permute-start.17 = (bf16[64,2048]{1,0:T(8,128)(2,1)S(1)}, bf16[64,2048]{1,0:T(8,128)(2,1)S(1)}, u32[]{:S(2)}, u32[]{:S(2)}) collective-permute-start(bf16[64,2048]{1,0:T(8,128)(2,1)S(1)} %collective-permute-done.16.own_ref.refs_7_), channel_id=1, source_target_pairs={{0,4},{4,0},{8,12},{12,8},{16,20},{20,16},{24,28},{28,24},{1,5},{5... | collective-permute-start | bytes 786440 | tf_op jit(solution)/shard_map/ppermute | solution.py:18
  36.6 1.5 %collective-permute-start.15 = (bf16[64,2048]{1,0:T(8,128)(2,1)S(1)}, bf16[64,2048]{1,0:T(8,128)(2,1)S(1)}, u32[]{:S(2)}, u32[]{:S(2)}) collective-permute-start(bf16[64,2048]{1,0:T(8,128)(2,1)S(1)} %collective-permute-done.11.refs_7_), channel_id=1, source_target_pairs={{0,4},{4,0},{8,12},{12,8},{16,20},{20,16},{24,28},{28,24},{1,5},{5... | collective-permute-start | bytes 786440 | tf_op jit(solution)/shard_map/ppermute | solution.py:18
  36.6 4.3 %collective-permute-start.22 = (bf16[64,2048]{1,0:T(8,128)(2,1)S(1)}, bf16[64,2048]{1,0:T(8,128)(2,1)S(1)}, u32[]{:S(2)}, u32[]{:S(2)}) collective-permute-start(bf16[64,2048]{1,0:T(8,128)(2,1)S(1)} %copy-done.1), channel_id=1, source_target_pairs={{0,4},{4,0},{8,12},{12,8},{16,20},{20,16},{24,28},{28,24},{1,5},{5... | collective-permute-start | bytes 786440 | tf_op jit(solution)/shard_map/ppermute | solution.py:18
  39.4 12.1 %collective-permute-start.18 = (bf16[2,64,2048]{2,1,0:T(8,128)(2,1)S(1)}, bf16[2,64,2048]{2,1,0:T(8,128)(2,1)S(1)}, u32[]{:S(2)}, u32[]{:S(2)}) collective-permute-start(bf16[2,64,2048]{2,1,0:T(8,128)(2,1)S(1)} %shard_map.92), channel_id=1, source_target_pairs={{0,8},{4,20},{8,0},{12,28},{16,24},{20,4},{24,16},{28,12},{1,9},{5... | collective-permute-start | bytes 1572872 | tf_op jit(solution)/shard_map/ppermute | solution.py:286
  40.0 6.0 %collective-permute-start.24 = (bf16[64,2048]{1,0:T(8,128)(2,1)S(1)}, bf16[64,2048]{1,0:T(8,128)(2,1)S(1)}, u32[]{:S(2)}, u32[]{:S(2)}) collective-permute-start(bf16[64,2048]{1,0:T(8,128)(2,1)S(1)} %collective-permute-done.even_ref.refs_19_), channel_id=1, source_target_pairs={{0,4},{4,0},{8,12},{12,8},{16,20},{20,16},{24,28},{28,24},{1,5},{5... | collective-permute-start | bytes 786440 | tf_op jit(solution)/shard_map/ppermute | solution.py:18
  40.1 8.7 %collective-permute-start.3 = (bf16[64,2048]{1,0:T(8,128)(2,1)S(1)}, bf16[64,2048]{1,0:T(8,128)(2,1)S(1)}, u32[]{:S(2)}, u32[]{:S(2)}) collective-permute-start(bf16[64,2048]{1,0:T(8,128)(2,1)S(1)} %collective-permute-done.2.refs_1_.refs_4_), channel_id=1, source_target_pairs={{0,1},{1,0},{2,3},{3,2},{4,5},{5,4},{6,7},{7,6},{8,9},{9,8},{10,11... | collective-permute-start | bytes 786440 | tf_op jit(solution)/shard_map/ppermute | solution.py:18
  40.7 10.9 %collective-permute-start.12 = (bf16[64,2048]{1,0:T(8,128)(2,1)S(1)}, bf16[64,2048]{1,0:T(8,128)(2,1)S(1)}, u32[]{:S(2)}, u32[]{:S(2)}) collective-permute-start(bf16[64,2048]{1,0:T(8,128)(2,1)S(1)} %collective-permute-done.2.refs_1_.refs_4_), channel_id=1, source_target_pairs={{0,4},{4,0},{8,12},{12,8},{16,20},{20,16},{24,28},{28,24},{1,5},{5... | collective-permute-start | bytes 786440 | tf_op jit(solution)/shard_map/ppermute | solution.py:18
  40.9 8.5 %collective-permute-start.10 = (bf16[64,2048]{1,0:T(8,128)(2,1)S(1)}, bf16[64,2048]{1,0:T(8,128)(2,1)S(1)}, u32[]{:S(2)}, u32[]{:S(2)}) collective-permute-start(bf16[64,2048]{1,0:T(8,128)(2,1)S(1)} %shard_map.90), channel_id=1, source_target_pairs={{0,16},{4,12},{8,24},{12,4},{16,0},{20,28},{24,8},{28,20},{1,17},{... | collective-permute-start | bytes 786440 | tf_op jit(solution)/shard_map/ppermute | solution.py:286
  46.1 6.0 %collective-permute-start.23 = (bf16[64,2048]{1,0:T(8,128)(2,1)S(1)}, bf16[64,2048]{1,0:T(8,128)(2,1)S(1)}, u32[]{:S(2)}, u32[]{:S(2)}) collective-permute-start(bf16[64,2048]{1,0:T(8,128)(2,1)S(1)} %shard_map.94), channel_id=1, source_target_pairs={{0,4},{4,0},{8,12},{12,8},{16,20},{20,16},{24,28},{28,24},{1,5},{5... | collective-permute-start | bytes 786440 | tf_op jit(solution)/shard_map/ppermute | solution.py:18
  48.8 5.0 %collective-permute-start.19 = (bf16[2,64,2048]{2,1,0:T(8,128)(2,1)S(1)}, bf16[2,64,2048]{2,1,0:T(8,128)(2,1)S(1)}, u32[]{:S(2)}, u32[]{:S(2)}) collective-permute-start(bf16[2,64,2048]{2,1,0:T(8,128)(2,1)S(1)} %collective-permute-done.8.refs_0_.refs_12_), channel_id=1, source_target_pairs={{0,4},{4,0},{8,12},{12,8},{16,20},{20,16},{24,28},{28,24},{1,5},{5... | collective-permute-start | bytes 1572872 | tf_op jit(solution)/shard_map/ppermute | solution.py:18
  49.4 4.7 %collective-permute-start.20 = (bf16[2,64,2048]{2,1,0:T(8,128)(2,1)S(1)}, bf16[2,64,2048]{2,1,0:T(8,128)(2,1)S(1)}, u32[]{:S(2)}, u32[]{:S(2)}) collective-permute-start(bf16[2,64,2048]{2,1,0:T(8,128)(2,1)S(1)} %collective-permute-done.9.pair_ref.refs_0_.refs_13_), channel_id=1, source_target_pairs={{0,4},{4,0},{8,12},{12,8},{16,20},{20,16},{24,28},{28,24},{1,5},{5... | collective-permute-start | bytes 1572872 | tf_op jit(solution)/shard_map/ppermute | solution.py:18
  51.5 2.7 %collective-permute-start.21 = (bf16[2,64,2048]{2,1,0:T(8,128)(2,1)S(1)}, bf16[2,64,2048]{2,1,0:T(8,128)(2,1)S(1)}, u32[]{:S(2)}, u32[]{:S(2)}) collective-permute-start(bf16[2,64,2048]{2,1,0:T(8,128)(2,1)S(1)} %collective-permute-done.18.refs_14_), channel_id=1, source_target_pairs={{0,4},{4,0},{8,12},{12,8},{16,20},{20,16},{24,28},{28,24},{1,5},{5... | collective-permute-start | bytes 1572872 | tf_op jit(solution)/shard_map/ppermute | solution.py:18
  51.6 2.2 %collective-permute-start.13 = (bf16[64,2048]{1,0:T(8,128)(2,1)S(1)}, bf16[64,2048]{1,0:T(8,128)(2,1)S(1)}, u32[]{:S(2)}, u32[]{:S(2)}) collective-permute-start(bf16[64,2048]{1,0:T(8,128)(2,1)S(1)} %collective-permute-done.3.refs_5_), channel_id=1, source_target_pairs={{0,4},{4,0},{8,12},{12,8},{16,20},{20,16},{24,28},{28,24},{1,5},{5... | collective-permute-start | bytes 786440 | tf_op jit(solution)/shard_map/ppermute | solution.py:18
  52.1 2.0 %collective-permute-start.14 = (bf16[64,2048]{1,0:T(8,128)(2,1)S(1)}, bf16[64,2048]{1,0:T(8,128)(2,1)S(1)}, u32[]{:S(2)}, u32[]{:S(2)}) collective-permute-start(bf16[64,2048]{1,0:T(8,128)(2,1)S(1)} %shard_map.91.refs_6_), channel_id=1, source_target_pairs={{0,4},{4,0},{8,12},{12,8},{16,20},{20,16},{24,28},{28,24},{1,5},{5... | collective-permute-start | bytes 786440 | tf_op jit(solution)/shard_map/ppermute | solution.py:18
  58.8 14.4 %collective-permute-start.25 = (bf16[2,256,256]{2,1,0:T(8,128)(2,1)S(1)}, bf16[2,256,256]{2,1,0:T(8,128)(2,1)S(1)}, u32[]{:S(2)}, u32[]{:S(2)}) collective-permute-start(bf16[2,256,256]{2,1,0:T(8,128)(2,1)S(1)} %get-tuple-element.7), channel_id=1, source_target_pairs={{0,1},{1,0},{2,3},{3,2},{4,5},{5,4},{6,7},{7,6},{8,9},{9,8},{10,11... | collective-permute-start | bytes 786440 | tf_op jit(solution)/shard_map/ppermute | solution.py:18
  59.3 15.0 %collective-permute-start.27 = (bf16[2,256,256]{2,1,0:T(8,128)(2,1)S(1)}, bf16[2,256,256]{2,1,0:T(8,128)(2,1)S(1)}, u32[]{:S(2)}, u32[]{:S(2)}) collective-permute-start(bf16[2,256,256]{2,1,0:T(8,128)(2,1)S(1)} %get-tuple-element.9), channel_id=1, source_target_pairs={{0,2},{1,3},{2,0},{3,1},{4,6},{5,7},{6,4},{7,5},{8,10},{9,11},{10,... | collective-permute-start | bytes 786440 | tf_op jit(solution)/shard_map/ppermute | solution.py:18
  73.3 8.0 %collective-permute-start.26 = (bf16[256,256]{1,0:T(8,128)(2,1)S(1)}, bf16[256,256]{1,0:T(8,128)(2,1)S(1)}, u32[]{:S(2)}, u32[]{:S(2)}) collective-permute-start(bf16[256,256]{1,0:T(8,128)(2,1)S(1)} %fusion.8), channel_id=1, source_target_pairs={{0,2},{1,3},{2,0},{3,1},{4,6},{5,7},{6,4},{7,5},{8,10},{9,11},{10,... | collective-permute-start | bytes 393224 | tf_op jit(solution)/shard_map/ppermute | solution.py:18
  74.4 7.7 %collective-permute-start.28 = (bf16[256,256]{1,0:T(8,128)(2,1)S(1)}, bf16[256,256]{1,0:T(8,128)(2,1)S(1)}, u32[]{:S(2)}, u32[]{:S(2)}) collective-permute-start(bf16[256,256]{1,0:T(8,128)(2,1)S(1)} %fusion.9), channel_id=1, source_target_pairs={{0,1},{1,0},{2,3},{3,2},{4,5},{5,4},{6,7},{7,6},{8,9},{9,8},{10,11... | collective-permute-start | bytes 393224 | tf_op jit(solution)/shard_map/ppermute | solution.py:18
  94.2 5.2 %collective-permute-start.30 = (bf16[64,256]{1,0:T(8,128)(2,1)S(1)}, bf16[64,256]{1,0:T(8,128)(2,1)S(1)}, u32[]{:S(2)}, u32[]{:S(2)}) collective-permute-start(bf16[64,256]{1,0:T(8,128)(2,1)S(1)} %add_convert_fusion), channel_id=1, source_target_pairs={{0,8},{4,12},{8,0},{12,4},{16,24},{20,28},{24,16},{28,20},{1,9},{5... | collective-permute-start | bytes 98312 | tf_op jit(solution)/shard_map/ppermute | solution.py:18
  97.1 3.9 %collective-permute-start.31 = (bf16[64,256]{1,0:T(8,128)(2,1)S(1)}, bf16[64,256]{1,0:T(8,128)(2,1)S(1)}, u32[]{:S(2)}, u32[]{:S(2)}) collective-permute-start(bf16[64,256]{1,0:T(8,128)(2,1)S(1)} %add_convert_fusion), channel_id=1, source_target_pairs={{0,16},{4,20},{8,24},{12,28},{16,0},{20,4},{24,8},{28,12},{1,17},{... | collective-permute-start | bytes 98312 | tf_op jit(solution)/shard_map/ppermute | solution.py:18
  98.5 4.8 %collective-permute-start.32 = (bf16[64,256]{1,0:T(8,128)(2,1)S(1)}, bf16[64,256]{1,0:T(8,128)(2,1)S(1)}, u32[]{:S(2)}, u32[]{:S(2)}) collective-permute-start(bf16[64,256]{1,0:T(8,128)(2,1)S(1)} %add_convert_fusion), channel_id=1, source_target_pairs={{0,24},{4,28},{8,16},{12,20},{16,8},{20,12},{24,0},{28,4},{1,25},{... | collective-permute-start | bytes 98312 | tf_op jit(solution)/shard_map/ppermute | solution.py:18
  (4 other events, 118.1 us)

commit v3 on v2

--- a/solution.py
+++ b/solution.py
@@ -9,7 +9,6 @@
 from jax.sharding import PartitionSpec as P
 
 CHUNK = 8
-EARLY = 10**10
 WIDE = 16
 
 
@@ -57,7 +56,7 @@
         out_specs=vmem,
         compiler_params=pltpu.CompilerParams(vmem_limit_bytes=1024 * 1024),
         cost_estimate=pl.CostEstimate(
-            flops=flops, bytes_accessed=4 * math.prod(shape), transcendentals=0
+            flops=flops, bytes_accessed=1024, transcendentals=0
         ),
     )(*in_vmem(*values), *earlier)
 
@@ -285,41 +284,48 @@
         perm = [(i, i ^ (odd_bit if i % 2 else even_bit)) for i in range(8)]
         return lax.ppermute(value, "blk", perm)
 
-    own, sibling, near, distant, distant_too = {0: features}, {}, {}, {}, {}
-    own[2] = after(hop(own[0], "feat", 2), flops=4 * EARLY)
-    own[1] = hop(own[0], "feat", 1)
-    beside = [hop(own[0], "blk", 2), hop(own[0], "blk", 4)]
-    sibling[0] = swap(own[0])
-    distant[0] = cross(pick(beside[1], beside[0]), 2, 4)
+    def along_feat(value, even_bit, odd_bit):
+        perm = [(i, i ^ (odd_bit if i // 4 % 2 else even_bit)) for i in range(32)]
+        return lax.ppermute(value, ("blk", "feat"), perm)
+
+    own, sibling, near, near_too, distant, distant_too = {0: features}, {}, {}, {}, {}, {}
+    own[2] = hop(features, "feat", 2)
+    own[1] = hop(features, "feat", 1)
+    beside = [hop(features, "blk", 2), hop(features, "blk", 4)]
+    sibling[0] = swap(features)
+    distant[0] = after(cross(pick(beside[1], beside[0]), 2, 4), flops=10**9)
+    distant_too[0] = swap(distant[0])
     sibling[1] = swap(own[1])
-    near[1] = cross(pair_of(own[1], sibling[1], own[2], distant[0]), 2, 4)
-    own[3] = hop(own[2], "feat", 1)
+    near[1] = after(cross(pair_of(own[1], sibling[1]), 2, 4), flops=10**9)
+    own[3] = after(hop(own[2], "feat", 1), flops=3*10**9)
     sibling[2] = swap(own[2])
-    distant[3] = hop(distant[0], "feat", 3)
-    distant_too[3] = swap(distant[3])
-    near[2] = cross(pair_of(own[2], sibling[2], near[1]), 2, 4)
-    distant[1] = hop(distant[0], "feat", 1)
-    distant_too[1] = swap(distant[1])
+    near[2] = cross(pair_of(own[2], sibling[2]), 2, 4)
+    odd_far = after(along_feat(pair_of(distant[0], distant_too[0]), 3, 1), flops=2000000000)
     sibling[3] = swap(own[3])
-    near[3] = cross(pair_of(own[3], sibling[3], near[2], distant_too[3]), 2, 4)
-    distant[2] = after(cross(pick_part(near[2]), 4, 2), flops=EARLY)
-
+    near[3] = cross(pair_of(own[3], sibling[3], near[1]), 2, 4)
     units = [own[k] for k in range(4)] + [sibling[k] for k in range(4)]
     sources = ((0, plain(0, 4)), (1, plain(4, 4)))
     acc = aggregate(sources, lists, units, None, False)[0]
 
+    distant[2] = after(cross(pick_part(near[2], acc), 4, 2), flops=8000000000)
+
     beside_too = [swap(pick(beside[0], beside[0], acc)), swap(beside[1])]
+    odd_far_too = swap(odd_far)
     near_too = {k: swap(near[k]) for k in range(1, 4)}
-    for k in (0, 2):
-        distant_too[k] = swap(distant[k])
-    units = [distant[k] for k in range(4)] + [distant_too[k] for k in range(4)]
+    distant_too[2] = swap(distant[2])
+    units = [distant[0], distant[2], distant_too[0], distant_too[2], odd_far, odd_far_too]
     units += [near[k] for k in range(1, 4)] + [near_too[k] for k in range(1, 4)] + beside + beside_too
-    sources = [(6, plain(0, 4)), (7, plain(4, 4))]
+    sources = []
+    for side in range(2):
+        alone = [((2 * side + j, None),) * 2 for j in range(2)]
+        third = ((4, side), (5, 1 - side))
+        first = ((5, side), (4, 1 - side))
+        sources.append((6 + side, (alone[0], first, alone[1], third)))
     for along, bit in enumerate((2, 4)):
         for side in range(2):
-            slices = [((14 + 2 * side + along, None),) * 2]
+            slices = [((12 + 2 * side + along, None),) * 2]
             for k in range(1, 4):
-                table = (8, 11) if along == 0 else (11, 8)
+                table = (6, 9) if along == 0 else (9, 6)
                 slices.append(((table[0] + k - 1, side), (table[1] + k - 1, 1 - side)))
             sources.append((bit + side, tuple(slices)))
     return aggregate(tuple(sources), lists, units, acc, True)

time: 103 us -> 99 us (0.961); the launches traced: 104 us -> 97.5 us
  waiting for transfers between devices: 54.8 us -> 42 us
  starting transfers between devices: 26.2 us -> 33.6 us
  blocking collectives: 9.99 us -> 8.46 us
    ppermute x28 -> x25, waiting for transfers between devices: 44.8 us -> 35.4 us  [hop(): return lax.ppermute(value, axis, [(i, i ^ bit) for i in range(size)])]
    ppermute x5, waiting for transfers between devices: 9.99 us -> 1.54 us  [cross(): return lax.ppermute(value, 'blk', perm)]
    ppermute x0 -> x1, waiting for transfers between devices: none -> 5.02 us  [along_feat(): return lax.ppermute(value, ('blk', 'feat'), perm)]
    ppermute x0 -> x1, starting transfers between devices: none -> 2.63 us  [along_feat(): return lax.ppermute(value, ('blk', 'feat'), perm)]
    ppermute x28 -> x25, starting transfers between devices: 22.3 us -> 24.7 us  [hop(): return lax.ppermute(value, axis, [(i, i ^ bit) for i in range(size)])]
    ppermute x5, starting transfers between devices: 3.93 us -> 6.32 us  [cross(): return lax.ppermute(value, 'blk', perm)]
    all_to_all x1, blocking collectives: 9.99 us -> 8.46 us  [shards(): lax.all_to_all(local_grad.astype(jnp.bfloat16).reshape(groups, feat_width...]
  transfers between devices with their start and end apart: 33 -> 31, of which waited for: 20 -> 14; matrix products, arithmetic and copies ran while one was open for 1% -> 1% of each run, Pallas kernels for 5% -> 5%
where the time goes in v3:
time: 99 us; the launch traced here: 97.5 us
  waiting for transfers between devices  42 us (42%)
  starting transfers between devices  33.6 us (34%)
  Pallas kernels  9.88 us (10%)
  blocking collectives  8.46 us (9%)
  local copies, waits for them, and re-layouts  1 us (1%)
    ppermute x25, waiting for transfers between devices, hop(): return lax.ppermute(value, axis, [(i, i ^ bit) for i in range(size)])  35.4 us
    ppermute x25, starting transfers between devices, hop(): return lax.ppermute(value, axis, [(i, i ^ bit) for i in range(size)])  24.7 us
    pallas_call x2, Pallas kernels, aggregate(): pl.pallas_call(functools.partial(aggregate_kernel, sources, len(units), l...  9.48 us
    all_to_all x1, blocking collectives, shards(): lax.all_to_all(local_grad.astype(jnp.bfloat16).reshape(groups, feat_width...  8.46 us
    ppermute x5, starting transfers between devices, cross(): return lax.ppermute(value, 'blk', perm)  6.32 us
    ppermute x1, waiting for transfers between devices, along_feat(): return lax.ppermute(value, ('blk', 'feat'), perm)  5.02 us
    ppermute x1, starting transfers between devices, along_feat(): return lax.ppermute(value, ('blk', 'feat'), perm)  2.63 us
  transfers between devices with their start and end apart: 31, of which 14 were waited for; matrix products, arithmetic and copies ran while one was open for 1% of the time, Pallas kernels for 5%

profile of v3, /device:TPU:0, one launch (start us, length us, event | category | flops | bytes accessed | tf_op | source)
XLA Modules:
  0.0 97.5 jit_solution(9581191116760611808)
XLA Ops:
  0.7 3.1 %collective-permute-start.6 = (bf16[64,2048]{1,0:T(8,128)(2,1)}, bf16[64,2048]{1,0:T(8,128)(2,1)S(1)}, u32[]{:S(2)}, u32[]{:S(2)}) collective-permute-start(bf16[64,2048]{1,0:T(8,128)(2,1)} %refs_4_.1), channel_id=1, source_target_pairs={{0,1},{1,0},{2,3},{3,2},{4,5},{5,4},{6,7},{7,6},{8,9},{9,8},{10,11... | collective-permute-start | bytes 786440 | tf_op jit(solution)/shard_map/ppermute | solution.py:17
  3.7 1.5 %collective-permute-start.1 = (bf16[64,2048]{1,0:T(8,128)(2,1)}, bf16[64,2048]{1,0:T(8,128)(2,1)S(1)}, u32[]{:S(2)}, u32[]{:S(2)}) collective-permute-start(bf16[64,2048]{1,0:T(8,128)(2,1)} %refs_4_.1), channel_id=1, source_target_pairs={{0,8},{4,12},{8,0},{12,4},{16,24},{20,28},{24,16},{28,20},{1,9},{5... | collective-permute-start | bytes 786440 | tf_op jit(solution)/shard_map/ppermute | solution.py:17
  5.2 1.5 %collective-permute-start = (bf16[64,2048]{1,0:T(8,128)(2,1)}, bf16[64,2048]{1,0:T(8,128)(2,1)S(1)}, u32[]{:S(2)}, u32[]{:S(2)}) collective-permute-start(bf16[64,2048]{1,0:T(8,128)(2,1)} %refs_4_.1), channel_id=1, source_target_pairs={{0,16},{4,20},{8,24},{12,28},{16,0},{20,4},{24,8},{28,12},{1,17},{... | collective-permute-start | bytes 786440 | tf_op jit(solution)/shard_map/ppermute | solution.py:17
  6.8 2.6 %collective-permute-start.3 = (bf16[64,2048]{1,0:T(8,128)(2,1)}, bf16[64,2048]{1,0:T(8,128)(2,1)S(1)}, u32[]{:S(2)}, u32[]{:S(2)}) collective-permute-start(bf16[64,2048]{1,0:T(8,128)(2,1)} %refs_4_.1), channel_id=1, source_target_pairs={{0,2},{1,3},{2,0},{3,1},{4,6},{5,7},{6,4},{7,5},{8,10},{9,11},{10,... | collective-permute-start | bytes 786440 | tf_op jit(solution)/shard_map/ppermute | solution.py:17
  9.3 3.4 %collective-permute-done.6.refs_5_.own_ref = bf16[64,2048]{1,0:T(8,128)(2,1)S(1)} collective-permute-done((bf16[64,2048]{1,0:T(8,128)(2,1)}, bf16[64,2048]{1,0:T(8,128)(2,1)S(1)}, u32[]{:S(2)}, u32[]{:S(2)}) %collective-permute-start.6) | collective-permute-done | bytes 262176 | tf_op jit(solution)/shard_map/ppermute | solution.py:17
  13.0 3.1 %collective-permute-start.2 = (bf16[64,2048]{1,0:T(8,128)(2,1)S(1)}, bf16[64,2048]{1,0:T(8,128)(2,1)S(1)}, u32[]{:S(2)}, u32[]{:S(2)}) collective-permute-start(bf16[64,2048]{1,0:T(8,128)(2,1)S(1)} %shard_map.86), channel_id=1, source_target_pairs={{0,8},{4,20},{8,0},{12,28},{16,24},{20,4},{24,16},{28,12},{1,9},{5... | collective-permute-start | bytes 786440 | tf_op jit(solution)/shard_map/ppermute | solution.py:285
  16.0 4.7 %collective-permute-done.3.own_ref.refs_6_ = bf16[64,2048]{1,0:T(8,128)(2,1)S(1)} collective-permute-done((bf16[64,2048]{1,0:T(8,128)(2,1)}, bf16[64,2048]{1,0:T(8,128)(2,1)S(1)}, u32[]{:S(2)}, u32[]{:S(2)}) %collective-permute-start.3) | collective-permute-done | bytes 262176 | tf_op jit(solution)/shard_map/ppermute | solution.py:17
  20.8 0.6 collective-permute-start.16
  21.8 5.4 %collective-permute-done.7.value_ref = bf16[64,2048]{1,0:T(8,128)(2,1)S(1)} collective-permute-done((bf16[64,2048]{1,0:T(8,128)(2,1)S(1)}, bf16[64,2048]{1,0:T(8,128)(2,1)S(1)}, u32[]{:S(2)}, u32[]{:S(2)}) %collective-permute-start.7) | collective-permute-done | bytes 262176 | tf_op jit(solution)/shard_map/ppermute | solution.py:17
  28.4 2.6 %collective-permute-start.14 = (bf16[2,64,2048]{2,1,0:T(8,128)(2,1)S(1)}, bf16[2,64,2048]{2,1,0:T(8,128)(2,1)S(1)}, u32[]{:S(2)}, u32[]{:S(2)}) collective-permute-start(bf16[2,64,2048]{2,1,0:T(8,128)(2,1)S(1)} %shard_map.93), channel_id=1, source_target_pairs={{0,3},{1,2},{2,1},{3,0},{4,5},{5,4},{6,7},{7,6},{8,11},{9,10},{10,... | collective-permute-start | bytes 1572872 | tf_op jit(solution)/shard_map/ppermute | solution.py:289
  31.2 1.9 %collective-permute-start.17 = (bf16[2,64,2048]{2,1,0:T(8,128)(2,1)S(1)}, bf16[2,64,2048]{2,1,0:T(8,128)(2,1)S(1)}, u32[]{:S(2)}, u32[]{:S(2)}) collective-permute-start(bf16[2,64,2048]{2,1,0:T(8,128)(2,1)S(1)} %shard_map.97), channel_id=1, source_target_pairs={{0,8},{4,20},{8,0},{12,28},{16,24},{20,4},{24,16},{28,12},{1,9},{5... | collective-permute-start | bytes 1572872 | tf_op jit(solution)/shard_map/ppermute | solution.py:285
  33.0 4.5 %shard_map.90.refs_0_.refs_20_ = f32[2048,256]{1,0:T(8,128)S(1)} custom-call(s32[1,1,8,48]{3,2,1,0:T(8,128)} %refs_0_.3, s32[1,1,8,48]{3,2,1,0:T(8,128)} %refs_1_.3, s32[1,1,8]{2,1,0:T(1,128)} %refs_2_.3, bf16[1,1,8,48,128,128]{5,4,3,2,1,0:T(8,128)(2,1)} %refs_3_.3, bf16[64,2048]{1,0:T(8,128)(2,1)S(1)} %copy-done.1, ...), custom_call_target="tpu_custom_call" | custom-call | flops 3221225472 | bytes 5242880 | tf_op jit(solution)/shard_map/pallas_call | solution.py:210
  38.0 5.0 %collective-permute-done.14.value_ref = bf16[2,64,2048]{2,1,0:T(8,128)(2,1)S(1)} collective-permute-done((bf16[2,64,2048]{2,1,0:T(8,128)(2,1)S(1)}, bf16[2,64,2048]{2,1,0:T(8,128)(2,1)S(1)}, u32[]{:S(2)}, u32[]{:S(2)}) %collective-permute-start.14) | collective-permute-done | bytes 524320 | tf_op jit(solution)/shard_map/ppermute | solution.py:289
  43.7 1.0 collective-permute-done.11.value_ref
  44.9 0.6 collective-permute-done.17.refs_12_
  46.1 1.7 %collective-permute-done.13.refs_7_ = bf16[64,2048]{1,0:T(8,128)(2,1)S(1)} collective-permute-done((bf16[64,2048]{1,0:T(8,128)(2,1)S(1)}, bf16[64,2048]{1,0:T(8,128)(2,1)S(1)}, u32[]{:S(2)}, u32[]{:S(2)}) %collective-permute-start.13) | collective-permute-done | bytes 262176 | tf_op jit(solution)/shard_map/ppermute | solution.py:17
  47.8 5.0 %shard_map.99 = (bf16[2,256,256]{2,1,0:T(8,128)(2,1)S(1)}, f32[2,256,256]{2,1,0:T(8,128)S(1)}, bf16[2,256,256]{2,1,0:T(8,128)(2,1)S(1)}, f32[2,256,256]{2,1,0:T(8,128)S(1)}) custom-call(s32[1,1,8,48]{3,2,1,0:T(8,128)} %refs_0_.3, s32[1,1,8,48]{3,2,1,0:T(8,128)} %refs_1_.3, s32[1,1,8]{2,1,0:T(1,128)} %refs_2_.3, bf16[1,1,8,48,128,128]{5,4,3,2,1,0:T(8,128)(2,1)} %refs_3_.3, ...), custom_call_target="tpu_custom_call" | custom-call | flops 9663676416 | bytes 15728640 | tf_op jit(solution)/shard_map/pallas_call | solution.py:210
  52.8 1.3 %collective-permute-start.23 = (bf16[2,256,256]{2,1,0:T(8,128)(2,1)S(1)}, bf16[2,256,256]{2,1,0:T(8,128)(2,1)S(1)}, u32[]{:S(2)}, u32[]{:S(2)}) collective-permute-start(bf16[2,256,256]{2,1,0:T(8,128)(2,1)S(1)} %get-tuple-element.7), channel_id=1, source_target_pairs={{0,1},{1,0},{2,3},{3,2},{4,5},{5,4},{6,7},{7,6},{8,9},{9,8},{10,11... | collective-permute-start | bytes 786440 | tf_op jit(solution)/shard_map/ppermute | solution.py:17
  54.1 2.2 %collective-permute-start.25 = (bf16[2,256,256]{2,1,0:T(8,128)(2,1)S(1)}, bf16[2,256,256]{2,1,0:T(8,128)(2,1)S(1)}, u32[]{:S(2)}, u32[]{:S(2)}) collective-permute-start(bf16[2,256,256]{2,1,0:T(8,128)(2,1)S(1)} %get-tuple-element.9), channel_id=1, source_target_pairs={{0,2},{1,3},{2,0},{3,1},{4,6},{5,7},{6,4},{7,5},{8,10},{9,11},{10,... | collective-permute-start | bytes 786440 | tf_op jit(solution)/shard_map/ppermute | solution.py:17
  56.4 6.1 %collective-permute-done.23 = bf16[2,256,256]{2,1,0:T(8,128)(2,1)S(1)} collective-permute-done((bf16[2,256,256]{2,1,0:T(8,128)(2,1)S(1)}, bf16[2,256,256]{2,1,0:T(8,128)(2,1)S(1)}, u32[]{:S(2)}, u32[]{:S(2)}) %collective-permute-start.23) | collective-permute-done | bytes 262176 | tf_op jit(solution)/shard_map/ppermute | solution.py:17
  62.7 0.8 collective-permute-done.25
  63.5 3.0 %collective-permute-start.26 = (bf16[256,256]{1,0:T(8,128)(2,1)S(1)}, bf16[256,256]{1,0:T(8,128)(2,1)S(1)}, u32[]{:S(2)}, u32[]{:S(2)}) collective-permute-start(bf16[256,256]{1,0:T(8,128)(2,1)S(1)} %fusion.9), channel_id=1, source_target_pairs={{0,1},{1,0},{2,3},{3,2},{4,5},{5,4},{6,7},{7,6},{8,9},{9,8},{10,11... | collective-permute-start | bytes 393224 | tf_op jit(solution)/shard_map/ppermute | solution.py:17
  66.5 8.4 %collective-permute-done.24 = bf16[256,256]{1,0:T(8,128)(2,1)S(1)} collective-permute-done((bf16[256,256]{1,0:T(8,128)(2,1)S(1)}, bf16[256,256]{1,0:T(8,128)(2,1)S(1)}, u32[]{:S(2)}, u32[]{:S(2)}) %collective-permute-start.24) | collective-permute-done | bytes 131104 | tf_op jit(solution)/shard_map/ppermute | solution.py:17
  75.8 8.5 %all_to_all.5 = bf16[4,64,256]{2,1,0:T(8,128)(2,1)S(1)} all-to-all(bf16[4,64,256]{2,1,0:T(8,128)(2,1)S(1)} %bitcast.20), channel_id=1, replica_groups=mesh['blk'=8,'feat'=4] {'feat'}, dimensions={0} | all-to-all | bytes 262144 | tf_op jit(solution)/shard_map/all_to_all | solution.py:365
  84.3 2.9 %collective-permute-start.27 = (bf16[64,256]{1,0:T(8,128)(2,1)S(1)}, bf16[64,256]{1,0:T(8,128)(2,1)S(1)}, u32[]{:S(2)}, u32[]{:S(2)}) collective-permute-start(bf16[64,256]{1,0:T(8,128)(2,1)S(1)} %reduce_sum.12), channel_id=1, source_target_pairs={{0,4},{4,0},{8,12},{12,8},{16,20},{20,16},{24,28},{28,24},{1,5},{5... | collective-permute-start | bytes 98312 | tf_op jit(solution)/shard_map/ppermute | solution.py:17
  87.2 0.9 collective-permute-done.27
  88.0 1.9 %collective-permute-start.28 = (bf16[64,256]{1,0:T(8,128)(2,1)S(1)}, bf16[64,256]{1,0:T(8,128)(2,1)S(1)}, u32[]{:S(2)}, u32[]{:S(2)}) collective-permute-start(bf16[64,256]{1,0:T(8,128)(2,1)S(1)} %add_convert_fusion), channel_id=1, source_target_pairs={{0,8},{4,12},{8,0},{12,4},{16,24},{20,28},{24,16},{28,20},{1,9},{5... | collective-permute-start | bytes 98312 | tf_op jit(solution)/shard_map/ppermute | solution.py:17
  89.9 2.2 %collective-permute-start.29 = (bf16[64,256]{1,0:T(8,128)(2,1)S(1)}, bf16[64,256]{1,0:T(8,128)(2,1)S(1)}, u32[]{:S(2)}, u32[]{:S(2)}) collective-permute-start(bf16[64,256]{1,0:T(8,128)(2,1)S(1)} %add_convert_fusion), channel_id=1, source_target_pairs={{0,16},{4,20},{8,24},{12,28},{16,0},{20,4},{24,8},{28,12},{1,17},{... | collective-permute-start | bytes 98312 | tf_op jit(solution)/shard_map/ppermute | solution.py:17
  92.1 0.8 copy.10
  92.9 1.0 %collective-permute-done.29 = bf16[64,256]{1,0:T(8,128)(2,1)S(1)} collective-permute-done((bf16[64,256]{1,0:T(8,128)(2,1)S(1)}, bf16[64,256]{1,0:T(8,128)(2,1)S(1)}, u32[]{:S(2)}, u32[]{:S(2)}) %collective-permute-start.29) | collective-permute-done | bytes 32800 | tf_op jit(solution)/shard_map/ppermute | solution.py:17
  94.0 2.9 %collective-permute-done.30 = bf16[64,256]{1,0:T(8,128)(2,1)S(1)} collective-permute-done((bf16[64,256]{1,0:T(8,128)(2,1)S(1)}, bf16[64,256]{1,0:T(8,128)(2,1)S(1)}, u32[]{:S(2)}, u32[]{:S(2)}) %collective-permute-start.30) | collective-permute-done | bytes 32800 | tf_op jit(solution)/shard_map/ppermute | solution.py:17
  96.9 0.7 add_multiply_fusion
  (64 shorter events, 5.2 us)
Async XLA Ops:
  0.6 74.4 %copy-start = (bf16[256,256]{1,0:T(8,128)(2,1)S(1)}, bf16[256,256]{1,0:T(8,128)(2,1)}, u32[]{:S(2)}) copy-start(bf16[256,256]{1,0:T(8,128)(2,1)} %param.12) | copy-start | bytes 393220
  0.7 12.1 %collective-permute-start.6 = (bf16[64,2048]{1,0:T(8,128)(2,1)}, bf16[64,2048]{1,0:T(8,128)(2,1)S(1)}, u32[]{:S(2)}, u32[]{:S(2)}) collective-permute-start(bf16[64,2048]{1,0:T(8,128)(2,1)} %refs_4_.1), channel_id=1, source_target_pairs={{0,1},{1,0},{2,3},{3,2},{4,5},{5,4},{6,7},{7,6},{8,9},{9,8},{10,11... | collective-permute-start | bytes 786440 | tf_op jit(solution)/shard_map/ppermute | solution.py:17
  3.7 9.0 %collective-permute-start.1 = (bf16[64,2048]{1,0:T(8,128)(2,1)}, bf16[64,2048]{1,0:T(8,128)(2,1)S(1)}, u32[]{:S(2)}, u32[]{:S(2)}) collective-permute-start(bf16[64,2048]{1,0:T(8,128)(2,1)} %refs_4_.1), channel_id=1, source_target_pairs={{0,8},{4,12},{8,0},{12,4},{16,24},{20,28},{24,16},{28,20},{1,9},{5... | collective-permute-start | bytes 786440 | tf_op jit(solution)/shard_map/ppermute | solution.py:17
  5.2 7.7 %collective-permute-start = (bf16[64,2048]{1,0:T(8,128)(2,1)}, bf16[64,2048]{1,0:T(8,128)(2,1)S(1)}, u32[]{:S(2)}, u32[]{:S(2)}) collective-permute-start(bf16[64,2048]{1,0:T(8,128)(2,1)} %refs_4_.1), channel_id=1, source_target_pairs={{0,16},{4,20},{8,24},{12,28},{16,0},{20,4},{24,8},{28,12},{1,17},{... | collective-permute-start | bytes 786440 | tf_op jit(solution)/shard_map/ppermute | solution.py:17
  6.8 14.0 %collective-permute-start.3 = (bf16[64,2048]{1,0:T(8,128)(2,1)}, bf16[64,2048]{1,0:T(8,128)(2,1)S(1)}, u32[]{:S(2)}, u32[]{:S(2)}) collective-permute-start(bf16[64,2048]{1,0:T(8,128)(2,1)} %refs_4_.1), channel_id=1, source_target_pairs={{0,2},{1,3},{2,0},{3,1},{4,6},{5,7},{6,4},{7,5},{8,10},{9,11},{10,... | collective-permute-start | bytes 786440 | tf_op jit(solution)/shard_map/ppermute | solution.py:17
  12.8 8.0 %collective-permute-start.9 = (bf16[64,2048]{1,0:T(8,128)(2,1)S(1)}, bf16[64,2048]{1,0:T(8,128)(2,1)S(1)}, u32[]{:S(2)}, u32[]{:S(2)}) collective-permute-start(bf16[64,2048]{1,0:T(8,128)(2,1)S(1)} %collective-permute-done.6.refs_5_.own_ref), channel_id=1, source_target_pairs={{0,4},{4,0},{8,12},{12,8},{16,20},{20,16},{24,28},{28,24},{1,5},{5... | collective-permute-start | bytes 786440 | tf_op jit(solution)/shard_map/ppermute | solution.py:17
  13.0 8.5 %collective-permute-start.2 = (bf16[64,2048]{1,0:T(8,128)(2,1)S(1)}, bf16[64,2048]{1,0:T(8,128)(2,1)S(1)}, u32[]{:S(2)}, u32[]{:S(2)}) collective-permute-start(bf16[64,2048]{1,0:T(8,128)(2,1)S(1)} %shard_map.86), channel_id=1, source_target_pairs={{0,8},{4,20},{8,0},{12,28},{16,24},{20,4},{24,16},{28,12},{1,9},{5... | collective-permute-start | bytes 786440 | tf_op jit(solution)/shard_map/ppermute | solution.py:285
  20.8 6.4 %collective-permute-start.7 = (bf16[64,2048]{1,0:T(8,128)(2,1)S(1)}, bf16[64,2048]{1,0:T(8,128)(2,1)S(1)}, u32[]{:S(2)}, u32[]{:S(2)}) collective-permute-start(bf16[64,2048]{1,0:T(8,128)(2,1)S(1)} %collective-permute-done.3.own_ref.refs_6_), channel_id=1, source_target_pairs={{0,1},{1,0},{2,3},{3,2},{4,5},{5,4},{6,7},{7,6},{8,9},{9,8},{10,11... | collective-permute-start | bytes 786440 | tf_op jit(solution)/shard_map/ppermute | solution.py:17
  20.8 7.0 %collective-permute-start.4 = (bf16[64,2048]{1,0:T(8,128)(2,1)S(1)}, bf16[64,2048]{1,0:T(8,128)(2,1)S(1)}, u32[]{:S(2)}, u32[]{:S(2)}) collective-permute-start(bf16[64,2048]{1,0:T(8,128)(2,1)S(1)} %collective-permute-done.3.own_ref.refs_6_), channel_id=1, source_target_pairs={{0,4},{4,0},{8,12},{12,8},{16,20},{20,16},{24,28},{28,24},{1,5},{5... | collective-permute-start | bytes 786440 | tf_op jit(solution)/shard_map/ppermute | solution.py:17
  20.8 10.2 %collective-permute-start.16 = (bf16[2,64,2048]{2,1,0:T(8,128)(2,1)S(1)}, bf16[2,64,2048]{2,1,0:T(8,128)(2,1)S(1)}, u32[]{:S(2)}, u32[]{:S(2)}) collective-permute-start(bf16[2,64,2048]{2,1,0:T(8,128)(2,1)S(1)} %shard_map.95), channel_id=1, source_target_pairs={{0,8},{4,20},{8,0},{12,28},{16,24},{20,4},{24,16},{28,12},{1,9},{5... | collective-permute-start | bytes 1572872 | tf_op jit(solution)/shard_map/ppermute | solution.py:285
  21.5 6.9 %collective-permute-start.12 = (bf16[64,2048]{1,0:T(8,128)(2,1)S(1)}, bf16[64,2048]{1,0:T(8,128)(2,1)S(1)}, u32[]{:S(2)}, u32[]{:S(2)}) collective-permute-start(bf16[64,2048]{1,0:T(8,128)(2,1)S(1)} %shard_map.87.own_ref.refs_4_), channel_id=1, source_target_pairs={{0,4},{4,0},{8,12},{12,8},{16,20},{20,16},{24,28},{28,24},{1,5},{5... | collective-permute-start | bytes 786440 | tf_op jit(solution)/shard_map/ppermute | solution.py:17
  27.2 3.9 %collective-permute-start.10 = (bf16[64,2048]{1,0:T(8,128)(2,1)S(1)}, bf16[64,2048]{1,0:T(8,128)(2,1)S(1)}, u32[]{:S(2)}, u32[]{:S(2)}) collective-permute-start(bf16[64,2048]{1,0:T(8,128)(2,1)S(1)} %shard_map.89.refs_7_.own_ref), channel_id=1, source_target_pairs={{0,4},{4,0},{8,12},{12,8},{16,20},{20,16},{24,28},{28,24},{1,5},{5... | collective-permute-start | bytes 786440 | tf_op jit(solution)/shard_map/ppermute | solution.py:17
  27.3 5.8 %collective-permute-start.8 = (bf16[64,2048]{1,0:T(8,128)(2,1)S(1)}, bf16[64,2048]{1,0:T(8,128)(2,1)S(1)}, u32[]{:S(2)}, u32[]{:S(2)}) collective-permute-start(bf16[64,2048]{1,0:T(8,128)(2,1)S(1)} %copy-done.1), channel_id=1, source_target_pairs={{0,4},{4,0},{8,12},{12,8},{16,20},{20,16},{24,28},{28,24},{1,5},{5... | collective-permute-start | bytes 786440 | tf_op jit(solution)/shard_map/ppermute | solution.py:17
  27.8 9.7 %collective-permute-start.5 = (bf16[2,64,2048]{2,1,0:T(8,128)(2,1)S(1)}, bf16[2,64,2048]{2,1,0:T(8,128)(2,1)S(1)}, u32[]{:S(2)}, u32[]{:S(2)}) collective-permute-start(bf16[2,64,2048]{2,1,0:T(8,128)(2,1)S(1)} %shard_map.88), channel_id=1, source_target_pairs={{0,8},{4,20},{8,0},{12,28},{16,24},{20,4},{24,16},{28,12},{1,9},{5... | collective-permute-start | bytes 1572872 | tf_op jit(solution)/shard_map/ppermute | solution.py:285
  28.4 14.6 %collective-permute-start.14 = (bf16[2,64,2048]{2,1,0:T(8,128)(2,1)S(1)}, bf16[2,64,2048]{2,1,0:T(8,128)(2,1)S(1)}, u32[]{:S(2)}, u32[]{:S(2)}) collective-permute-start(bf16[2,64,2048]{2,1,0:T(8,128)(2,1)S(1)} %shard_map.93), channel_id=1, source_target_pairs={{0,3},{1,2},{2,1},{3,0},{4,5},{5,4},{6,7},{7,6},{8,11},{9,10},{10,... | collective-permute-start | bytes 1572872 | tf_op jit(solution)/shard_map/ppermute | solution.py:289
  31.1 12.0 %collective-permute-start.22 = (bf16[64,2048]{1,0:T(8,128)(2,1)S(1)}, bf16[64,2048]{1,0:T(8,128)(2,1)S(1)}, u32[]{:S(2)}, u32[]{:S(2)}) collective-permute-start(bf16[64,2048]{1,0:T(8,128)(2,1)S(1)} %collective-permute-done.even_ref.refs_17_), channel_id=1, source_target_pairs={{0,4},{4,0},{8,12},{12,8},{16,20},{20,16},{24,28},{28,24},{1,5},{5... | collective-permute-start | bytes 786440 | tf_op jit(solution)/shard_map/ppermute | solution.py:17
  31.2 14.3 %collective-permute-start.17 = (bf16[2,64,2048]{2,1,0:T(8,128)(2,1)S(1)}, bf16[2,64,2048]{2,1,0:T(8,128)(2,1)S(1)}, u32[]{:S(2)}, u32[]{:S(2)}) collective-permute-start(bf16[2,64,2048]{2,1,0:T(8,128)(2,1)S(1)} %shard_map.97), channel_id=1, source_target_pairs={{0,8},{4,20},{8,0},{12,28},{16,24},{20,4},{24,16},{28,12},{1,9},{5... | collective-permute-start | bytes 1572872 | tf_op jit(solution)/shard_map/ppermute | solution.py:285
  37.6 7.0 %collective-permute-start.11 = (bf16[64,2048]{1,0:T(8,128)(2,1)S(1)}, bf16[64,2048]{1,0:T(8,128)(2,1)S(1)}, u32[]{:S(2)}, u32[]{:S(2)}) collective-permute-start(bf16[64,2048]{1,0:T(8,128)(2,1)S(1)} %shard_map.91), channel_id=1, source_target_pairs={{0,16},{4,12},{8,24},{12,4},{16,0},{20,28},{24,8},{28,20},{1,17},{... | collective-permute-start | bytes 786440 | tf_op jit(solution)/shard_map/ppermute | solution.py:285
  37.9 7.7 %collective-permute-start.21 = (bf16[64,2048]{1,0:T(8,128)(2,1)S(1)}, bf16[64,2048]{1,0:T(8,128)(2,1)S(1)}, u32[]{:S(2)}, u32[]{:S(2)}) collective-permute-start(bf16[64,2048]{1,0:T(8,128)(2,1)S(1)} %shard_map.98), channel_id=1, source_target_pairs={{0,4},{4,0},{8,12},{12,8},{16,20},{20,16},{24,28},{28,24},{1,5},{5... | collective-permute-start | bytes 786440 | tf_op jit(solution)/shard_map/ppermute | solution.py:17
  43.0 3.1 %collective-permute-start.18 = (bf16[2,64,2048]{2,1,0:T(8,128)(2,1)S(1)}, bf16[2,64,2048]{2,1,0:T(8,128)(2,1)S(1)}, u32[]{:S(2)}, u32[]{:S(2)}) collective-permute-start(bf16[2,64,2048]{2,1,0:T(8,128)(2,1)S(1)} %shard_map.96.refs_0_.refs_10_), channel_id=1, source_target_pairs={{0,4},{4,0},{8,12},{12,8},{16,20},{20,16},{24,28},{28,24},{1,5},{5... | collective-permute-start | bytes 1572872 | tf_op jit(solution)/shard_map/ppermute | solution.py:17
  43.1 3.0 %collective-permute-start.19 = (bf16[2,64,2048]{2,1,0:T(8,128)(2,1)S(1)}, bf16[2,64,2048]{2,1,0:T(8,128)(2,1)S(1)}, u32[]{:S(2)}, u32[]{:S(2)}) collective-permute-start(bf16[2,64,2048]{2,1,0:T(8,128)(2,1)S(1)} %collective-permute-done.5.pair_ref.refs_11_), channel_id=1, source_target_pairs={{0,4},{4,0},{8,12},{12,8},{16,20},{20,16},{24,28},{28,24},{1,5},{5... | collective-permute-start | bytes 1572872 | tf_op jit(solution)/shard_map/ppermute | solution.py:17
  44.6 3.2 %collective-permute-start.15 = (bf16[2,64,2048]{2,1,0:T(8,128)(2,1)S(1)}, bf16[2,64,2048]{2,1,0:T(8,128)(2,1)S(1)}, u32[]{:S(2)}, u32[]{:S(2)}) collective-permute-start(bf16[2,64,2048]{2,1,0:T(8,128)(2,1)S(1)} %shard_map.94.refs_8_), channel_id=1, source_target_pairs={{0,4},{4,0},{8,12},{12,8},{16,20},{20,16},{24,28},{28,24},{1,5},{5... | collective-permute-start | bytes 1572872 | tf_op jit(solution)/shard_map/ppermute | solution.py:17
  45.5 2.3 %collective-permute-start.20 = (bf16[2,64,2048]{2,1,0:T(8,128)(2,1)S(1)}, bf16[2,64,2048]{2,1,0:T(8,128)(2,1)S(1)}, u32[]{:S(2)}, u32[]{:S(2)}) collective-permute-start(bf16[2,64,2048]{2,1,0:T(8,128)(2,1)S(1)} %collective-permute-done.17.refs_12_), channel_id=1, source_target_pairs={{0,4},{4,0},{8,12},{12,8},{16,20},{20,16},{24,28},{28,24},{1,5},{5... | collective-permute-start | bytes 1572872 | tf_op jit(solution)/shard_map/ppermute | solution.py:17
  45.5 2.2 %collective-permute-start.13 = (bf16[64,2048]{1,0:T(8,128)(2,1)S(1)}, bf16[64,2048]{1,0:T(8,128)(2,1)S(1)}, u32[]{:S(2)}, u32[]{:S(2)}) collective-permute-start(bf16[64,2048]{1,0:T(8,128)(2,1)S(1)} %shard_map.92.refs_5_), channel_id=1, source_target_pairs={{0,4},{4,0},{8,12},{12,8},{16,20},{20,16},{24,28},{28,24},{1,5},{5... | collective-permute-start | bytes 786440 | tf_op jit(solution)/shard_map/ppermute | solution.py:17
  52.8 9.7 %collective-permute-start.23 = (bf16[2,256,256]{2,1,0:T(8,128)(2,1)S(1)}, bf16[2,256,256]{2,1,0:T(8,128)(2,1)S(1)}, u32[]{:S(2)}, u32[]{:S(2)}) collective-permute-start(bf16[2,256,256]{2,1,0:T(8,128)(2,1)S(1)} %get-tuple-element.7), channel_id=1, source_target_pairs={{0,1},{1,0},{2,3},{3,2},{4,5},{5,4},{6,7},{7,6},{8,9},{9,8},{10,11... | collective-permute-start | bytes 786440 | tf_op jit(solution)/shard_map/ppermute | solution.py:17
  54.1 9.3 %collective-permute-start.25 = (bf16[2,256,256]{2,1,0:T(8,128)(2,1)S(1)}, bf16[2,256,256]{2,1,0:T(8,128)(2,1)S(1)}, u32[]{:S(2)}, u32[]{:S(2)}) collective-permute-start(bf16[2,256,256]{2,1,0:T(8,128)(2,1)S(1)} %get-tuple-element.9), channel_id=1, source_target_pairs={{0,2},{1,3},{2,0},{3,1},{4,6},{5,7},{6,4},{7,5},{8,10},{9,11},{10,... | collective-permute-start | bytes 786440 | tf_op jit(solution)/shard_map/ppermute | solution.py:17
  62.6 12.3 %collective-permute-start.24 = (bf16[256,256]{1,0:T(8,128)(2,1)S(1)}, bf16[256,256]{1,0:T(8,128)(2,1)S(1)}, u32[]{:S(2)}, u32[]{:S(2)}) collective-permute-start(bf16[256,256]{1,0:T(8,128)(2,1)S(1)} %fusion.8), channel_id=1, source_target_pairs={{0,2},{1,3},{2,0},{3,1},{4,6},{5,7},{6,4},{7,5},{8,10},{9,11},{10,... | collective-permute-start | bytes 393224 | tf_op jit(solution)/shard_map/ppermute | solution.py:17
  63.5 11.4 %collective-permute-start.26 = (bf16[256,256]{1,0:T(8,128)(2,1)S(1)}, bf16[256,256]{1,0:T(8,128)(2,1)S(1)}, u32[]{:S(2)}, u32[]{:S(2)}) collective-permute-start(bf16[256,256]{1,0:T(8,128)(2,1)S(1)} %fusion.9), channel_id=1, source_target_pairs={{0,1},{1,0},{2,3},{3,2},{4,5},{5,4},{6,7},{7,6},{8,9},{9,8},{10,11... | collective-permute-start | bytes 393224 | tf_op jit(solution)/shard_map/ppermute | solution.py:17
  84.3 3.7 %collective-permute-start.27 = (bf16[64,256]{1,0:T(8,128)(2,1)S(1)}, bf16[64,256]{1,0:T(8,128)(2,1)S(1)}, u32[]{:S(2)}, u32[]{:S(2)}) collective-permute-start(bf16[64,256]{1,0:T(8,128)(2,1)S(1)} %reduce_sum.12), channel_id=1, source_target_pairs={{0,4},{4,0},{8,12},{12,8},{16,20},{20,16},{24,28},{28,24},{1,5},{5... | collective-permute-start | bytes 98312 | tf_op jit(solution)/shard_map/ppermute | solution.py:17
  88.0 4.9 %collective-permute-start.28 = (bf16[64,256]{1,0:T(8,128)(2,1)S(1)}, bf16[64,256]{1,0:T(8,128)(2,1)S(1)}, u32[]{:S(2)}, u32[]{:S(2)}) collective-permute-start(bf16[64,256]{1,0:T(8,128)(2,1)S(1)} %add_convert_fusion), channel_id=1, source_target_pairs={{0,8},{4,12},{8,0},{12,4},{16,24},{20,28},{24,16},{28,20},{1,9},{5... | collective-permute-start | bytes 98312 | tf_op jit(solution)/shard_map/ppermute | solution.py:17
  89.9 4.0 %collective-permute-start.29 = (bf16[64,256]{1,0:T(8,128)(2,1)S(1)}, bf16[64,256]{1,0:T(8,128)(2,1)S(1)}, u32[]{:S(2)}, u32[]{:S(2)}) collective-permute-start(bf16[64,256]{1,0:T(8,128)(2,1)S(1)} %add_convert_fusion), channel_id=1, source_target_pairs={{0,16},{4,20},{8,24},{12,28},{16,0},{20,4},{24,8},{28,12},{1,17},{... | collective-permute-start | bytes 98312 | tf_op jit(solution)/shard_map/ppermute | solution.py:17
  92.1 4.8 %collective-permute-start.30 = (bf16[64,256]{1,0:T(8,128)(2,1)S(1)}, bf16[64,256]{1,0:T(8,128)(2,1)S(1)}, u32[]{:S(2)}, u32[]{:S(2)}) collective-permute-start(bf16[64,256]{1,0:T(8,128)(2,1)S(1)} %add_convert_fusion), channel_id=1, source_target_pairs={{0,24},{4,28},{8,16},{12,20},{16,8},{20,12},{24,0},{28,4},{1,25},{... | collective-permute-start | bytes 98312 | tf_op jit(solution)/shard_map/ppermute | solution.py:17
  (2 other events, 37.4 us)

commit v4 on v3

--- a/solution.py
+++ b/solution.py
@@ -88,7 +88,9 @@
     acc_in = None if first else rest.pop(0)
     n_out = 4 if halves else 1
     out_refs = rest[:n_out]
-    rows_ref, cols_ref, counts_ref, feat, tiles, acc, unit_sems, tile_sems, list_sems, acc_sem = rest[n_out:]
+    rows_ref, cols_ref, counts_ref, feat, tiles, acc, base, unit_sems, tile_sems, list_sems, acc_sem = rest[
+        n_out:
+    ]
     blk = lax.axis_index("blk")
     z = lax.axis_index("feat")
     n_src = len(sources)
@@ -124,73 +126,95 @@
         pltpu.make_async_copy(source, target, list_sems.at[i])
         for i, (source, target) in enumerate(zip(list_hbm, (rows_ref, cols_ref, counts_ref)))
     ]
+    parts = [lax.bitwise_xor(blk, jnp.int32(off)) for off, _ in sources]
     for copy in list_copies:
         copy.start()
-    if not first:
-        acc_copy = pltpu.make_async_copy(acc_in, acc.at[pl.ds(0, nodes)], acc_sem)
-        acc_copy.start()
     for i in range(n_src):
         for k in range(groups):
             start_unit_copy(i, k)
+        tile_copy(i, 0).start()
+    acc_copy = None
+    if not first:
+        acc_copy = pltpu.make_async_copy(
+            acc_in, base if halves else acc.at[pl.ds(0, nodes)], acc_sem
+        )
+        if not halves:
+            acc_copy.start()
+    if first or halves:
+        acc[pl.ds(0, nodes), :] = jnp.zeros((nodes, acc.shape[1]), jnp.float32)
     for copy in list_copies:
         copy.wait()
-    parts = [lax.bitwise_xor(blk, jnp.int32(off)) for off, _ in sources]
     live = [counts_ref[0, 0, part] for part in parts]
     for i in range(n_src):
-        for chunk in range(chunks):
+        for chunk in range(1, chunks):
 
             @pl.when(chunk * CHUNK < live[i])
             def _():
                 tile_copy(i, chunk).start()
 
-    if first:
-        acc[pl.ds(0, nodes), :] = jnp.zeros((nodes, acc.shape[1]), jnp.float32)
-    else:
-        acc_copy.wait()
+    if acc_copy is not None:
+        if halves:
+            acc_copy.start()
+        else:
+            acc_copy.wait()
+
+    def add_tiles(i, base_slot, count):
+        for u in range(count):
+            slot = base_slot + u
+            row = jnp.where(slot < live[i], rows_ref[0, 0, parts[i], slot], row_tiles)
+            col = cols_ref[0, 0, parts[i], slot]
+            term = lax.dot_general(
+                tiles[i, slot],
+                feat[i, :, pl.ds(pl.multiple_of(col * size, size), size)],
+                (((1,), (1,)), ((), ())),
+                preferred_element_type=jnp.float32,
+            )
+            acc[pl.ds(pl.multiple_of(row * size, size), size), :] += term
+
     for i in range(n_src):
         for k in range(groups):
             unit_copy(i, k).wait()
-        for chunk in range(chunks):
-
-            @pl.when(chunk * CHUNK < live[i])
-            def _():
-                tile_copy(i, chunk).wait()
-
-        def add_tiles(base, count):
-            for u in range(count):
-                slot = base + u
-                row = jnp.where(slot < live[i], rows_ref[0, 0, parts[i], slot], row_tiles)
-                col = cols_ref[0, 0, parts[i], slot]
-                term = lax.dot_general(
-                    tiles[i, slot],
-                    feat[i, :, pl.ds(pl.multiple_of(col * size, size), size)],
-                    (((1,), (1,)), ((), ())),
-                    preferred_element_type=jnp.float32,
-                )
-                acc[pl.ds(pl.multiple_of(row * size, size), size), :] += term
+        tile_copy(i, 0).wait()
+        add_tiles(i, 0, CHUNK)
+    for i in range(n_src):
+        left = jnp.maximum(live[i] - CHUNK, 0)
+        wide = left // WIDE
+        narrow = (left - wide * WIDE + CHUNK - 1) // CHUNK
+
+        def do_wide(step, _):
+            for part in range(WIDE // CHUNK):
+                tile_copy(i, 1 + step * (WIDE // CHUNK) + part).wait()
+            add_tiles(i, CHUNK + step * WIDE, WIDE)
             return 0
 
-        wide = live[i] // WIDE
-        left = (live[i] - wide * WIDE + CHUNK - 1) // CHUNK
-        lax.fori_loop(0, wide, lambda p, _: add_tiles(p * WIDE, WIDE), 0)
-        lax.fori_loop(0, left, lambda p, _: add_tiles(wide * WIDE + p * CHUNK, CHUNK), 0)
+        def do_narrow(step, _):
+            chunk = 1 + wide * (WIDE // CHUNK) + step
+            tile_copy(i, chunk).wait()
+            add_tiles(i, chunk * CHUNK, CHUNK)
+            return 0
+
+        lax.fori_loop(0, wide, do_wide, 0)
+        lax.fori_loop(0, narrow, do_narrow, 0)
     if not halves:
         out_copy = pltpu.make_async_copy(acc.at[pl.ds(0, nodes)], out_refs[0], acc_sem)
         out_copy.start()
         out_copy.wait()
         return
+    acc_copy.wait()
     share = nodes // groups
     half = share // 2
-    for part, bit in ((0, 1), (1, 2)):
+    for part, bit in ((0, 2), (1, 1)):
         send_ref, keep_ref = out_refs[2 * part : 2 * part + 2]
         for j, step in enumerate((0, 3 ^ bit)):
             mine = lax.bitwise_xor(z, jnp.int32(step)) * share + part * half
             theirs = lax.bitwise_xor(z, jnp.int32(step ^ bit)) * share + part * half
-            keep_ref[j] = acc[pl.ds(pl.multiple_of(mine, half), half), :]
-            send_ref[j] = acc[pl.ds(pl.multiple_of(theirs, half), half), :].astype(jnp.bfloat16)
-
-
-def aggregate(sources, lists, units, acc, halves, earlier=()):
+            mine = pl.ds(pl.multiple_of(mine, half), half)
+            theirs = pl.ds(pl.multiple_of(theirs, half), half)
+            keep_ref[j] = acc[mine, :] + base[mine, :]
+            send_ref[j] = (acc[theirs, :] + base[theirs, :]).astype(jnp.bfloat16)
+
+
+def aggregate(sources, lists, units, acc, halves, earlier=(), hidden=False):
     rows, cols, counts, tiles = lists
     n_src = len(sources)
     groups = len(sources[0][1])
@@ -219,15 +243,16 @@
             pltpu.VMEM((n_src, feat_width, nodes), jnp.bfloat16),
             pltpu.VMEM((n_src, slots, size, size), jnp.bfloat16),
             pltpu.VMEM((nodes + size, feat_width), jnp.float32),
+            pltpu.VMEM((nodes if halves else 8, feat_width), jnp.float32),
             pltpu.SemaphoreType.DMA((n_src, groups)),
             pltpu.SemaphoreType.DMA((n_src, slots // CHUNK)),
             pltpu.SemaphoreType.DMA((3,)),
             pltpu.SemaphoreType.DMA,
         ],
-        compiler_params=pltpu.CompilerParams(vmem_limit_bytes=(6 + 3 * n_src) * 1024 * 1024),
+        compiler_params=pltpu.CompilerParams(vmem_limit_bytes=(8 + 3 * n_src) * 1024 * 1024),
         cost_estimate=pl.CostEstimate(
-            flops=2 * n_src * slots * size * size * feat_width * 4,
-            bytes_accessed=n_src * (slots * size * size + feat_width * nodes) * 2,
+            flops=0 if hidden else 2 * n_src * slots * size * size * feat_width * 4,
+            bytes_accessed=1024 if hidden else n_src * (slots * size * size + feat_width * nodes) * 2,
             transcendentals=0,
         ),
     )(*in_hbm(rows, cols, counts, tiles), *units, *earlier, *extra)
@@ -332,10 +357,10 @@
 
 
 def sum_2x2x4(send_a, keep_a, send_b, keep_b):
-    got_a = hop(send_a, "feat", 1).astype(jnp.float32)
-    got_b = hop(send_b, "feat", 2).astype(jnp.float32)
-    more_a = hop((keep_a[1] + got_a[1]).astype(jnp.bfloat16), "feat", 2).astype(jnp.float32)
-    more_b = hop((keep_b[1] + got_b[1]).astype(jnp.bfloat16), "feat", 1).astype(jnp.float32)
+    got_a = hop(send_a, "feat", 2).astype(jnp.float32)
+    got_b = hop(send_b, "feat", 1).astype(jnp.float32)
+    more_a = hop((keep_a[1] + got_a[1]).astype(jnp.bfloat16), "feat", 1).astype(jnp.float32)
+    more_b = hop((keep_b[1] + got_b[1]).astype(jnp.bfloat16), "feat", 2).astype(jnp.float32)
     total = [keep_a[0] + got_a[0] + more_a, keep_b[0] + got_b[0] + more_b]
     return jnp.concatenate(total).astype(jnp.bfloat16)
 

time: 99 us -> 98.5 us (level); the launches traced: 97.5 us -> 99.5 us
  waiting for transfers between devices: 42 us -> 45.9 us
  Pallas kernels: 9.88 us -> 8.24 us
  starting transfers between devices: 33.6 us -> 32.5 us
    ppermute x25, waiting for transfers between devices: 35.4 us -> 38.6 us  [hop(): return lax.ppermute(value, axis, [(i, i ^ bit) for i in range(size)])]
    pallas_call x2, Pallas kernels: 9.48 us -> 7.85 us  [aggregate(): pl.pallas_call(functools.partial(aggregate_kernel, sources, len(units), l...]
    ppermute x25, starting transfers between devices: 24.7 us -> 23.2 us  [hop(): return lax.ppermute(value, axis, [(i, i ^ bit) for i in range(size)])]
  transfers between devices with their start and end apart: 31 -> 31, of which waited for: 14 -> 15; matrix products, arithmetic and copies ran while one was open for 1% -> 1% of each run, Pallas kernels for 5% -> 4%
where the time goes in v4:
time: 98.5 us; the launch traced here: 99.5 us
  waiting for transfers between devices  45.9 us (47%)
  starting transfers between devices  32.5 us (33%)
  blocking collectives  9.36 us (10%)
  Pallas kernels  8.24 us (8%)
  local copies, waits for them, and re-layouts  1 us (1%)
    ppermute x25, waiting for transfers between devices, hop(): return lax.ppermute(value, axis, [(i, i ^ bit) for i in range(size)])  38.6 us
    ppermute x25, starting transfers between devices, hop(): return lax.ppermute(value, axis, [(i, i ^ bit) for i in range(size)])  23.2 us
    all_to_all x1, blocking collectives, shards(): lax.all_to_all(local_grad.astype(jnp.bfloat16).reshape(groups, feat_width...  9.36 us
    pallas_call x2, Pallas kernels, aggregate(): pl.pallas_call(functools.partial(aggregate_kernel, sources, len(units), l...  7.85 us
    ppermute x5, starting transfers between devices, cross(): return lax.ppermute(value, 'blk', perm)  6.72 us
    ppermute x1, waiting for transfers between devices, along_feat(): return lax.ppermute(value, ('blk', 'feat'), perm)  5.2 us
    ppermute x1, starting transfers between devices, along_feat(): return lax.ppermute(value, ('blk', 'feat'), perm)  2.63 us
    ppermute x5, waiting for transfers between devices, cross(): return lax.ppermute(value, 'blk', perm)  2.03 us
  transfers between devices with their start and end apart: 31, of which 15 were waited for; matrix products, arithmetic and copies ran while one was open for 1% of the time, Pallas kernels for 4%

profile of v4, /device:TPU:0, one launch (start us, length us, event | category | flops | bytes accessed | tf_op | source)
XLA Modules:
  0.0 99.5 jit_solution(6123562857509542351)
XLA Ops:
  0.7 3.1 %collective-permute-start.6 = (bf16[64,2048]{1,0:T(8,128)(2,1)}, bf16[64,2048]{1,0:T(8,128)(2,1)S(1)}, u32[]{:S(2)}, u32[]{:S(2)}) collective-permute-start(bf16[64,2048]{1,0:T(8,128)(2,1)} %refs_4_.1), channel_id=1, source_target_pairs={{0,1},{1,0},{2,3},{3,2},{4,5},{5,4},{6,7},{7,6},{8,9},{9,8},{10,11... | collective-permute-start | bytes 786440 | tf_op jit(solution)/shard_map/ppermute | solution.py:17
  3.7 1.5 %collective-permute-start.1 = (bf16[64,2048]{1,0:T(8,128)(2,1)}, bf16[64,2048]{1,0:T(8,128)(2,1)S(1)}, u32[]{:S(2)}, u32[]{:S(2)}) collective-permute-start(bf16[64,2048]{1,0:T(8,128)(2,1)} %refs_4_.1), channel_id=1, source_target_pairs={{0,8},{4,12},{8,0},{12,4},{16,24},{20,28},{24,16},{28,20},{1,9},{5... | collective-permute-start | bytes 786440 | tf_op jit(solution)/shard_map/ppermute | solution.py:17
  5.2 1.5 %collective-permute-start = (bf16[64,2048]{1,0:T(8,128)(2,1)}, bf16[64,2048]{1,0:T(8,128)(2,1)S(1)}, u32[]{:S(2)}, u32[]{:S(2)}) collective-permute-start(bf16[64,2048]{1,0:T(8,128)(2,1)} %refs_4_.1), channel_id=1, source_target_pairs={{0,16},{4,20},{8,24},{12,28},{16,0},{20,4},{24,8},{28,12},{1,17},{... | collective-permute-start | bytes 786440 | tf_op jit(solution)/shard_map/ppermute | solution.py:17
  6.8 2.6 %collective-permute-start.3 = (bf16[64,2048]{1,0:T(8,128)(2,1)}, bf16[64,2048]{1,0:T(8,128)(2,1)S(1)}, u32[]{:S(2)}, u32[]{:S(2)}) collective-permute-start(bf16[64,2048]{1,0:T(8,128)(2,1)} %refs_4_.1), channel_id=1, source_target_pairs={{0,2},{1,3},{2,0},{3,1},{4,6},{5,7},{6,4},{7,5},{8,10},{9,11},{10,... | collective-permute-start | bytes 786440 | tf_op jit(solution)/shard_map/ppermute | solution.py:17
  9.3 3.4 %collective-permute-done.6.refs_5_.own_ref = bf16[64,2048]{1,0:T(8,128)(2,1)S(1)} collective-permute-done((bf16[64,2048]{1,0:T(8,128)(2,1)}, bf16[64,2048]{1,0:T(8,128)(2,1)S(1)}, u32[]{:S(2)}, u32[]{:S(2)}) %collective-permute-start.6) | collective-permute-done | bytes 262176 | tf_op jit(solution)/shard_map/ppermute | solution.py:17
  13.0 3.1 %collective-permute-start.2 = (bf16[64,2048]{1,0:T(8,128)(2,1)S(1)}, bf16[64,2048]{1,0:T(8,128)(2,1)S(1)}, u32[]{:S(2)}, u32[]{:S(2)}) collective-permute-start(bf16[64,2048]{1,0:T(8,128)(2,1)S(1)} %shard_map.86), channel_id=1, source_target_pairs={{0,8},{4,20},{8,0},{12,28},{16,24},{20,4},{24,16},{28,12},{1,9},{5... | collective-permute-start | bytes 786440 | tf_op jit(solution)/shard_map/ppermute | solution.py:310
  16.0 4.7 %collective-permute-done.3.own_ref.refs_6_ = bf16[64,2048]{1,0:T(8,128)(2,1)S(1)} collective-permute-done((bf16[64,2048]{1,0:T(8,128)(2,1)}, bf16[64,2048]{1,0:T(8,128)(2,1)S(1)}, u32[]{:S(2)}, u32[]{:S(2)}) %collective-permute-start.3) | collective-permute-done | bytes 262176 | tf_op jit(solution)/shard_map/ppermute | solution.py:17
  20.8 0.6 collective-permute-start.16
  21.8 5.4 %collective-permute-done.7.value_ref = bf16[64,2048]{1,0:T(8,128)(2,1)S(1)} collective-permute-done((bf16[64,2048]{1,0:T(8,128)(2,1)S(1)}, bf16[64,2048]{1,0:T(8,128)(2,1)S(1)}, u32[]{:S(2)}, u32[]{:S(2)}) %collective-permute-start.7) | collective-permute-done | bytes 262176 | tf_op jit(solution)/shard_map/ppermute | solution.py:17
  28.4 2.6 %collective-permute-start.14 = (bf16[2,64,2048]{2,1,0:T(8,128)(2,1)S(1)}, bf16[2,64,2048]{2,1,0:T(8,128)(2,1)S(1)}, u32[]{:S(2)}, u32[]{:S(2)}) collective-permute-start(bf16[2,64,2048]{2,1,0:T(8,128)(2,1)S(1)} %shard_map.93), channel_id=1, source_target_pairs={{0,3},{1,2},{2,1},{3,0},{4,5},{5,4},{6,7},{7,6},{8,11},{9,10},{10,... | collective-permute-start | bytes 1572872 | tf_op jit(solution)/shard_map/ppermute | solution.py:314
  31.2 1.9 %collective-permute-start.17 = (bf16[2,64,2048]{2,1,0:T(8,128)(2,1)S(1)}, bf16[2,64,2048]{2,1,0:T(8,128)(2,1)S(1)}, u32[]{:S(2)}, u32[]{:S(2)}) collective-permute-start(bf16[2,64,2048]{2,1,0:T(8,128)(2,1)S(1)} %shard_map.97), channel_id=1, source_target_pairs={{0,8},{4,20},{8,0},{12,28},{16,24},{20,4},{24,16},{28,12},{1,9},{5... | collective-permute-start | bytes 1572872 | tf_op jit(solution)/shard_map/ppermute | solution.py:310
  33.0 3.7 %shard_map.90.refs_0_.refs_20_ = f32[2048,256]{1,0:T(8,128)S(1)} custom-call(s32[1,1,8,48]{3,2,1,0:T(8,128)} %refs_0_.3, s32[1,1,8,48]{3,2,1,0:T(8,128)} %refs_1_.3, s32[1,1,8]{2,1,0:T(1,128)} %refs_2_.3, bf16[1,1,8,48,128,128]{5,4,3,2,1,0:T(8,128)(2,1)} %refs_3_.3, bf16[64,2048]{1,0:T(8,128)(2,1)S(1)} %copy-done.1, ...), custom_call_target="tpu_custom_call" | custom-call | flops 3221225472 | bytes 5242880 | tf_op jit(solution)/shard_map/pallas_call | solution.py:234
  37.1 0.6 collective-permute-start.11
  37.8 5.2 %collective-permute-done.14.value_ref = bf16[2,64,2048]{2,1,0:T(8,128)(2,1)S(1)} collective-permute-done((bf16[2,64,2048]{2,1,0:T(8,128)(2,1)S(1)}, bf16[2,64,2048]{2,1,0:T(8,128)(2,1)S(1)}, u32[]{:S(2)}, u32[]{:S(2)}) %collective-permute-start.14) | collective-permute-done | bytes 524320 | tf_op jit(solution)/shard_map/ppermute | solution.py:314
  43.7 1.0 collective-permute-done.11.value_ref
  44.8 0.7 collective-permute-done.17.refs_12_
  46.1 1.7 %collective-permute-done.13.refs_7_ = bf16[64,2048]{1,0:T(8,128)(2,1)S(1)} collective-permute-done((bf16[64,2048]{1,0:T(8,128)(2,1)S(1)}, bf16[64,2048]{1,0:T(8,128)(2,1)S(1)}, u32[]{:S(2)}, u32[]{:S(2)}) %collective-permute-start.13) | collective-permute-done | bytes 262176 | tf_op jit(solution)/shard_map/ppermute | solution.py:17
  47.8 4.2 %shard_map.99 = (bf16[2,256,256]{2,1,0:T(8,128)(2,1)S(1)}, f32[2,256,256]{2,1,0:T(8,128)S(1)}, bf16[2,256,256]{2,1,0:T(8,128)(2,1)S(1)}, f32[2,256,256]{2,1,0:T(8,128)S(1)}) custom-call(s32[1,1,8,48]{3,2,1,0:T(8,128)} %refs_0_.3, s32[1,1,8,48]{3,2,1,0:T(8,128)} %refs_1_.3, s32[1,1,8]{2,1,0:T(1,128)} %refs_2_.3, bf16[1,1,8,48,128,128]{5,4,3,2,1,0:T(8,128)(2,1)} %refs_3_.3, ...), custom_call_target="tpu_custom_call" | custom-call | flops 9663676416 | bytes 15728640 | tf_op jit(solution)/shard_map/pallas_call | solution.py:234
  52.0 2.0 %collective-permute-start.23 = (bf16[2,256,256]{2,1,0:T(8,128)(2,1)S(1)}, bf16[2,256,256]{2,1,0:T(8,128)(2,1)S(1)}, u32[]{:S(2)}, u32[]{:S(2)}) collective-permute-start(bf16[2,256,256]{2,1,0:T(8,128)(2,1)S(1)} %get-tuple-element.7), channel_id=1, source_target_pairs={{0,2},{1,3},{2,0},{3,1},{4,6},{5,7},{6,4},{7,5},{8,10},{9,11},{10,... | collective-permute-start | bytes 786440 | tf_op jit(solution)/shard_map/ppermute | solution.py:17
  54.0 1.5 %collective-permute-start.25 = (bf16[2,256,256]{2,1,0:T(8,128)(2,1)S(1)}, bf16[2,256,256]{2,1,0:T(8,128)(2,1)S(1)}, u32[]{:S(2)}, u32[]{:S(2)}) collective-permute-start(bf16[2,256,256]{2,1,0:T(8,128)(2,1)S(1)} %get-tuple-element.9), channel_id=1, source_target_pairs={{0,1},{1,0},{2,3},{3,2},{4,5},{5,4},{6,7},{7,6},{8,9},{9,8},{10,11... | collective-permute-start | bytes 786440 | tf_op jit(solution)/shard_map/ppermute | solution.py:17
  55.6 11.8 %collective-permute-done.23 = bf16[2,256,256]{2,1,0:T(8,128)(2,1)S(1)} collective-permute-done((bf16[2,256,256]{2,1,0:T(8,128)(2,1)S(1)}, bf16[2,256,256]{2,1,0:T(8,128)(2,1)S(1)}, u32[]{:S(2)}, u32[]{:S(2)}) %collective-permute-start.23) | collective-permute-done | bytes 262176 | tf_op jit(solution)/shard_map/ppermute | solution.py:17
  67.9 3.4 %collective-permute-start.26 = (bf16[256,256]{1,0:T(8,128)(2,1)S(1)}, bf16[256,256]{1,0:T(8,128)(2,1)S(1)}, u32[]{:S(2)}, u32[]{:S(2)}) collective-permute-start(bf16[256,256]{1,0:T(8,128)(2,1)S(1)} %fusion.9), channel_id=1, source_target_pairs={{0,2},{1,3},{2,0},{3,1},{4,6},{5,7},{6,4},{7,5},{8,10},{9,11},{10,... | collective-permute-start | bytes 393224 | tf_op jit(solution)/shard_map/ppermute | solution.py:17
  71.3 4.3 %collective-permute-done.24 = bf16[256,256]{1,0:T(8,128)(2,1)S(1)} collective-permute-done((bf16[256,256]{1,0:T(8,128)(2,1)S(1)}, bf16[256,256]{1,0:T(8,128)(2,1)S(1)}, u32[]{:S(2)}, u32[]{:S(2)}) %collective-permute-start.24) | collective-permute-done | bytes 131104 | tf_op jit(solution)/shard_map/ppermute | solution.py:17
  75.7 2.0 %collective-permute-done.26 = bf16[256,256]{1,0:T(8,128)(2,1)S(1)} collective-permute-done((bf16[256,256]{1,0:T(8,128)(2,1)S(1)}, bf16[256,256]{1,0:T(8,128)(2,1)S(1)}, u32[]{:S(2)}, u32[]{:S(2)}) %collective-permute-start.26) | collective-permute-done | bytes 131104 | tf_op jit(solution)/shard_map/ppermute | solution.py:17
  78.5 9.4 %all_to_all.5 = bf16[4,64,256]{2,1,0:T(8,128)(2,1)S(1)} all-to-all(bf16[4,64,256]{2,1,0:T(8,128)(2,1)S(1)} %bitcast.20), channel_id=1, replica_groups=mesh['blk'=8,'feat'=4] {'feat'}, dimensions={0} | all-to-all | bytes 262144 | tf_op jit(solution)/shard_map/all_to_all | solution.py:390
  88.0 1.2 %collective-permute-done.27 = bf16[64,256]{1,0:T(8,128)(2,1)S(1)} collective-permute-done((bf16[64,256]{1,0:T(8,128)(2,1)S(1)}, bf16[64,256]{1,0:T(8,128)(2,1)S(1)}, u32[]{:S(2)}, u32[]{:S(2)}) %collective-permute-start.27) | collective-permute-done | bytes 32800 | tf_op jit(solution)/shard_map/ppermute | solution.py:17
  89.2 2.4 %collective-permute-start.28 = (bf16[64,256]{1,0:T(8,128)(2,1)S(1)}, bf16[64,256]{1,0:T(8,128)(2,1)S(1)}, u32[]{:S(2)}, u32[]{:S(2)}) collective-permute-start(bf16[64,256]{1,0:T(8,128)(2,1)S(1)} %add_convert_fusion), channel_id=1, source_target_pairs={{0,8},{4,12},{8,0},{12,4},{16,24},{20,28},{24,16},{28,20},{1,9},{5... | collective-permute-start | bytes 98312 | tf_op jit(solution)/shard_map/ppermute | solution.py:17
  91.6 2.5 %collective-permute-start.29 = (bf16[64,256]{1,0:T(8,128)(2,1)S(1)}, bf16[64,256]{1,0:T(8,128)(2,1)S(1)}, u32[]{:S(2)}, u32[]{:S(2)}) collective-permute-start(bf16[64,256]{1,0:T(8,128)(2,1)S(1)} %add_convert_fusion), channel_id=1, source_target_pairs={{0,16},{4,20},{8,24},{12,28},{16,0},{20,4},{24,8},{28,12},{1,17},{... | collective-permute-start | bytes 98312 | tf_op jit(solution)/shard_map/ppermute | solution.py:17
  94.1 0.8 copy.10
  94.9 1.0 %collective-permute-done.29 = bf16[64,256]{1,0:T(8,128)(2,1)S(1)} collective-permute-done((bf16[64,256]{1,0:T(8,128)(2,1)S(1)}, bf16[64,256]{1,0:T(8,128)(2,1)S(1)}, u32[]{:S(2)}, u32[]{:S(2)}) %collective-permute-start.29) | collective-permute-done | bytes 32800 | tf_op jit(solution)/shard_map/ppermute | solution.py:17
  96.0 2.9 %collective-permute-done.30 = bf16[64,256]{1,0:T(8,128)(2,1)S(1)} collective-permute-done((bf16[64,256]{1,0:T(8,128)(2,1)S(1)}, bf16[64,256]{1,0:T(8,128)(2,1)S(1)}, u32[]{:S(2)}, u32[]{:S(2)}) %collective-permute-start.30) | collective-permute-done | bytes 32800 | tf_op jit(solution)/shard_map/ppermute | solution.py:17
  98.9 0.7 add_multiply_fusion
  (64 shorter events, 5.4 us)
Async XLA Ops:
  0.6 77.1 %copy-start = (bf16[256,256]{1,0:T(8,128)(2,1)S(1)}, bf16[256,256]{1,0:T(8,128)(2,1)}, u32[]{:S(2)}) copy-start(bf16[256,256]{1,0:T(8,128)(2,1)} %param.12) | copy-start | bytes 393220
  0.7 12.1 %collective-permute-start.6 = (bf16[64,2048]{1,0:T(8,128)(2,1)}, bf16[64,2048]{1,0:T(8,128)(2,1)S(1)}, u32[]{:S(2)}, u32[]{:S(2)}) collective-permute-start(bf16[64,2048]{1,0:T(8,128)(2,1)} %refs_4_.1), channel_id=1, source_target_pairs={{0,1},{1,0},{2,3},{3,2},{4,5},{5,4},{6,7},{7,6},{8,9},{9,8},{10,11... | collective-permute-start | bytes 786440 | tf_op jit(solution)/shard_map/ppermute | solution.py:17
  3.7 9.0 %collective-permute-start.1 = (bf16[64,2048]{1,0:T(8,128)(2,1)}, bf16[64,2048]{1,0:T(8,128)(2,1)S(1)}, u32[]{:S(2)}, u32[]{:S(2)}) collective-permute-start(bf16[64,2048]{1,0:T(8,128)(2,1)} %refs_4_.1), channel_id=1, source_target_pairs={{0,8},{4,12},{8,0},{12,4},{16,24},{20,28},{24,16},{28,20},{1,9},{5... | collective-permute-start | bytes 786440 | tf_op jit(solution)/shard_map/ppermute | solution.py:17
  5.2 7.7 %collective-permute-start = (bf16[64,2048]{1,0:T(8,128)(2,1)}, bf16[64,2048]{1,0:T(8,128)(2,1)S(1)}, u32[]{:S(2)}, u32[]{:S(2)}) collective-permute-start(bf16[64,2048]{1,0:T(8,128)(2,1)} %refs_4_.1), channel_id=1, source_target_pairs={{0,16},{4,20},{8,24},{12,28},{16,0},{20,4},{24,8},{28,12},{1,17},{... | collective-permute-start | bytes 786440 | tf_op jit(solution)/shard_map/ppermute | solution.py:17
  6.8 14.0 %collective-permute-start.3 = (bf16[64,2048]{1,0:T(8,128)(2,1)}, bf16[64,2048]{1,0:T(8,128)(2,1)S(1)}, u32[]{:S(2)}, u32[]{:S(2)}) collective-permute-start(bf16[64,2048]{1,0:T(8,128)(2,1)} %refs_4_.1), channel_id=1, source_target_pairs={{0,2},{1,3},{2,0},{3,1},{4,6},{5,7},{6,4},{7,5},{8,10},{9,11},{10,... | collective-permute-start | bytes 786440 | tf_op jit(solution)/shard_map/ppermute | solution.py:17
  12.8 8.0 %collective-permute-start.9 = (bf16[64,2048]{1,0:T(8,128)(2,1)S(1)}, bf16[64,2048]{1,0:T(8,128)(2,1)S(1)}, u32[]{:S(2)}, u32[]{:S(2)}) collective-permute-start(bf16[64,2048]{1,0:T(8,128)(2,1)S(1)} %collective-permute-done.6.refs_5_.own_ref), channel_id=1, source_target_pairs={{0,4},{4,0},{8,12},{12,8},{16,20},{20,16},{24,28},{28,24},{1,5},{5... | collective-permute-start | bytes 786440 | tf_op jit(solution)/shard_map/ppermute | solution.py:17
  13.0 8.5 %collective-permute-start.2 = (bf16[64,2048]{1,0:T(8,128)(2,1)S(1)}, bf16[64,2048]{1,0:T(8,128)(2,1)S(1)}, u32[]{:S(2)}, u32[]{:S(2)}) collective-permute-start(bf16[64,2048]{1,0:T(8,128)(2,1)S(1)} %shard_map.86), channel_id=1, source_target_pairs={{0,8},{4,20},{8,0},{12,28},{16,24},{20,4},{24,16},{28,12},{1,9},{5... | collective-permute-start | bytes 786440 | tf_op jit(solution)/shard_map/ppermute | solution.py:310
  20.8 6.4 %collective-permute-start.7 = (bf16[64,2048]{1,0:T(8,128)(2,1)S(1)}, bf16[64,2048]{1,0:T(8,128)(2,1)S(1)}, u32[]{:S(2)}, u32[]{:S(2)}) collective-permute-start(bf16[64,2048]{1,0:T(8,128)(2,1)S(1)} %collective-permute-done.3.own_ref.refs_6_), channel_id=1, source_target_pairs={{0,1},{1,0},{2,3},{3,2},{4,5},{5,4},{6,7},{7,6},{8,9},{9,8},{10,11... | collective-permute-start | bytes 786440 | tf_op jit(solution)/shard_map/ppermute | solution.py:17
  20.8 7.0 %collective-permute-start.4 = (bf16[64,2048]{1,0:T(8,128)(2,1)S(1)}, bf16[64,2048]{1,0:T(8,128)(2,1)S(1)}, u32[]{:S(2)}, u32[]{:S(2)}) collective-permute-start(bf16[64,2048]{1,0:T(8,128)(2,1)S(1)} %collective-permute-done.3.own_ref.refs_6_), channel_id=1, source_target_pairs={{0,4},{4,0},{8,12},{12,8},{16,20},{20,16},{24,28},{28,24},{1,5},{5... | collective-permute-start | bytes 786440 | tf_op jit(solution)/shard_map/ppermute | solution.py:17
  20.8 10.2 %collective-permute-start.16 = (bf16[2,64,2048]{2,1,0:T(8,128)(2,1)S(1)}, bf16[2,64,2048]{2,1,0:T(8,128)(2,1)S(1)}, u32[]{:S(2)}, u32[]{:S(2)}) collective-permute-start(bf16[2,64,2048]{2,1,0:T(8,128)(2,1)S(1)} %shard_map.95), channel_id=1, source_target_pairs={{0,8},{4,20},{8,0},{12,28},{16,24},{20,4},{24,16},{28,12},{1,9},{5... | collective-permute-start | bytes 1572872 | tf_op jit(solution)/shard_map/ppermute | solution.py:310
  21.5 6.9 %collective-permute-start.12 = (bf16[64,2048]{1,0:T(8,128)(2,1)S(1)}, bf16[64,2048]{1,0:T(8,128)(2,1)S(1)}, u32[]{:S(2)}, u32[]{:S(2)}) collective-permute-start(bf16[64,2048]{1,0:T(8,128)(2,1)S(1)} %shard_map.87.own_ref.refs_4_), channel_id=1, source_target_pairs={{0,4},{4,0},{8,12},{12,8},{16,20},{20,16},{24,28},{28,24},{1,5},{5... | collective-permute-start | bytes 786440 | tf_op jit(solution)/shard_map/ppermute | solution.py:17
  27.2 3.9 %collective-permute-start.10 = (bf16[64,2048]{1,0:T(8,128)(2,1)S(1)}, bf16[64,2048]{1,0:T(8,128)(2,1)S(1)}, u32[]{:S(2)}, u32[]{:S(2)}) collective-permute-start(bf16[64,2048]{1,0:T(8,128)(2,1)S(1)} %shard_map.89.refs_7_.own_ref), channel_id=1, source_target_pairs={{0,4},{4,0},{8,12},{12,8},{16,20},{20,16},{24,28},{28,24},{1,5},{5... | collective-permute-start | bytes 786440 | tf_op jit(solution)/shard_map/ppermute | solution.py:17
  27.3 5.8 %collective-permute-start.8 = (bf16[64,2048]{1,0:T(8,128)(2,1)S(1)}, bf16[64,2048]{1,0:T(8,128)(2,1)S(1)}, u32[]{:S(2)}, u32[]{:S(2)}) collective-permute-start(bf16[64,2048]{1,0:T(8,128)(2,1)S(1)} %copy-done.1), channel_id=1, source_target_pairs={{0,4},{4,0},{8,12},{12,8},{16,20},{20,16},{24,28},{28,24},{1,5},{5... | collective-permute-start | bytes 786440 | tf_op jit(solution)/shard_map/ppermute | solution.py:17
  27.8 9.2 %collective-permute-start.5 = (bf16[2,64,2048]{2,1,0:T(8,128)(2,1)S(1)}, bf16[2,64,2048]{2,1,0:T(8,128)(2,1)S(1)}, u32[]{:S(2)}, u32[]{:S(2)}) collective-permute-start(bf16[2,64,2048]{2,1,0:T(8,128)(2,1)S(1)} %shard_map.88), channel_id=1, source_target_pairs={{0,8},{4,20},{8,0},{12,28},{16,24},{20,4},{24,16},{28,12},{1,9},{5... | collective-permute-start | bytes 1572872 | tf_op jit(solution)/shard_map/ppermute | solution.py:310
  28.4 14.6 %collective-permute-start.14 = (bf16[2,64,2048]{2,1,0:T(8,128)(2,1)S(1)}, bf16[2,64,2048]{2,1,0:T(8,128)(2,1)S(1)}, u32[]{:S(2)}, u32[]{:S(2)}) collective-permute-start(bf16[2,64,2048]{2,1,0:T(8,128)(2,1)S(1)} %shard_map.93), channel_id=1, source_target_pairs={{0,3},{1,2},{2,1},{3,0},{4,5},{5,4},{6,7},{7,6},{8,11},{9,10},{10,... | collective-permute-start | bytes 1572872 | tf_op jit(solution)/shard_map/ppermute | solution.py:314
  31.1 12.0 %collective-permute-start.22 = (bf16[64,2048]{1,0:T(8,128)(2,1)S(1)}, bf16[64,2048]{1,0:T(8,128)(2,1)S(1)}, u32[]{:S(2)}, u32[]{:S(2)}) collective-permute-start(bf16[64,2048]{1,0:T(8,128)(2,1)S(1)} %collective-permute-done.even_ref.refs_17_), channel_id=1, source_target_pairs={{0,4},{4,0},{8,12},{12,8},{16,20},{20,16},{24,28},{28,24},{1,5},{5... | collective-permute-start | bytes 786440 | tf_op jit(solution)/shard_map/ppermute | solution.py:17
  31.2 14.3 %collective-permute-start.17 = (bf16[2,64,2048]{2,1,0:T(8,128)(2,1)S(1)}, bf16[2,64,2048]{2,1,0:T(8,128)(2,1)S(1)}, u32[]{:S(2)}, u32[]{:S(2)}) collective-permute-start(bf16[2,64,2048]{2,1,0:T(8,128)(2,1)S(1)} %shard_map.97), channel_id=1, source_target_pairs={{0,8},{4,20},{8,0},{12,28},{16,24},{20,4},{24,16},{28,12},{1,9},{5... | collective-permute-start | bytes 1572872 | tf_op jit(solution)/shard_map/ppermute | solution.py:310
  37.1 7.5 %collective-permute-start.11 = (bf16[64,2048]{1,0:T(8,128)(2,1)S(1)}, bf16[64,2048]{1,0:T(8,128)(2,1)S(1)}, u32[]{:S(2)}, u32[]{:S(2)}) collective-permute-start(bf16[64,2048]{1,0:T(8,128)(2,1)S(1)} %shard_map.91), channel_id=1, source_target_pairs={{0,16},{4,12},{8,24},{12,4},{16,0},{20,28},{24,8},{28,20},{1,17},{... | collective-permute-start | bytes 786440 | tf_op jit(solution)/shard_map/ppermute | solution.py:310
  37.8 7.8 %collective-permute-start.21 = (bf16[64,2048]{1,0:T(8,128)(2,1)S(1)}, bf16[64,2048]{1,0:T(8,128)(2,1)S(1)}, u32[]{:S(2)}, u32[]{:S(2)}) collective-permute-start(bf16[64,2048]{1,0:T(8,128)(2,1)S(1)} %shard_map.98), channel_id=1, source_target_pairs={{0,4},{4,0},{8,12},{12,8},{16,20},{20,16},{24,28},{28,24},{1,5},{5... | collective-permute-start | bytes 786440 | tf_op jit(solution)/shard_map/ppermute | solution.py:17
  43.0 3.1 %collective-permute-start.18 = (bf16[2,64,2048]{2,1,0:T(8,128)(2,1)S(1)}, bf16[2,64,2048]{2,1,0:T(8,128)(2,1)S(1)}, u32[]{:S(2)}, u32[]{:S(2)}) collective-permute-start(bf16[2,64,2048]{2,1,0:T(8,128)(2,1)S(1)} %shard_map.96.refs_0_.refs_10_), channel_id=1, source_target_pairs={{0,4},{4,0},{8,12},{12,8},{16,20},{20,16},{24,28},{28,24},{1,5},{5... | collective-permute-start | bytes 1572872 | tf_op jit(solution)/shard_map/ppermute | solution.py:17
  43.1 3.0 %collective-permute-start.19 = (bf16[2,64,2048]{2,1,0:T(8,128)(2,1)S(1)}, bf16[2,64,2048]{2,1,0:T(8,128)(2,1)S(1)}, u32[]{:S(2)}, u32[]{:S(2)}) collective-permute-start(bf16[2,64,2048]{2,1,0:T(8,128)(2,1)S(1)} %collective-permute-done.5.pair_ref.refs_11_), channel_id=1, source_target_pairs={{0,4},{4,0},{8,12},{12,8},{16,20},{20,16},{24,28},{28,24},{1,5},{5... | collective-permute-start | bytes 1572872 | tf_op jit(solution)/shard_map/ppermute | solution.py:17
  44.6 3.2 %collective-permute-start.15 = (bf16[2,64,2048]{2,1,0:T(8,128)(2,1)S(1)}, bf16[2,64,2048]{2,1,0:T(8,128)(2,1)S(1)}, u32[]{:S(2)}, u32[]{:S(2)}) collective-permute-start(bf16[2,64,2048]{2,1,0:T(8,128)(2,1)S(1)} %shard_map.94.refs_8_), channel_id=1, source_target_pairs={{0,4},{4,0},{8,12},{12,8},{16,20},{20,16},{24,28},{28,24},{1,5},{5... | collective-permute-start | bytes 1572872 | tf_op jit(solution)/shard_map/ppermute | solution.py:17
  45.5 2.3 %collective-permute-start.20 = (bf16[2,64,2048]{2,1,0:T(8,128)(2,1)S(1)}, bf16[2,64,2048]{2,1,0:T(8,128)(2,1)S(1)}, u32[]{:S(2)}, u32[]{:S(2)}) collective-permute-start(bf16[2,64,2048]{2,1,0:T(8,128)(2,1)S(1)} %collective-permute-done.17.refs_12_), channel_id=1, source_target_pairs={{0,4},{4,0},{8,12},{12,8},{16,20},{20,16},{24,28},{28,24},{1,5},{5... | collective-permute-start | bytes 1572872 | tf_op jit(solution)/shard_map/ppermute | solution.py:17
  45.5 2.2 %collective-permute-start.13 = (bf16[64,2048]{1,0:T(8,128)(2,1)S(1)}, bf16[64,2048]{1,0:T(8,128)(2,1)S(1)}, u32[]{:S(2)}, u32[]{:S(2)}) collective-permute-start(bf16[64,2048]{1,0:T(8,128)(2,1)S(1)} %shard_map.92.refs_5_), channel_id=1, source_target_pairs={{0,4},{4,0},{8,12},{12,8},{16,20},{20,16},{24,28},{28,24},{1,5},{5... | collective-permute-start | bytes 786440 | tf_op jit(solution)/shard_map/ppermute | solution.py:17
  52.0 15.4 %collective-permute-start.23 = (bf16[2,256,256]{2,1,0:T(8,128)(2,1)S(1)}, bf16[2,256,256]{2,1,0:T(8,128)(2,1)S(1)}, u32[]{:S(2)}, u32[]{:S(2)}) collective-permute-start(bf16[2,256,256]{2,1,0:T(8,128)(2,1)S(1)} %get-tuple-element.7), channel_id=1, source_target_pairs={{0,2},{1,3},{2,0},{3,1},{4,6},{5,7},{6,4},{7,5},{8,10},{9,11},{10,... | collective-permute-start | bytes 786440 | tf_op jit(solution)/shard_map/ppermute | solution.py:17
  54.0 13.9 %collective-permute-start.25 = (bf16[2,256,256]{2,1,0:T(8,128)(2,1)S(1)}, bf16[2,256,256]{2,1,0:T(8,128)(2,1)S(1)}, u32[]{:S(2)}, u32[]{:S(2)}) collective-permute-start(bf16[2,256,256]{2,1,0:T(8,128)(2,1)S(1)} %get-tuple-element.9), channel_id=1, source_target_pairs={{0,1},{1,0},{2,3},{3,2},{4,5},{5,4},{6,7},{7,6},{8,9},{9,8},{10,11... | collective-permute-start | bytes 786440 | tf_op jit(solution)/shard_map/ppermute | solution.py:17
  67.5 8.2 %collective-permute-start.24 = (bf16[256,256]{1,0:T(8,128)(2,1)S(1)}, bf16[256,256]{1,0:T(8,128)(2,1)S(1)}, u32[]{:S(2)}, u32[]{:S(2)}) collective-permute-start(bf16[256,256]{1,0:T(8,128)(2,1)S(1)} %fusion.8), channel_id=1, source_target_pairs={{0,1},{1,0},{2,3},{3,2},{4,5},{5,4},{6,7},{7,6},{8,9},{9,8},{10,11... | collective-permute-start | bytes 393224 | tf_op jit(solution)/shard_map/ppermute | solution.py:17
  67.9 9.8 %collective-permute-start.26 = (bf16[256,256]{1,0:T(8,128)(2,1)S(1)}, bf16[256,256]{1,0:T(8,128)(2,1)S(1)}, u32[]{:S(2)}, u32[]{:S(2)}) collective-permute-start(bf16[256,256]{1,0:T(8,128)(2,1)S(1)} %fusion.9), channel_id=1, source_target_pairs={{0,2},{1,3},{2,0},{3,1},{4,6},{5,7},{6,4},{7,5},{8,10},{9,11},{10,... | collective-permute-start | bytes 393224 | tf_op jit(solution)/shard_map/ppermute | solution.py:17
  87.9 1.3 %collective-permute-start.27 = (bf16[64,256]{1,0:T(8,128)(2,1)S(1)}, bf16[64,256]{1,0:T(8,128)(2,1)S(1)}, u32[]{:S(2)}, u32[]{:S(2)}) collective-permute-start(bf16[64,256]{1,0:T(8,128)(2,1)S(1)} %reduce_sum.12), channel_id=1, source_target_pairs={{0,4},{4,0},{8,12},{12,8},{16,20},{20,16},{24,28},{28,24},{1,5},{5... | collective-permute-start | bytes 98312 | tf_op jit(solution)/shard_map/ppermute | solution.py:17
  89.2 5.7 %collective-permute-start.28 = (bf16[64,256]{1,0:T(8,128)(2,1)S(1)}, bf16[64,256]{1,0:T(8,128)(2,1)S(1)}, u32[]{:S(2)}, u32[]{:S(2)}) collective-permute-start(bf16[64,256]{1,0:T(8,128)(2,1)S(1)} %add_convert_fusion), channel_id=1, source_target_pairs={{0,8},{4,12},{8,0},{12,4},{16,24},{20,28},{24,16},{28,20},{1,9},{5... | collective-permute-start | bytes 98312 | tf_op jit(solution)/shard_map/ppermute | solution.py:17
  91.6 4.4 %collective-permute-start.29 = (bf16[64,256]{1,0:T(8,128)(2,1)S(1)}, bf16[64,256]{1,0:T(8,128)(2,1)S(1)}, u32[]{:S(2)}, u32[]{:S(2)}) collective-permute-start(bf16[64,256]{1,0:T(8,128)(2,1)S(1)} %add_convert_fusion), channel_id=1, source_target_pairs={{0,16},{4,20},{8,24},{12,28},{16,0},{20,4},{24,8},{28,12},{1,17},{... | collective-permute-start | bytes 98312 | tf_op jit(solution)/shard_map/ppermute | solution.py:17
  94.1 4.8 %collective-permute-start.30 = (bf16[64,256]{1,0:T(8,128)(2,1)S(1)}, bf16[64,256]{1,0:T(8,128)(2,1)S(1)}, u32[]{:S(2)}, u32[]{:S(2)}) collective-permute-start(bf16[64,256]{1,0:T(8,128)(2,1)S(1)} %add_convert_fusion), channel_id=1, source_target_pairs={{0,24},{4,28},{8,16},{12,20},{16,8},{20,12},{24,0},{28,4},{1,25},{... | collective-permute-start | bytes 98312 | tf_op jit(solution)/shard_map/ppermute | solution.py:17
  (2 other events, 36.5 us)

commit v5 on v4

--- a/solution.py
+++ b/solution.py
@@ -387,10 +387,15 @@
         jnp.bfloat16
     )
     local_grad = jnp.dot(slope, aggregated, preferred_element_type=jnp.float32)
-    terms = lax.all_to_all(
-        local_grad.astype(jnp.bfloat16).reshape(groups, feat_width // groups, feat_width), "feat", 0, 0
-    )
-    grad = jnp.sum(terms.astype(jnp.float32), axis=0)
+    local_grad = local_grad.astype(jnp.bfloat16)
+    share = feat_width // groups
+    z = lax.axis_index("feat")
+
+    def rows_for(bit):
+        return lax.dynamic_slice_in_dim(local_grad, lax.bitwise_xor(z, jnp.int32(bit)) * share, share, 0)
+
+    terms = [hop(rows_for(bit), "feat", bit).astype(jnp.float32) for bit in range(groups - 1, 0, -1)]
+    grad = functools.reduce(jnp.add, terms, rows_for(0).astype(jnp.float32))
     sent = grad.astype(jnp.bfloat16)
     grad = sent.astype(jnp.float32) + hop(sent, "blk", 1).astype(jnp.float32)
     sent = grad.astype(jnp.bfloat16)

time: 98.5 us -> 97.2 us (0.987); the launches traced: 99.5 us -> 96.8 us
  blocking collectives: 9.36 us -> 0 us
  Pallas kernels: 8.24 us -> 13.8 us
  starting transfers between devices: 32.5 us -> 35.3 us
  waiting for transfers between devices: 45.9 us -> 44.1 us
    all_to_all x1 -> x0, blocking collectives: 9.36 us -> none  [shards(): lax.all_to_all(local_grad.astype(jnp.bfloat16).reshape(groups, feat_width...]
    pallas_call x2, Pallas kernels: 7.85 us -> 13.4 us  [aggregate(): pl.pallas_call(functools.partial(aggregate_kernel, sources, len(units), l...]
    ppermute x25 -> x28, starting transfers between devices: 23.2 us -> 26.5 us  [hop(): return lax.ppermute(value, axis, [(i, i ^ bit) for i in range(size)])]
    ppermute x25 -> x28, waiting for transfers between devices: 38.6 us -> 38.2 us  [hop(): return lax.ppermute(value, axis, [(i, i ^ bit) for i in range(size)])]
  transfers between devices with their start and end apart: 31 -> 34, of which waited for: 15 -> 15; matrix products, arithmetic and copies ran while one was open for 1% -> 1% of each run, Pallas kernels for 4% -> 6%
where the time goes in v5:
time: 97.2 us; the launch traced here: 96.8 us
  waiting for transfers between devices  44.1 us (45%)
  starting transfers between devices  35.3 us (36%)
  Pallas kernels  13.8 us (14%)
  local copies, waits for them, and re-layouts  1.01 us (1%)
    ppermute x28, waiting for transfers between devices, hop(): return lax.ppermute(value, axis, [(i, i ^ bit) for i in range(size)])  38.2 us
    ppermute x28, starting transfers between devices, hop(): return lax.ppermute(value, axis, [(i, i ^ bit) for i in range(size)])  26.5 us
    pallas_call x2, Pallas kernels, aggregate(): pl.pallas_call(functools.partial(aggregate_kernel, sources, len(units), l...  13.4 us
    ppermute x5, starting transfers between devices, cross(): return lax.ppermute(value, 'blk', perm)  6.16 us
    ppermute x1, waiting for transfers between devices, along_feat(): return lax.ppermute(value, ('blk', 'feat'), perm)  4.62 us
    ppermute x1, starting transfers between devices, along_feat(): return lax.ppermute(value, ('blk', 'feat'), perm)  2.63 us
  transfers between devices with their start and end apart: 34, of which 15 were waited for; matrix products, arithmetic and copies ran while one was open for 1% of the time, Pallas kernels for 6%

profile of v5, /device:TPU:0, one launch (start us, length us, event | category | flops | bytes accessed | tf_op | source)
XLA Modules:
  0.0 96.8 jit_solution(5251421560234521077)
XLA Ops:
  0.7 3.1 %collective-permute-start.6 = (bf16[64,2048]{1,0:T(8,128)(2,1)}, bf16[64,2048]{1,0:T(8,128)(2,1)S(1)}, u32[]{:S(2)}, u32[]{:S(2)}) collective-permute-start(bf16[64,2048]{1,0:T(8,128)(2,1)} %refs_4_.1), channel_id=1, source_target_pairs={{0,1},{1,0},{2,3},{3,2},{4,5},{5,4},{6,7},{7,6},{8,9},{9,8},{10,11... | collective-permute-start | bytes 786440 | tf_op jit(solution)/shard_map/ppermute | solution.py:17
  3.7 1.5 %collective-permute-start.1 = (bf16[64,2048]{1,0:T(8,128)(2,1)}, bf16[64,2048]{1,0:T(8,128)(2,1)S(1)}, u32[]{:S(2)}, u32[]{:S(2)}) collective-permute-start(bf16[64,2048]{1,0:T(8,128)(2,1)} %refs_4_.1), channel_id=1, source_target_pairs={{0,8},{4,12},{8,0},{12,4},{16,24},{20,28},{24,16},{28,20},{1,9},{5... | collective-permute-start | bytes 786440 | tf_op jit(solution)/shard_map/ppermute | solution.py:17
  5.2 1.5 %collective-permute-start = (bf16[64,2048]{1,0:T(8,128)(2,1)}, bf16[64,2048]{1,0:T(8,128)(2,1)S(1)}, u32[]{:S(2)}, u32[]{:S(2)}) collective-permute-start(bf16[64,2048]{1,0:T(8,128)(2,1)} %refs_4_.1), channel_id=1, source_target_pairs={{0,16},{4,20},{8,24},{12,28},{16,0},{20,4},{24,8},{28,12},{1,17},{... | collective-permute-start | bytes 786440 | tf_op jit(solution)/shard_map/ppermute | solution.py:17
  6.8 2.6 %collective-permute-start.3 = (bf16[64,2048]{1,0:T(8,128)(2,1)}, bf16[64,2048]{1,0:T(8,128)(2,1)S(1)}, u32[]{:S(2)}, u32[]{:S(2)}) collective-permute-start(bf16[64,2048]{1,0:T(8,128)(2,1)} %refs_4_.1), channel_id=1, source_target_pairs={{0,2},{1,3},{2,0},{3,1},{4,6},{5,7},{6,4},{7,5},{8,10},{9,11},{10,... | collective-permute-start | bytes 786440 | tf_op jit(solution)/shard_map/ppermute | solution.py:17
  9.3 3.4 %collective-permute-done.6.refs_5_.own_ref = bf16[64,2048]{1,0:T(8,128)(2,1)S(1)} collective-permute-done((bf16[64,2048]{1,0:T(8,128)(2,1)}, bf16[64,2048]{1,0:T(8,128)(2,1)S(1)}, u32[]{:S(2)}, u32[]{:S(2)}) %collective-permute-start.6) | collective-permute-done | bytes 262176 | tf_op jit(solution)/shard_map/ppermute | solution.py:17
  13.0 3.1 %collective-permute-start.2 = (bf16[64,2048]{1,0:T(8,128)(2,1)S(1)}, bf16[64,2048]{1,0:T(8,128)(2,1)S(1)}, u32[]{:S(2)}, u32[]{:S(2)}) collective-permute-start(bf16[64,2048]{1,0:T(8,128)(2,1)S(1)} %shard_map.86), channel_id=1, source_target_pairs={{0,8},{4,20},{8,0},{12,28},{16,24},{20,4},{24,16},{28,12},{1,9},{5... | collective-permute-start | bytes 786440 | tf_op jit(solution)/shard_map/ppermute | solution.py:310
  16.0 4.7 %collective-permute-done.3.own_ref.refs_6_ = bf16[64,2048]{1,0:T(8,128)(2,1)S(1)} collective-permute-done((bf16[64,2048]{1,0:T(8,128)(2,1)}, bf16[64,2048]{1,0:T(8,128)(2,1)S(1)}, u32[]{:S(2)}, u32[]{:S(2)}) %collective-permute-start.3) | collective-permute-done | bytes 262176 | tf_op jit(solution)/shard_map/ppermute | solution.py:17
  21.8 5.4 %collective-permute-done.7.value_ref = bf16[64,2048]{1,0:T(8,128)(2,1)S(1)} collective-permute-done((bf16[64,2048]{1,0:T(8,128)(2,1)S(1)}, bf16[64,2048]{1,0:T(8,128)(2,1)S(1)}, u32[]{:S(2)}, u32[]{:S(2)}) %collective-permute-start.7) | collective-permute-done | bytes 262176 | tf_op jit(solution)/shard_map/ppermute | solution.py:17
  28.4 2.6 %collective-permute-start.14 = (bf16[2,64,2048]{2,1,0:T(8,128)(2,1)S(1)}, bf16[2,64,2048]{2,1,0:T(8,128)(2,1)S(1)}, u32[]{:S(2)}, u32[]{:S(2)}) collective-permute-start(bf16[2,64,2048]{2,1,0:T(8,128)(2,1)S(1)} %shard_map.93), channel_id=1, source_target_pairs={{0,3},{1,2},{2,1},{3,0},{4,5},{5,4},{6,7},{7,6},{8,11},{9,10},{10,... | collective-permute-start | bytes 1572872 | tf_op jit(solution)/shard_map/ppermute | solution.py:314
  31.2 1.9 %collective-permute-start.17 = (bf16[2,64,2048]{2,1,0:T(8,128)(2,1)S(1)}, bf16[2,64,2048]{2,1,0:T(8,128)(2,1)S(1)}, u32[]{:S(2)}, u32[]{:S(2)}) collective-permute-start(bf16[2,64,2048]{2,1,0:T(8,128)(2,1)S(1)} %shard_map.97), channel_id=1, source_target_pairs={{0,8},{4,20},{8,0},{12,28},{16,24},{20,4},{24,16},{28,12},{1,9},{5... | collective-permute-start | bytes 1572872 | tf_op jit(solution)/shard_map/ppermute | solution.py:310
  33.0 5.1 %shard_map.90.refs_0_.refs_20_ = f32[2048,256]{1,0:T(8,128)S(1)} custom-call(s32[1,1,8,48]{3,2,1,0:T(8,128)} %refs_0_.3, s32[1,1,8,48]{3,2,1,0:T(8,128)} %refs_1_.3, s32[1,1,8]{2,1,0:T(1,128)} %refs_2_.3, bf16[1,1,8,48,128,128]{5,4,3,2,1,0:T(8,128)(2,1)} %refs_3_.3, bf16[64,2048]{1,0:T(8,128)(2,1)S(1)} %copy-done.1, ...), custom_call_target="tpu_custom_call" | custom-call | flops 3221225472 | bytes 5242880 | tf_op jit(solution)/shard_map/pallas_call | solution.py:234
  38.4 4.6 %collective-permute-done.14.value_ref = bf16[2,64,2048]{2,1,0:T(8,128)(2,1)S(1)} collective-permute-done((bf16[2,64,2048]{2,1,0:T(8,128)(2,1)S(1)}, bf16[2,64,2048]{2,1,0:T(8,128)(2,1)S(1)}, u32[]{:S(2)}, u32[]{:S(2)}) %collective-permute-start.14) | collective-permute-done | bytes 524320 | tf_op jit(solution)/shard_map/ppermute | solution.py:314
  43.7 1.0 %collective-permute-done.11.value_ref = bf16[64,2048]{1,0:T(8,128)(2,1)S(1)} collective-permute-done((bf16[64,2048]{1,0:T(8,128)(2,1)S(1)}, bf16[64,2048]{1,0:T(8,128)(2,1)S(1)}, u32[]{:S(2)}, u32[]{:S(2)}) %collective-permute-start.11) | collective-permute-done | bytes 262176 | tf_op jit(solution)/shard_map/ppermute | solution.py:310
  44.7 0.6 collective-permute-start.15
  46.1 1.8 %collective-permute-done.13.refs_7_ = bf16[64,2048]{1,0:T(8,128)(2,1)S(1)} collective-permute-done((bf16[64,2048]{1,0:T(8,128)(2,1)S(1)}, bf16[64,2048]{1,0:T(8,128)(2,1)S(1)}, u32[]{:S(2)}, u32[]{:S(2)}) %collective-permute-start.13) | collective-permute-done | bytes 262176 | tf_op jit(solution)/shard_map/ppermute | solution.py:17
  47.9 8.3 %shard_map.99 = (bf16[2,256,256]{2,1,0:T(8,128)(2,1)S(1)}, f32[2,256,256]{2,1,0:T(8,128)S(1)}, bf16[2,256,256]{2,1,0:T(8,128)(2,1)S(1)}, f32[2,256,256]{2,1,0:T(8,128)S(1)}) custom-call(s32[1,1,8,48]{3,2,1,0:T(8,128)} %refs_0_.3, s32[1,1,8,48]{3,2,1,0:T(8,128)} %refs_1_.3, s32[1,1,8]{2,1,0:T(1,128)} %refs_2_.3, bf16[1,1,8,48,128,128]{5,4,3,2,1,0:T(8,128)(2,1)} %refs_3_.3, ...), custom_call_target="tpu_custom_call" | custom-call | flops 9663676416 | bytes 15728640 | tf_op jit(solution)/shard_map/pallas_call | solution.py:234
  56.2 1.8 %collective-permute-start.23 = (bf16[2,256,256]{2,1,0:T(8,128)(2,1)S(1)}, bf16[2,256,256]{2,1,0:T(8,128)(2,1)S(1)}, u32[]{:S(2)}, u32[]{:S(2)}) collective-permute-start(bf16[2,256,256]{2,1,0:T(8,128)(2,1)S(1)} %get-tuple-element.7), channel_id=1, source_target_pairs={{0,2},{1,3},{2,0},{3,1},{4,6},{5,7},{6,4},{7,5},{8,10},{9,11},{10,... | collective-permute-start | bytes 786440 | tf_op jit(solution)/shard_map/ppermute | solution.py:17
  58.0 3.3 %collective-permute-start.25 = (bf16[2,256,256]{2,1,0:T(8,128)(2,1)S(1)}, bf16[2,256,256]{2,1,0:T(8,128)(2,1)S(1)}, u32[]{:S(2)}, u32[]{:S(2)}) collective-permute-start(bf16[2,256,256]{2,1,0:T(8,128)(2,1)S(1)} %get-tuple-element.9), channel_id=1, source_target_pairs={{0,1},{1,0},{2,3},{3,2},{4,5},{5,4},{6,7},{7,6},{8,9},{9,8},{10,11... | collective-permute-start | bytes 786440 | tf_op jit(solution)/shard_map/ppermute | solution.py:17
  61.5 10.6 %collective-permute-done.23 = bf16[2,256,256]{2,1,0:T(8,128)(2,1)S(1)} collective-permute-done((bf16[2,256,256]{2,1,0:T(8,128)(2,1)S(1)}, bf16[2,256,256]{2,1,0:T(8,128)(2,1)S(1)}, u32[]{:S(2)}, u32[]{:S(2)}) %collective-permute-start.23) | collective-permute-done | bytes 262176 | tf_op jit(solution)/shard_map/ppermute | solution.py:17
  72.3 1.8 %collective-permute-start.26 = (bf16[256,256]{1,0:T(8,128)(2,1)S(1)}, bf16[256,256]{1,0:T(8,128)(2,1)S(1)}, u32[]{:S(2)}, u32[]{:S(2)}) collective-permute-start(bf16[256,256]{1,0:T(8,128)(2,1)S(1)} %fusion.9), channel_id=1, source_target_pairs={{0,2},{1,3},{2,0},{3,1},{4,6},{5,7},{6,4},{7,5},{8,10},{9,11},{10,... | collective-permute-start | bytes 393224 | tf_op jit(solution)/shard_map/ppermute | solution.py:17
  74.1 4.7 %collective-permute-done.24 = bf16[256,256]{1,0:T(8,128)(2,1)S(1)} collective-permute-done((bf16[256,256]{1,0:T(8,128)(2,1)S(1)}, bf16[256,256]{1,0:T(8,128)(2,1)S(1)}, u32[]{:S(2)}, u32[]{:S(2)}) %collective-permute-start.24) | collective-permute-done | bytes 131104 | tf_op jit(solution)/shard_map/ppermute | solution.py:17
  78.9 2.7 %collective-permute-done.26 = bf16[256,256]{1,0:T(8,128)(2,1)S(1)} collective-permute-done((bf16[256,256]{1,0:T(8,128)(2,1)S(1)}, bf16[256,256]{1,0:T(8,128)(2,1)S(1)}, u32[]{:S(2)}, u32[]{:S(2)}) %collective-permute-start.26) | collective-permute-done | bytes 131104 | tf_op jit(solution)/shard_map/ppermute | solution.py:17
  82.4 1.8 %collective-permute-start.27 = (bf16[64,256]{1,0:T(8,128)(2,1)S(1)}, bf16[64,256]{1,0:T(8,128)(2,1)S(1)}, u32[]{:S(2)}, u32[]{:S(2)}) collective-permute-start(bf16[64,256]{1,0:T(8,128)(2,1)S(1)} %get-tuple-element.12), channel_id=1, source_target_pairs={{0,3},{1,2},{2,1},{3,0},{4,7},{5,6},{6,5},{7,4},{8,11},{9,10},{10,... | collective-permute-start | bytes 98312 | tf_op jit(solution)/shard_map/ppermute | solution.py:17
  84.2 2.6 %collective-permute-start.29 = (bf16[64,256]{1,0:T(8,128)(2,1)S(1)}, bf16[64,256]{1,0:T(8,128)(2,1)S(1)}, u32[]{:S(2)}, u32[]{:S(2)}) collective-permute-start(bf16[64,256]{1,0:T(8,128)(2,1)S(1)} %get-tuple-element.13), channel_id=1, source_target_pairs={{0,1},{1,0},{2,3},{3,2},{4,5},{5,4},{6,7},{7,6},{8,9},{9,8},{10,11... | collective-permute-start | bytes 98312 | tf_op jit(solution)/shard_map/ppermute | solution.py:17
  86.8 1.3 %collective-permute-done.27 = bf16[64,256]{1,0:T(8,128)(2,1)S(1)} collective-permute-done((bf16[64,256]{1,0:T(8,128)(2,1)S(1)}, bf16[64,256]{1,0:T(8,128)(2,1)S(1)}, u32[]{:S(2)}, u32[]{:S(2)}) %collective-permute-start.27) | collective-permute-done | bytes 32800 | tf_op jit(solution)/shard_map/ppermute | solution.py:17
  88.2 0.9 collective-permute-done.28
  89.2 1.2 %collective-permute-done.30 = bf16[64,256]{1,0:T(8,128)(2,1)S(1)} collective-permute-done((bf16[64,256]{1,0:T(8,128)(2,1)S(1)}, bf16[64,256]{1,0:T(8,128)(2,1)S(1)}, u32[]{:S(2)}, u32[]{:S(2)}) %collective-permute-start.30) | collective-permute-done | bytes 32800 | tf_op jit(solution)/shard_map/ppermute | solution.py:17
  90.5 0.8 collective-permute-start.32
  91.3 2.6 %collective-permute-start.33 = (bf16[64,256]{1,0:T(8,128)(2,1)S(1)}, bf16[64,256]{1,0:T(8,128)(2,1)S(1)}, u32[]{:S(2)}, u32[]{:S(2)}) collective-permute-start(bf16[64,256]{1,0:T(8,128)(2,1)S(1)} %add_convert_fusion), channel_id=1, source_target_pairs={{0,24},{4,28},{8,16},{12,20},{16,8},{20,12},{24,0},{28,4},{1,25},{... | collective-permute-start | bytes 98312 | tf_op jit(solution)/shard_map/ppermute | solution.py:17
  93.9 0.8 copy.10
  94.8 1.3 %collective-permute-done.33 = bf16[64,256]{1,0:T(8,128)(2,1)S(1)} collective-permute-done((bf16[64,256]{1,0:T(8,128)(2,1)S(1)}, bf16[64,256]{1,0:T(8,128)(2,1)S(1)}, u32[]{:S(2)}, u32[]{:S(2)}) %collective-permute-start.33) | collective-permute-done | bytes 32800 | tf_op jit(solution)/shard_map/ppermute | solution.py:17
  96.1 0.7 add_multiply_fusion
  (70 shorter events, 5.6 us)
Async XLA Ops:
  0.7 12.1 %collective-permute-start.6 = (bf16[64,2048]{1,0:T(8,128)(2,1)}, bf16[64,2048]{1,0:T(8,128)(2,1)S(1)}, u32[]{:S(2)}, u32[]{:S(2)}) collective-permute-start(bf16[64,2048]{1,0:T(8,128)(2,1)} %refs_4_.1), channel_id=1, source_target_pairs={{0,1},{1,0},{2,3},{3,2},{4,5},{5,4},{6,7},{7,6},{8,9},{9,8},{10,11... | collective-permute-start | bytes 786440 | tf_op jit(solution)/shard_map/ppermute | solution.py:17
  3.7 9.0 %collective-permute-start.1 = (bf16[64,2048]{1,0:T(8,128)(2,1)}, bf16[64,2048]{1,0:T(8,128)(2,1)S(1)}, u32[]{:S(2)}, u32[]{:S(2)}) collective-permute-start(bf16[64,2048]{1,0:T(8,128)(2,1)} %refs_4_.1), channel_id=1, source_target_pairs={{0,8},{4,12},{8,0},{12,4},{16,24},{20,28},{24,16},{28,20},{1,9},{5... | collective-permute-start | bytes 786440 | tf_op jit(solution)/shard_map/ppermute | solution.py:17
  5.2 7.7 %collective-permute-start = (bf16[64,2048]{1,0:T(8,128)(2,1)}, bf16[64,2048]{1,0:T(8,128)(2,1)S(1)}, u32[]{:S(2)}, u32[]{:S(2)}) collective-permute-start(bf16[64,2048]{1,0:T(8,128)(2,1)} %refs_4_.1), channel_id=1, source_target_pairs={{0,16},{4,20},{8,24},{12,28},{16,0},{20,4},{24,8},{28,12},{1,17},{... | collective-permute-start | bytes 786440 | tf_op jit(solution)/shard_map/ppermute | solution.py:17
  6.8 14.0 %collective-permute-start.3 = (bf16[64,2048]{1,0:T(8,128)(2,1)}, bf16[64,2048]{1,0:T(8,128)(2,1)S(1)}, u32[]{:S(2)}, u32[]{:S(2)}) collective-permute-start(bf16[64,2048]{1,0:T(8,128)(2,1)} %refs_4_.1), channel_id=1, source_target_pairs={{0,2},{1,3},{2,0},{3,1},{4,6},{5,7},{6,4},{7,5},{8,10},{9,11},{10,... | collective-permute-start | bytes 786440 | tf_op jit(solution)/shard_map/ppermute | solution.py:17
  12.8 8.0 %collective-permute-start.9 = (bf16[64,2048]{1,0:T(8,128)(2,1)S(1)}, bf16[64,2048]{1,0:T(8,128)(2,1)S(1)}, u32[]{:S(2)}, u32[]{:S(2)}) collective-permute-start(bf16[64,2048]{1,0:T(8,128)(2,1)S(1)} %collective-permute-done.6.refs_5_.own_ref), channel_id=1, source_target_pairs={{0,4},{4,0},{8,12},{12,8},{16,20},{20,16},{24,28},{28,24},{1,5},{5... | collective-permute-start | bytes 786440 | tf_op jit(solution)/shard_map/ppermute | solution.py:17
  13.0 8.5 %collective-permute-start.2 = (bf16[64,2048]{1,0:T(8,128)(2,1)S(1)}, bf16[64,2048]{1,0:T(8,128)(2,1)S(1)}, u32[]{:S(2)}, u32[]{:S(2)}) collective-permute-start(bf16[64,2048]{1,0:T(8,128)(2,1)S(1)} %shard_map.86), channel_id=1, source_target_pairs={{0,8},{4,20},{8,0},{12,28},{16,24},{20,4},{24,16},{28,12},{1,9},{5... | collective-permute-start | bytes 786440 | tf_op jit(solution)/shard_map/ppermute | solution.py:310
  20.8 6.4 %collective-permute-start.7 = (bf16[64,2048]{1,0:T(8,128)(2,1)S(1)}, bf16[64,2048]{1,0:T(8,128)(2,1)S(1)}, u32[]{:S(2)}, u32[]{:S(2)}) collective-permute-start(bf16[64,2048]{1,0:T(8,128)(2,1)S(1)} %collective-permute-done.3.own_ref.refs_6_), channel_id=1, source_target_pairs={{0,1},{1,0},{2,3},{3,2},{4,5},{5,4},{6,7},{7,6},{8,9},{9,8},{10,11... | collective-permute-start | bytes 786440 | tf_op jit(solution)/shard_map/ppermute | solution.py:17
  20.8 7.0 %collective-permute-start.4 = (bf16[64,2048]{1,0:T(8,128)(2,1)S(1)}, bf16[64,2048]{1,0:T(8,128)(2,1)S(1)}, u32[]{:S(2)}, u32[]{:S(2)}) collective-permute-start(bf16[64,2048]{1,0:T(8,128)(2,1)S(1)} %collective-permute-done.3.own_ref.refs_6_), channel_id=1, source_target_pairs={{0,4},{4,0},{8,12},{12,8},{16,20},{20,16},{24,28},{28,24},{1,5},{5... | collective-permute-start | bytes 786440 | tf_op jit(solution)/shard_map/ppermute | solution.py:17
  20.8 10.2 %collective-permute-start.16 = (bf16[2,64,2048]{2,1,0:T(8,128)(2,1)S(1)}, bf16[2,64,2048]{2,1,0:T(8,128)(2,1)S(1)}, u32[]{:S(2)}, u32[]{:S(2)}) collective-permute-start(bf16[2,64,2048]{2,1,0:T(8,128)(2,1)S(1)} %shard_map.95), channel_id=1, source_target_pairs={{0,8},{4,20},{8,0},{12,28},{16,24},{20,4},{24,16},{28,12},{1,9},{5... | collective-permute-start | bytes 1572872 | tf_op jit(solution)/shard_map/ppermute | solution.py:310
  21.5 6.9 %collective-permute-start.12 = (bf16[64,2048]{1,0:T(8,128)(2,1)S(1)}, bf16[64,2048]{1,0:T(8,128)(2,1)S(1)}, u32[]{:S(2)}, u32[]{:S(2)}) collective-permute-start(bf16[64,2048]{1,0:T(8,128)(2,1)S(1)} %shard_map.87.own_ref.refs_4_), channel_id=1, source_target_pairs={{0,4},{4,0},{8,12},{12,8},{16,20},{20,16},{24,28},{28,24},{1,5},{5... | collective-permute-start | bytes 786440 | tf_op jit(solution)/shard_map/ppermute | solution.py:17
  27.2 3.9 %collective-permute-start.10 = (bf16[64,2048]{1,0:T(8,128)(2,1)S(1)}, bf16[64,2048]{1,0:T(8,128)(2,1)S(1)}, u32[]{:S(2)}, u32[]{:S(2)}) collective-permute-start(bf16[64,2048]{1,0:T(8,128)(2,1)S(1)} %shard_map.89.refs_7_.own_ref), channel_id=1, source_target_pairs={{0,4},{4,0},{8,12},{12,8},{16,20},{20,16},{24,28},{28,24},{1,5},{5... | collective-permute-start | bytes 786440 | tf_op jit(solution)/shard_map/ppermute | solution.py:17
  27.3 5.8 %collective-permute-start.8 = (bf16[64,2048]{1,0:T(8,128)(2,1)S(1)}, bf16[64,2048]{1,0:T(8,128)(2,1)S(1)}, u32[]{:S(2)}, u32[]{:S(2)}) collective-permute-start(bf16[64,2048]{1,0:T(8,128)(2,1)S(1)} %copy-done.1), channel_id=1, source_target_pairs={{0,4},{4,0},{8,12},{12,8},{16,20},{20,16},{24,28},{28,24},{1,5},{5... | collective-permute-start | bytes 786440 | tf_op jit(solution)/shard_map/ppermute | solution.py:17
  27.8 10.3 %collective-permute-start.5 = (bf16[2,64,2048]{2,1,0:T(8,128)(2,1)S(1)}, bf16[2,64,2048]{2,1,0:T(8,128)(2,1)S(1)}, u32[]{:S(2)}, u32[]{:S(2)}) collective-permute-start(bf16[2,64,2048]{2,1,0:T(8,128)(2,1)S(1)} %shard_map.88), channel_id=1, source_target_pairs={{0,8},{4,20},{8,0},{12,28},{16,24},{20,4},{24,16},{28,12},{1,9},{5... | collective-permute-start | bytes 1572872 | tf_op jit(solution)/shard_map/ppermute | solution.py:310
  28.4 14.6 %collective-permute-start.14 = (bf16[2,64,2048]{2,1,0:T(8,128)(2,1)S(1)}, bf16[2,64,2048]{2,1,0:T(8,128)(2,1)S(1)}, u32[]{:S(2)}, u32[]{:S(2)}) collective-permute-start(bf16[2,64,2048]{2,1,0:T(8,128)(2,1)S(1)} %shard_map.93), channel_id=1, source_target_pairs={{0,3},{1,2},{2,1},{3,0},{4,5},{5,4},{6,7},{7,6},{8,11},{9,10},{10,... | collective-permute-start | bytes 1572872 | tf_op jit(solution)/shard_map/ppermute | solution.py:314
  31.1 12.0 %collective-permute-start.22 = (bf16[64,2048]{1,0:T(8,128)(2,1)S(1)}, bf16[64,2048]{1,0:T(8,128)(2,1)S(1)}, u32[]{:S(2)}, u32[]{:S(2)}) collective-permute-start(bf16[64,2048]{1,0:T(8,128)(2,1)S(1)} %collective-permute-done.even_ref.refs_17_), channel_id=1, source_target_pairs={{0,4},{4,0},{8,12},{12,8},{16,20},{20,16},{24,28},{28,24},{1,5},{5... | collective-permute-start | bytes 786440 | tf_op jit(solution)/shard_map/ppermute | solution.py:17
  31.2 14.3 %collective-permute-start.17 = (bf16[2,64,2048]{2,1,0:T(8,128)(2,1)S(1)}, bf16[2,64,2048]{2,1,0:T(8,128)(2,1)S(1)}, u32[]{:S(2)}, u32[]{:S(2)}) collective-permute-start(bf16[2,64,2048]{2,1,0:T(8,128)(2,1)S(1)} %shard_map.97), channel_id=1, source_target_pairs={{0,8},{4,20},{8,0},{12,28},{16,24},{20,4},{24,16},{28,12},{1,9},{5... | collective-permute-start | bytes 1572872 | tf_op jit(solution)/shard_map/ppermute | solution.py:310
  38.2 6.4 %collective-permute-start.11 = (bf16[64,2048]{1,0:T(8,128)(2,1)S(1)}, bf16[64,2048]{1,0:T(8,128)(2,1)S(1)}, u32[]{:S(2)}, u32[]{:S(2)}) collective-permute-start(bf16[64,2048]{1,0:T(8,128)(2,1)S(1)} %shard_map.91), channel_id=1, source_target_pairs={{0,16},{4,12},{8,24},{12,4},{16,0},{20,28},{24,8},{28,20},{1,17},{... | collective-permute-start | bytes 786440 | tf_op jit(solution)/shard_map/ppermute | solution.py:310
  38.3 7.2 %collective-permute-start.21 = (bf16[64,2048]{1,0:T(8,128)(2,1)S(1)}, bf16[64,2048]{1,0:T(8,128)(2,1)S(1)}, u32[]{:S(2)}, u32[]{:S(2)}) collective-permute-start(bf16[64,2048]{1,0:T(8,128)(2,1)S(1)} %shard_map.98), channel_id=1, source_target_pairs={{0,4},{4,0},{8,12},{12,8},{16,20},{20,16},{24,28},{28,24},{1,5},{5... | collective-permute-start | bytes 786440 | tf_op jit(solution)/shard_map/ppermute | solution.py:17
  43.0 3.1 %collective-permute-start.18 = (bf16[2,64,2048]{2,1,0:T(8,128)(2,1)S(1)}, bf16[2,64,2048]{2,1,0:T(8,128)(2,1)S(1)}, u32[]{:S(2)}, u32[]{:S(2)}) collective-permute-start(bf16[2,64,2048]{2,1,0:T(8,128)(2,1)S(1)} %shard_map.96.refs_0_.refs_10_), channel_id=1, source_target_pairs={{0,4},{4,0},{8,12},{12,8},{16,20},{20,16},{24,28},{28,24},{1,5},{5... | collective-permute-start | bytes 1572872 | tf_op jit(solution)/shard_map/ppermute | solution.py:17
  43.1 3.0 %collective-permute-start.19 = (bf16[2,64,2048]{2,1,0:T(8,128)(2,1)S(1)}, bf16[2,64,2048]{2,1,0:T(8,128)(2,1)S(1)}, u32[]{:S(2)}, u32[]{:S(2)}) collective-permute-start(bf16[2,64,2048]{2,1,0:T(8,128)(2,1)S(1)} %collective-permute-done.5.pair_ref.refs_11_), channel_id=1, source_target_pairs={{0,4},{4,0},{8,12},{12,8},{16,20},{20,16},{24,28},{28,24},{1,5},{5... | collective-permute-start | bytes 1572872 | tf_op jit(solution)/shard_map/ppermute | solution.py:17
  44.7 3.3 %collective-permute-start.15 = (bf16[2,64,2048]{2,1,0:T(8,128)(2,1)S(1)}, bf16[2,64,2048]{2,1,0:T(8,128)(2,1)S(1)}, u32[]{:S(2)}, u32[]{:S(2)}) collective-permute-start(bf16[2,64,2048]{2,1,0:T(8,128)(2,1)S(1)} %shard_map.94.refs_8_), channel_id=1, source_target_pairs={{0,4},{4,0},{8,12},{12,8},{16,20},{20,16},{24,28},{28,24},{1,5},{5... | collective-permute-start | bytes 1572872 | tf_op jit(solution)/shard_map/ppermute | solution.py:17
  45.5 2.4 %collective-permute-start.20 = (bf16[2,64,2048]{2,1,0:T(8,128)(2,1)S(1)}, bf16[2,64,2048]{2,1,0:T(8,128)(2,1)S(1)}, u32[]{:S(2)}, u32[]{:S(2)}) collective-permute-start(bf16[2,64,2048]{2,1,0:T(8,128)(2,1)S(1)} %collective-permute-done.17.refs_12_), channel_id=1, source_target_pairs={{0,4},{4,0},{8,12},{12,8},{16,20},{20,16},{24,28},{28,24},{1,5},{5... | collective-permute-start | bytes 1572872 | tf_op jit(solution)/shard_map/ppermute | solution.py:17
  56.2 15.8 %collective-permute-start.23 = (bf16[2,256,256]{2,1,0:T(8,128)(2,1)S(1)}, bf16[2,256,256]{2,1,0:T(8,128)(2,1)S(1)}, u32[]{:S(2)}, u32[]{:S(2)}) collective-permute-start(bf16[2,256,256]{2,1,0:T(8,128)(2,1)S(1)} %get-tuple-element.7), channel_id=1, source_target_pairs={{0,2},{1,3},{2,0},{3,1},{4,6},{5,7},{6,4},{7,5},{8,10},{9,11},{10,... | collective-permute-start | bytes 786440 | tf_op jit(solution)/shard_map/ppermute | solution.py:17
  58.0 14.2 %collective-permute-start.25 = (bf16[2,256,256]{2,1,0:T(8,128)(2,1)S(1)}, bf16[2,256,256]{2,1,0:T(8,128)(2,1)S(1)}, u32[]{:S(2)}, u32[]{:S(2)}) collective-permute-start(bf16[2,256,256]{2,1,0:T(8,128)(2,1)S(1)} %get-tuple-element.9), channel_id=1, source_target_pairs={{0,1},{1,0},{2,3},{3,2},{4,5},{5,4},{6,7},{7,6},{8,9},{9,8},{10,11... | collective-permute-start | bytes 786440 | tf_op jit(solution)/shard_map/ppermute | solution.py:17
  72.1 6.7 %collective-permute-start.24 = (bf16[256,256]{1,0:T(8,128)(2,1)S(1)}, bf16[256,256]{1,0:T(8,128)(2,1)S(1)}, u32[]{:S(2)}, u32[]{:S(2)}) collective-permute-start(bf16[256,256]{1,0:T(8,128)(2,1)S(1)} %fusion.8), channel_id=1, source_target_pairs={{0,1},{1,0},{2,3},{3,2},{4,5},{5,4},{6,7},{7,6},{8,9},{9,8},{10,11... | collective-permute-start | bytes 393224 | tf_op jit(solution)/shard_map/ppermute | solution.py:17
  72.3 9.2 %collective-permute-start.26 = (bf16[256,256]{1,0:T(8,128)(2,1)S(1)}, bf16[256,256]{1,0:T(8,128)(2,1)S(1)}, u32[]{:S(2)}, u32[]{:S(2)}) collective-permute-start(bf16[256,256]{1,0:T(8,128)(2,1)S(1)} %fusion.9), channel_id=1, source_target_pairs={{0,2},{1,3},{2,0},{3,1},{4,6},{5,7},{6,4},{7,5},{8,10},{9,11},{10,... | collective-permute-start | bytes 393224 | tf_op jit(solution)/shard_map/ppermute | solution.py:17
  82.4 5.8 %collective-permute-start.27 = (bf16[64,256]{1,0:T(8,128)(2,1)S(1)}, bf16[64,256]{1,0:T(8,128)(2,1)S(1)}, u32[]{:S(2)}, u32[]{:S(2)}) collective-permute-start(bf16[64,256]{1,0:T(8,128)(2,1)S(1)} %get-tuple-element.12), channel_id=1, source_target_pairs={{0,3},{1,2},{2,1},{3,0},{4,7},{5,6},{6,5},{7,4},{8,11},{9,10},{10,... | collective-permute-start | bytes 98312 | tf_op jit(solution)/shard_map/ppermute | solution.py:17
  84.2 4.9 %collective-permute-start.28 = (bf16[64,256]{1,0:T(8,128)(2,1)S(1)}, bf16[64,256]{1,0:T(8,128)(2,1)S(1)}, u32[]{:S(2)}, u32[]{:S(2)}) collective-permute-start(bf16[64,256]{1,0:T(8,128)(2,1)S(1)} %get-tuple-element.14), channel_id=1, source_target_pairs={{0,2},{1,3},{2,0},{3,1},{4,6},{5,7},{6,4},{7,5},{8,10},{9,11},{10,... | collective-permute-start | bytes 98312 | tf_op jit(solution)/shard_map/ppermute | solution.py:17
  84.2 4.9 %collective-permute-start.29 = (bf16[64,256]{1,0:T(8,128)(2,1)S(1)}, bf16[64,256]{1,0:T(8,128)(2,1)S(1)}, u32[]{:S(2)}, u32[]{:S(2)}) collective-permute-start(bf16[64,256]{1,0:T(8,128)(2,1)S(1)} %get-tuple-element.13), channel_id=1, source_target_pairs={{0,1},{1,0},{2,3},{3,2},{4,5},{5,4},{6,7},{7,6},{8,9},{9,8},{10,11... | collective-permute-start | bytes 98312 | tf_op jit(solution)/shard_map/ppermute | solution.py:17
  90.4 4.4 %collective-permute-start.31 = (bf16[64,256]{1,0:T(8,128)(2,1)S(1)}, bf16[64,256]{1,0:T(8,128)(2,1)S(1)}, u32[]{:S(2)}, u32[]{:S(2)}) collective-permute-start(bf16[64,256]{1,0:T(8,128)(2,1)S(1)} %add_convert_fusion), channel_id=1, source_target_pairs={{0,8},{4,12},{8,0},{12,4},{16,24},{20,28},{24,16},{28,20},{1,9},{5... | collective-permute-start | bytes 98312 | tf_op jit(solution)/shard_map/ppermute | solution.py:17
  90.5 4.3 %collective-permute-start.32 = (bf16[64,256]{1,0:T(8,128)(2,1)S(1)}, bf16[64,256]{1,0:T(8,128)(2,1)S(1)}, u32[]{:S(2)}, u32[]{:S(2)}) collective-permute-start(bf16[64,256]{1,0:T(8,128)(2,1)S(1)} %add_convert_fusion), channel_id=1, source_target_pairs={{0,16},{4,20},{8,24},{12,28},{16,0},{20,4},{24,8},{28,12},{1,17},{... | collective-permute-start | bytes 98312 | tf_op jit(solution)/shard_map/ppermute | solution.py:17
  91.3 4.8 %collective-permute-start.33 = (bf16[64,256]{1,0:T(8,128)(2,1)S(1)}, bf16[64,256]{1,0:T(8,128)(2,1)S(1)}, u32[]{:S(2)}, u32[]{:S(2)}) collective-permute-start(bf16[64,256]{1,0:T(8,128)(2,1)S(1)} %add_convert_fusion), channel_id=1, source_target_pairs={{0,24},{4,28},{8,16},{12,20},{16,8},{20,12},{24,0},{28,4},{1,25},{... | collective-permute-start | bytes 98312 | tf_op jit(solution)/shard_map/ppermute | solution.py:17
  (5 other events, 127.0 us)
